TPU v7x, 32 devices: a whole 2x2x4 slice. The times are simulated.
32 devices in a mesh: section: 2 (over x), dp: 16 (over z, y, core).
Axes of the slice: x: 2, y: 2, z: 4, core: 2. Of those that a mesh axis runs over, the one named last changes fastest.
Arguments:
- spectra: bfloat16 [2, 16, 4096, 80], P(None, 'dp'), may hold values from -6 to 6
- lengths: int32 [2, 16], P(None, 'dp'), may hold values from 128 to 512, as said below
- languages: int32 [2, 16], P(None, 'dp'), may hold values from 0 to 7
- token_masks: int32 [8, 1024], replicated, may hold values from 0 to 1, as said below
- cotangent: bfloat16 [2, 2, 16, 512, 1024], P('section', None, 'dp'), may hold values from -6 to 6
- feed_in: float32 [2, 2, 512, 2048], P('section', None, 'dp'), may hold values from -0.25 to 0.25
- feed_out: float32 [2, 2, 2048, 512], P('section', None, 'dp'), may hold values from -0.25 to 0.25
- attend_in: float32 [2, 512, 1536], P('section', 'dp'), may hold values from -0.25 to 0.25
- attend_out: float32 [2, 512, 512], P('section', 'dp'), may hold values from -0.75 to 0.75
- conv_in: float32 [2, 512, 1024], P('section', 'dp'), may hold values from -0.25 to 0.25
- conv_depth: float32 [2, 9, 512], P('section', None, 'dp'), may hold values from -2 to 2
- conv_out: float32 [2, 512, 512], P('section', 'dp'), may hold values from -0.375 to 0.375
- norm_gains: float32 [2, 6, 512], P('section', None, 'dp'), may hold values from 0.1 to 1.9
- stem_in: float32 [640, 256], P(None, ('section', 'dp')), may hold values from -0.25 to 0.25
- stem_out: float32 [256, 512], P(('section', 'dp')), may hold values from -0.5 to 0.5
- head_weight: float32 [512, 1024], P(None, ('section', 'dp')), may hold values from -0.5 to 0.5
Outputs:
- activations: float32 [2, 2, 16, 512, 512], P('section', None, 'dp')
- log_probs: float32 [2, 2, 16, 512, 1024], P('section', None, 'dp')
- input_grads: float32 [2, 2, 16, 512, 512], P('section', None, 'dp')
- grad_feed_in: float32 [2, 2, 512, 2048], P('section', None, 'dp')
- grad_feed_out: float32 [2, 2, 2048, 512], P('section', None, 'dp')
- grad_attend_in: float32 [2, 512, 1536], P('section', 'dp')
- grad_attend_out: float32 [2, 512, 512], P('section', 'dp')
- grad_conv_in: float32 [2, 512, 1024], P('section', 'dp')
- grad_conv_depth: float32 [2, 9, 512], P('section', None, 'dp')
- grad_conv_out: float32 [2, 512, 512], P('section', 'dp')
- grad_gains: float32 [2, 6, 512], P('section', None, 'dp')
- grad_stem_in: float32 [640, 256], P(None, ('section', 'dp'))
- grad_stem_out: float32 [256, 512], P(('section', 'dp'))
- grad_head: float32 [512, 1024], P(None, ('section', 'dp'))
Inputs may be any that keep to these rules, and one draw needn't show every extreme that they name: `lengths`: every micro-batch holds an utterance of exactly 512 tokens. `token_masks`: token 0 is allowed for every language group.
All inputs are finite; a program needn't handle non-finite values.
Results may differ from a plain program's by a relative error of at most 0.02.
Values may be sent and summed in bfloat16 or wider, within the bound.
No kernel may reach another device: no remote copies, remote signals or barrier semaphores. Data moves between devices by JAX's collectives and lax.ppermute only.
A program may use at most 256 MiB of HBM per device.

v0:
```python
import jax
import jax.numpy as jnp
from jax import lax
from jax.sharding import PartitionSpec as P

D = 512
HEADS = 8
HDIM = 64


epsilon = 1e-05
masked_score = -1e30


def shifted(value, axis, steps):
    count = lax.axis_size(axis)
    leading, last = (max(0, -steps), min(count, count - steps))
    return lax.ppermute(value, axis, [(source, source + steps) for source in range(leading, last)])


def matmul(left, right):
    return jnp.dot(left, right, preferred_element_type=jnp.float32)


def matmul_left(left, right):
    return lax.dot_general(
        left, right, (((0,), (0,)), ((), ())), preferred_element_type=jnp.float32
    )


def matmul_right(left, right):
    return lax.dot_general(
        left, right, (((1,), (1,)), ((), ())), preferred_element_type=jnp.float32
    )


def silu_grad(pre_act):
    sigmoid_v = jax.nn.sigmoid(pre_act)
    return sigmoid_v * (1.0 + pre_act * (1.0 - sigmoid_v))


def norm_forward(x_rows, norm_gain):
    centered = x_rows - jnp.mean(x_rows, axis=-1, keepdims=True)
    inv_scale = lax.rsqrt(jnp.mean(centered * centered, axis=-1, keepdims=True) + epsilon)
    unit_rows = centered * inv_scale
    return (unit_rows * norm_gain, (unit_rows, inv_scale))


def norm_backward(grad_out, norm_kept, norm_gain):
    unit_rows, inv_scale = norm_kept
    grad_unit = grad_out * norm_gain
    grad_rows = inv_scale * (
        grad_unit
        - jnp.mean(grad_unit, axis=-1, keepdims=True)
        - unit_rows * jnp.mean(grad_unit * unit_rows, axis=-1, keepdims=True)
    )
    return (grad_rows, jnp.sum(grad_out * unit_rows, axis=0))


def feed_forward(x_rows, norm_gain, w_in, w_out):
    normed, norm_kept = norm_forward(x_rows, norm_gain)
    normed = normed.astype(jnp.bfloat16)
    hidden = matmul(normed, w_in)
    active = jax.nn.silu(hidden).astype(jnp.bfloat16)
    return (matmul(active, w_out), (norm_kept, normed, hidden, active))


def feed_backward(grad_res, kept, norm_gain, w_in, w_out):
    norm_kept, normed, hidden, active = kept
    grad_b = (0.5 * grad_res).astype(jnp.bfloat16)
    grad_w_out = matmul_left(active, grad_b)
    grad_hidden = (matmul_right(grad_b, w_out) * silu_grad(hidden)).astype(jnp.bfloat16)
    grad_w_in = matmul_left(normed, grad_hidden)
    grad_rows, grad_gain = norm_backward(matmul_right(grad_hidden, w_in), norm_kept, norm_gain)
    return (grad_res + grad_rows, grad_w_in, grad_w_out, grad_gain)


def score_rows(queries, key_rows, valid_mask):
    scores = jnp.einsum(
        "uqhd,ukhd->uhqk", queries, key_rows, preferred_element_type=jnp.float32
    ) * HDIM ** (-0.5)
    return jnp.where(valid_mask[:, None, None, :] > 0, scores, masked_score)


def attention_forward(x_rows, norm_gain, w_in, w_out, valid_mask):
    groups, length = valid_mask.shape
    normed, norm_kept = norm_forward(x_rows, norm_gain)
    normed = normed.astype(jnp.bfloat16)
    split_heads = matmul(normed, w_in).astype(jnp.bfloat16).reshape(groups, length, 3, HEADS, HDIM)
    scores = score_rows(split_heads[:, :, 0], split_heads[:, :, 1], valid_mask)
    top_score = jnp.max(scores, axis=-1, keepdims=True)
    logsum = top_score + jnp.log(jnp.sum(jnp.exp(scores - top_score), axis=-1, keepdims=True))
    attn_probs = jnp.exp(scores - logsum).astype(jnp.bfloat16)
    mixed_rows = jnp.einsum(
        "uhqk,ukhd->uqhd", attn_probs, split_heads[:, :, 2], preferred_element_type=jnp.float32
    )
    mixed_rows = mixed_rows.reshape(groups * length, -1).astype(jnp.bfloat16)
    return (matmul(mixed_rows, w_out), (norm_kept, normed, split_heads, logsum, mixed_rows))


def attention_backward(grad_res, kept, norm_gain, w_in, w_out, valid_mask):
    norm_kept, normed, split_heads, logsum, mixed_rows = kept
    groups, length = valid_mask.shape
    queries, key_rows, value_rows = (
        split_heads[:, :, 0],
        split_heads[:, :, 1],
        split_heads[:, :, 2],
    )
    grad_b = grad_res.astype(jnp.bfloat16)
    grad_w_out = matmul_left(mixed_rows, grad_b)
    grad_mixed = (
        matmul_right(grad_b, w_out).astype(jnp.bfloat16).reshape(groups, length, HEADS, HDIM)
    )
    attn_probs = jnp.exp(score_rows(queries, key_rows, valid_mask) - logsum)
    grad_probs = jnp.einsum(
        "uqhd,ukhd->uhqk", grad_mixed, value_rows, preferred_element_type=jnp.float32
    )
    grad_values = jnp.einsum(
        "uhqk,uqhd->ukhd",
        attn_probs.astype(jnp.bfloat16),
        grad_mixed,
        preferred_element_type=jnp.float32,
    )
    grad_scores = attn_probs * (
        grad_probs - jnp.sum(attn_probs * grad_probs, axis=-1, keepdims=True)
    )
    grad_scores = (grad_scores * HDIM ** (-0.5)).astype(jnp.bfloat16)
    grad_queries = jnp.einsum(
        "uhqk,ukhd->uqhd", grad_scores, key_rows, preferred_element_type=jnp.float32
    )
    grad_keys = jnp.einsum(
        "uhqk,uqhd->ukhd", grad_scores, queries, preferred_element_type=jnp.float32
    )
    grad_packed = (
        jnp.stack([grad_queries, grad_keys, grad_values], axis=2)
        .reshape(groups * length, -1)
        .astype(jnp.bfloat16)
    )
    grad_w_in = matmul_left(normed, grad_packed)
    grad_rows, grad_gain = norm_backward(matmul_right(grad_packed, w_in), norm_kept, norm_gain)
    return (grad_res + grad_rows, grad_w_in, grad_w_out, grad_gain)


def conv_forward(x_rows, gain_in, gain_mid, w_in, depth, w_out, valid_mask):
    groups, length = valid_mask.shape
    normed, norm_kept = norm_forward(x_rows, gain_in)
    normed = normed.astype(jnp.bfloat16)
    gated_rows = matmul(normed, w_in)
    half_width = gated_rows.shape[1] // 2
    glu_rows = gated_rows[:, :half_width] * jax.nn.sigmoid(gated_rows[:, half_width:])
    glu_rows = glu_rows.reshape(groups, length, half_width) * valid_mask[:, :, None]
    depth_float = depth.astype(jnp.float32)
    half_kernel = depth.shape[0] // 2
    padded = jnp.pad(glu_rows, ((0, 0), (half_kernel, half_kernel), (0, 0)))
    deep_rows = depth_float[0] * padded[:, 0:length]
    for offset in range(1, depth.shape[0]):
        deep_rows = deep_rows + depth_float[offset] * padded[:, offset : offset + length]
    middle, mid_kept = norm_forward(deep_rows.reshape(groups * length, half_width), gain_mid)
    active = jax.nn.silu(middle).astype(jnp.bfloat16)
    return (
        matmul(active, w_out),
        (norm_kept, normed, gated_rows, padded, mid_kept, middle, active),
    )


def conv_backward(grad_res, kept, gain_in, gain_mid, w_in, depth, w_out, valid_mask):
    norm_kept, normed, gated_rows, padded, mid_kept, middle, active = kept
    groups, length = valid_mask.shape
    half_width = gated_rows.shape[1] // 2
    depth_float = depth.astype(jnp.float32)
    tap_count = depth.shape[0]
    half_kernel = tap_count // 2
    grad_b = grad_res.astype(jnp.bfloat16)
    grad_w_out = matmul_left(active, grad_b)
    grad_middle = matmul_right(grad_b, w_out) * silu_grad(middle)
    grad_deep, grad_gain_mid = norm_backward(grad_middle, mid_kept, gain_mid)
    grad_deep = grad_deep.reshape(groups, length, half_width)
    grad_depth = jnp.stack(
        [
            jnp.sum(grad_deep * padded[:, offset : offset + length], axis=(0, 1))
            for offset in range(tap_count)
        ]
    )
    grad_pad = jnp.pad(grad_deep, ((0, 0), (half_kernel, half_kernel), (0, 0)))
    grad_glu = depth_float[0] * grad_pad[:, 2 * half_kernel : 2 * half_kernel + length]
    for offset in range(1, tap_count):
        begin = 2 * half_kernel - offset
        grad_glu = grad_glu + depth_float[offset] * grad_pad[:, begin : begin + length]
    grad_glu = (grad_glu * valid_mask[:, :, None]).reshape(groups * length, half_width)
    left_half = gated_rows[:, :half_width]
    gate_sig = jax.nn.sigmoid(gated_rows[:, half_width:])
    grad_gated = jnp.concatenate(
        [grad_glu * gate_sig, grad_glu * left_half * gate_sig * (1.0 - gate_sig)], axis=1
    ).astype(jnp.bfloat16)
    grad_w_in = matmul_left(normed, grad_gated)
    grad_rows, grad_gain_in = norm_backward(matmul_right(grad_gated, w_in), norm_kept, gain_in)
    return (grad_res + grad_rows, grad_w_in, grad_depth, grad_w_out, grad_gain_in, grad_gain_mid)


def layer_forward(x_rows, valid_mask, weights):
    feed_in, feed_out, attend_in, attend_out, conv_in, conv_depth, conv_out, norm_gains = weights
    gain_values = norm_gains.astype(jnp.float32)
    first_feed, kept_one = feed_forward(x_rows, gain_values[0], feed_in[0], feed_out[0])
    stream_one = x_rows + 0.5 * first_feed
    attended, kept_two = attention_forward(
        stream_one, gain_values[1], attend_in, attend_out, valid_mask
    )
    stream_two = stream_one + attended
    convolved, kept_three = conv_forward(
        stream_two, gain_values[2], gain_values[3], conv_in, conv_depth, conv_out, valid_mask
    )
    stream_three = stream_two + convolved
    second_feed, kept_four = feed_forward(stream_three, gain_values[4], feed_in[1], feed_out[1])
    stream_four = stream_three + 0.5 * second_feed
    finished, kept_five = norm_forward(stream_four, gain_values[5])
    return (
        finished * valid_mask.reshape(-1, 1),
        (kept_one, kept_two, kept_three, kept_four, kept_five),
    )


def layer_backward(grad_act, kept, valid_mask, weights):
    feed_in, feed_out, attend_in, attend_out, conv_in, conv_depth, conv_out, norm_gains = weights
    kept_one, kept_two, kept_three, kept_four, kept_five = kept
    gain_values = norm_gains.astype(jnp.float32)
    grad_four, gain_five = norm_backward(
        grad_act * valid_mask.reshape(-1, 1), kept_five, gain_values[5]
    )
    grad_three, feed_in_two, feed_out_two, gain_four = feed_backward(
        grad_four, kept_four, gain_values[4], feed_in[1], feed_out[1]
    )
    grad_two, conv_in_grad, depth_grad, conv_out_grad, gain_two, gain_three = conv_backward(
        grad_three,
        kept_three,
        gain_values[2],
        gain_values[3],
        conv_in,
        conv_depth,
        conv_out,
        valid_mask,
    )
    grad_one, attend_in_grad, attend_out_grad, gain_one = attention_backward(
        grad_two, kept_two, gain_values[1], attend_in, attend_out, valid_mask
    )
    grad_input, feed_in_one, feed_out_one, gain_zero = feed_backward(
        grad_one, kept_one, gain_values[0], feed_in[0], feed_out[0]
    )
    grads = (
        jnp.stack([feed_in_one, feed_in_two]),
        jnp.stack([feed_out_one, feed_out_two]),
        attend_in_grad,
        attend_out_grad,
        conv_in_grad,
        depth_grad,
        conv_out_grad,
        jnp.stack([gain_zero, gain_one, gain_two, gain_three, gain_four, gain_five]),
    )
    return (grad_input, grads)


def head_forward(sent_rows, head_w, allowed, valid_mask):
    groups, length = valid_mask.shape
    logits = matmul(sent_rows, head_w).reshape(groups, length, -1)
    permit = allowed[:, None, :] > 0
    top_logit = jnp.max(jnp.where(permit, logits, masked_score), axis=-1, keepdims=True)
    exp_total = jnp.sum(
        jnp.exp(jnp.where(permit, logits - top_logit, masked_score)), axis=-1, keepdims=True
    )
    logsum = top_logit + jnp.log(exp_total)
    log_probs = jnp.where(permit, logits - logsum, 0.0) * valid_mask[:, :, None]
    return (log_probs, logits, logsum)


def head_backward(tangent, sent_rows, head_w, allowed, valid_mask, logits, logsum):
    permit = allowed[:, None, :] > 0
    weighted = jnp.where(permit, tangent, 0.0) * valid_mask[:, :, None]
    token_probs = jnp.exp(jnp.where(permit, logits - logsum, masked_score))
    grad_logits = weighted - token_probs * jnp.sum(weighted, axis=-1, keepdims=True)
    grad_logits = grad_logits.reshape(sent_rows.shape[0], -1).astype(jnp.bfloat16)
    return (matmul_left(sent_rows, grad_logits), matmul_right(grad_logits, head_w))


def stem_hidden(frames, stem_w_in):
    pre_act = matmul(frames, stem_w_in)
    return (pre_act, jax.nn.silu(pre_act).astype(jnp.bfloat16))


def stem_backward(grad_x, frames, stem_w_in, stem_w_out, valid_rows):
    pre_act, hidden = stem_hidden(frames, stem_w_in)
    grad_b = (grad_x * valid_rows).astype(jnp.bfloat16)
    grad_w_out = matmul_left(hidden, grad_b)
    grad_pre = (matmul_right(grad_b, stem_w_out) * silu_grad(pre_act)).astype(jnp.bfloat16)
    return (matmul_left(frames, grad_pre), grad_w_out)


def on_device(
    spectra,
    lengths,
    languages,
    token_masks,
    cotangent,
    feed_in,
    feed_out,
    attend_in,
    attend_out,
    conv_in,
    conv_depth,
    conv_out,
    norm_gains,
    stem_in,
    stem_out,
    head_weight,
):
    section_index = lax.axis_index("section")
    first_flag = (section_index == 0).astype(jnp.float32)
    micro_count, groups = lengths.shape
    length = cotangent.shape[3]
    row_count = groups * length
    weights = (
        lax.all_gather(feed_in[0].astype(jnp.bfloat16), "dp", axis=1, tiled=True),
        lax.all_gather(feed_out[0].astype(jnp.bfloat16), "dp", axis=1, tiled=True),
        lax.all_gather(attend_in[0].astype(jnp.bfloat16), "dp", axis=0, tiled=True),
        lax.all_gather(attend_out[0].astype(jnp.bfloat16), "dp", axis=0, tiled=True),
        lax.all_gather(conv_in[0].astype(jnp.bfloat16), "dp", axis=0, tiled=True),
        lax.all_gather(conv_depth[0].astype(jnp.bfloat16), "dp", axis=1, tiled=True),
        lax.all_gather(conv_out[0].astype(jnp.bfloat16), "dp", axis=0, tiled=True),
        lax.all_gather(norm_gains[0].astype(jnp.bfloat16), "dp", axis=1, tiled=True),
    )
    stem_w_in, stem_w_out, head_w = (
        lax.all_gather(stem_in.astype(jnp.bfloat16), ("section", "dp"), axis=1, tiled=True),
        lax.all_gather(stem_out.astype(jnp.bfloat16), ("section", "dp"), axis=0, tiled=True),
        lax.all_gather(head_weight.astype(jnp.bfloat16), ("section", "dp"), axis=1, tiled=True),
    )
    positions = jnp.arange(length)
    valid_all = (positions[None, None, :] < lengths[:, :, None]).astype(jnp.float32)
    choose = (languages[:, :, None] == jnp.arange(token_masks.shape[0])[None, None, :]).astype(
        jnp.float32
    )
    allowed_all = jnp.einsum("mul,lv->muv", choose, token_masks.astype(jnp.float32))
    received = jnp.zeros((row_count, D), jnp.bfloat16)
    input_list, act_list, logp_list, kept_list = ([], [], [], [])
    for timestep in range(micro_count + 1):
        batch_index = jnp.clip(timestep - section_index, 0, micro_count - 1)
        valid_mask = lax.dynamic_index_in_dim(valid_all, batch_index, 0, keepdims=False)
        allowed = lax.dynamic_index_in_dim(allowed_all, batch_index, 0, keepdims=False)
        layer_in = received
        if timestep < micro_count:
            frames = spectra[timestep].reshape(row_count, -1)
            pre_act, hidden = stem_hidden(frames, stem_w_in)
            stem_rows = (matmul(hidden, stem_w_out) * valid_mask.reshape(-1, 1)).astype(
                jnp.bfloat16
            )
            layer_in = jnp.where(section_index == 0, stem_rows, received)
        activated, kept = layer_forward(layer_in.astype(jnp.float32), valid_mask, weights)
        sent_rows = activated.astype(jnp.bfloat16)
        log_probs, logits, logsum = head_forward(sent_rows, head_w, allowed, valid_mask)
        input_list.append(layer_in)
        act_list.append(activated)
        logp_list.append(log_probs)
        kept_list.append(kept)
        if timestep < micro_count:
            received = shifted(sent_rows, "section", 1)
    input_stack = jnp.stack(input_list)
    act_stack = jnp.stack(act_list)
    logp_stack = jnp.stack(logp_list)
    activations = lax.dynamic_slice_in_dim(
        act_stack.reshape(micro_count + 1, groups, length, -1), section_index, micro_count, 0
    )[None]
    log_probs_out = lax.dynamic_slice_in_dim(logp_stack, section_index, micro_count, 0)[None]
    shard_sums = tuple(
        (
            jnp.zeros(master.shape[1:], jnp.float32)
            for master in (
                feed_in,
                feed_out,
                attend_in,
                attend_out,
                conv_in,
                conv_depth,
                conv_out,
                norm_gains,
            )
        )
    )
    stem_in_sum = jnp.zeros(stem_w_in.shape, jnp.float32)
    stem_out_sum = jnp.zeros(stem_w_out.shape, jnp.float32)
    head_sum = jnp.zeros(head_w.shape, jnp.float32)
    grad_received = jnp.zeros((row_count, D), jnp.bfloat16)
    grad_list = []
    for timestep in range(micro_count + 1):
        batch_index = timestep - 1 + section_index
        live_flag = ((batch_index >= 0) & (batch_index < micro_count)).astype(jnp.float32)
        clipped = jnp.clip(batch_index, 0, micro_count - 1)
        source = jnp.clip(timestep - 1 + 2 * section_index, 0, micro_count)
        valid_mask = lax.dynamic_index_in_dim(valid_all, clipped, 0, keepdims=False)
        allowed = lax.dynamic_index_in_dim(allowed_all, clipped, 0, keepdims=False)
        layer_in = lax.dynamic_index_in_dim(input_stack, source, 0, keepdims=False)
        activated, kept = layer_forward(layer_in.astype(jnp.float32), valid_mask, weights)
        sent_rows = activated.astype(jnp.bfloat16)
        unused_probs, logits, logsum = head_forward(sent_rows, head_w, allowed, valid_mask)
        tangent = (
            lax.dynamic_index_in_dim(cotangent[0], clipped, 0, keepdims=False).astype(jnp.float32)
            * live_flag
        )
        head_part, grad_sent = head_backward(
            tangent, sent_rows, head_w, allowed, valid_mask, logits, logsum
        )
        grad_act = grad_sent + grad_received.astype(jnp.float32)
        grad_input, layer_grads = layer_backward(grad_act, kept, valid_mask, weights)
        grad_list.append(grad_input)
        if timestep < micro_count:
            grad_received = shifted(grad_input.astype(jnp.bfloat16), "section", -1)
        frames = lax.dynamic_index_in_dim(spectra, clipped, 0, keepdims=False).reshape(
            row_count, -1
        )
        stem_part_in, stem_part_out = stem_backward(
            grad_input * first_flag, frames, stem_w_in, stem_w_out, valid_mask.reshape(-1, 1)
        )
        stem_in_sum = stem_in_sum + stem_part_in
        stem_out_sum = stem_out_sum + stem_part_out
        head_sum = head_sum + head_part
        shares = (
            lax.psum_scatter(layer_grads[0], "dp", scatter_dimension=1, tiled=True),
            lax.psum_scatter(layer_grads[1], "dp", scatter_dimension=1, tiled=True),
            lax.psum_scatter(layer_grads[2], "dp", scatter_dimension=0, tiled=True),
            lax.psum_scatter(layer_grads[3], "dp", scatter_dimension=0, tiled=True),
            lax.psum_scatter(layer_grads[4], "dp", scatter_dimension=0, tiled=True),
            lax.psum_scatter(layer_grads[5], "dp", scatter_dimension=1, tiled=True),
            lax.psum_scatter(layer_grads[6], "dp", scatter_dimension=0, tiled=True),
            lax.psum_scatter(layer_grads[7], "dp", scatter_dimension=1, tiled=True),
        )
        shard_sums = tuple(
            (running + share_part for running, share_part in zip(shard_sums, shares))
        )
    grad_stem_in, grad_stem_out, grad_head = (
        lax.psum_scatter(stem_in_sum, ("section", "dp"), scatter_dimension=1, tiled=True),
        lax.psum_scatter(stem_out_sum, ("section", "dp"), scatter_dimension=0, tiled=True),
        lax.psum_scatter(head_sum, ("section", "dp"), scatter_dimension=1, tiled=True),
    )
    grad_stack = jnp.stack(grad_list).reshape(micro_count + 1, groups, length, -1)
    input_grads = lax.dynamic_slice_in_dim(grad_stack, 1 - section_index, micro_count, 0)[None]
    return (
        activations,
        log_probs_out,
        input_grads,
        shard_sums[0][None],
        shard_sums[1][None],
        shard_sums[2][None],
        shard_sums[3][None],
        shard_sums[4][None],
        shard_sums[5][None],
        shard_sums[6][None],
        shard_sums[7][None],
        grad_stem_in,
        grad_stem_out,
        grad_head,
    )


def solution(mesh):
    return jax.shard_map(
        on_device,
        mesh=mesh,
        in_specs=(
            P(None, "dp", None, None),
            P(None, "dp"),
            P(None, "dp"),
            P(),
            P("section", None, "dp", None, None),
            P("section", None, "dp", None),
            P("section", None, "dp", None),
            P("section", "dp", None),
            P("section", "dp", None),
            P("section", "dp", None),
            P("section", None, "dp"),
            P("section", "dp", None),
            P("section", None, "dp"),
            P(None, ("section", "dp")),
            P(("section", "dp"), None),
            P(None, ("section", "dp")),
        ),
        out_specs=(
            P("section", None, "dp", None, None),
            P("section", None, "dp", None, None),
            P("section", None, "dp", None, None),
            P("section", None, "dp", None),
            P("section", None, "dp", None),
            P("section", "dp", None),
            P("section", "dp", None),
            P("section", "dp", None),
            P("section", None, "dp"),
            P("section", "dp", None),
            P("section", None, "dp"),
            P(None, ("section", "dp")),
            P(("section", "dp"), None),
            P(None, ("section", "dp")),
        ),
        check_vma=False,
    )
```

profile of v0, /device:TPU:0, one launch (start us, length us, event | category | flops | bytes accessed | tf_op | source)
XLA Modules:
  0.0 1709.3 jit_solution(10992221073761376238)
XLA Ops:
  25.7 24.5 %all-gather = bf16[1,6,512]{1,0,2:T(2,128)(2,1)S(1)} all-gather(bf16[1,6,32]{1,0,2:T(2,128)(2,1)S(1)} %copy.223), channel_id=2, replica_groups=mesh['section'=2,'dp'=16] {'dp'}, dimensions={2}, use_global_device_ids=true | all-gather | bytes 6528 | tf_op jit(solution)/shard_map/all_gather | solution.py:327
  50.4 11.7 slice_reduce_fusion
  62.1 18.4 %all-gather.5 = bf16[1,9,512]{1,0,2:T(2,128)(2,1)S(1)} all-gather(bf16[1,9,32]{1,0,2:T(2,128)(2,1)S(1)} %copy.227), channel_id=7, replica_groups=mesh['section'=2,'dp'=16] {'dp'}, dimensions={2}, use_global_device_ids=true | all-gather | bytes 9792 | tf_op jit(solution)/shard_map/all_gather | solution.py:325
  80.8 15.7 slice_reduce_fusion.12
  96.5 42.7 %all_gather.34 = bf16[256,512]{1,0:T(8,128)(2,1)} all-gather(bf16[8,512]{1,0:T(8,128)(2,1)S(1)} %convert_element_type.615), channel_id=1, replica_groups=mesh['section'=2,'dp'=16] {'section','dp'}, dimensions={0}, use_global_device_ids=true | all-gather | bytes 270336 | tf_op jit(solution)/shard_map/all_gather | solution.py:331
  139.3 37.8 %all_gather.33 = bf16[640,256]{0,1:T(8,128)(2,1)S(1)} all-gather(bf16[640,8]{0,1:T(8,128)(2,1)S(1)} %convert_element_type.613), channel_id=1, replica_groups=mesh['section'=2,'dp'=16] {'section','dp'}, dimensions={1}, use_global_device_ids=true | all-gather | bytes 337920 | tf_op jit(solution)/shard_map/all_gather | solution.py:330
  177.1 21.9 %all-gather.7 = bf16[1,512,512]{2,1,0:T(8,128)(2,1)} all-gather(bf16[1,32,512]{2,1,0:T(8,128)(2,1)S(1)} %convert_element_type.646), channel_id=9, replica_groups=mesh['section'=2,'dp'=16] {'dp'}, dimensions={1}, use_global_device_ids=true | all-gather | bytes 557056 | tf_op jit(solution)/shard_map/all_gather | solution.py:326
  199.0 18.9 %all-gather.4 = bf16[1,512,512]{2,1,0:T(8,128)(2,1)S(1)} all-gather(bf16[1,32,512]{2,1,0:T(8,128)(2,1)S(1)} %convert_element_type.637), channel_id=6, replica_groups=mesh['section'=2,'dp'=16] {'dp'}, dimensions={1}, use_global_device_ids=true | all-gather | bytes 557056 | tf_op jit(solution)/shard_map/all_gather | solution.py:323
  265.9 6.3 fusion.750
  280.5 8.2 collective-permute-done
  328.1 8.6 collective-permute-done.1
  400.5 16.3 fusion.205
  416.8 14.3 fusion.202
  451.0 6.1 fusion.767
  544.6 14.2 fusion.211
  558.8 14.2 fusion.208
  608.4 6.3 fusion.729
  616.8 6.7 fusion.774
  672.4 13.2 fusion.217
  685.7 14.2 fusion.214
  773.0 7.4 fusion.4
  797.1 6.4 fusion.3
  820.7 7.0 reduce-scatter.31.cloned.1.call-done
  829.1 131.6 %all-reduce.12.cloned.1.call-done = f32[640,256]{0,1:T(8,128)} async-done(((f32[640,256]{0,1:T(8,128)}), f32[640,256]{0,1:T(8,128)}) %all-reduce.12.cloned.1.call-update) | async-done | bytes 655376
  962.1 134.5 %reduce-scatter.15.cloned.1.call-done = f32[8,512]{1,0:T(8,128)} async-done(((f32[256,512]{1,0:T(8,128)}), f32[8,512]{1,0:T(8,128)}) %reduce-scatter.15.cloned.1.call-update) | async-done | bytes 16400 | tf_op jit(solution)/shard_map/reduce_scatter | solution.py:437
  1096.5 57.8 %reduce-scatter.29.cloned.1.call-done = f32[32,512]{1,0:T(8,128)} async-done(((f32[512,512]{1,0:T(8,128)}), f32[32,512]{1,0:T(8,128)}) %reduce-scatter.29.cloned.1.call-update) | async-done | bytes 65552 | tf_op jit(solution)/shard_map/reduce_scatter | solution.py:429
  1154.3 61.1 %reduce-scatter.25.cloned.1.call-done = f32[32,512]{1,0:T(8,128)} async-done(((f32[512,512]{1,0:T(8,128)}), f32[32,512]{1,0:T(8,128)}) %reduce-scatter.25.cloned.1.call-update) | async-done | bytes 65552 | tf_op jit(solution)/shard_map/reduce_scatter | solution.py:426
  1215.4 64.8 %reduce-scatter.27.cloned.1.call-done = f32[32,1024]{1,0:T(8,128)} async-done(((f32[512,1024]{1,0:T(8,128)}), f32[32,1024]{1,0:T(8,128)}) %reduce-scatter.27.cloned.1.call-update) | async-done | bytes 131088 | tf_op jit(solution)/shard_map/reduce_scatter | solution.py:427
  1280.1 138.9 %reduce-scatter.17.cloned.1.call-done = f32[512,32]{0,1:T(8,128)} async-done(((f32[512,1024]{0,1:T(8,128)}), f32[512,32]{0,1:T(8,128)}) %reduce-scatter.17.cloned.1.call-update) | async-done | bytes 65552 | tf_op jit(solution)/shard_map/reduce_scatter | solution.py:438
  1419.1 66.5 %reduce-scatter.23.cloned.1.call-done = f32[32,1536]{1,0:T(8,128)} async-done(((f32[512,1536]{1,0:T(8,128)}), f32[32,1536]{1,0:T(8,128)}) %reduce-scatter.23.cloned.1.call-update) | async-done | bytes 196624 | tf_op jit(solution)/shard_map/reduce_scatter | solution.py:425
  1485.5 108.1 %reduce-scatter.21.cloned.1.call-done = f32[2,128,512]{2,1,0:T(8,128)} async-done(((f32[2,2048,512]{2,1,0:T(8,128)}), f32[2,128,512]{2,1,0:T(8,128)}) %reduce-scatter.21.cloned.1.call-update) | async-done | bytes 524304 | tf_op jit(solution)/shard_map/reduce_scatter | solution.py:424
  1593.7 108.9 %reduce-scatter.19.cloned.1.call-done = f32[2,32,2048]{2,1,0:T(8,128)} async-done(((f32[2,512,2048]{2,1,0:T(8,128)}), f32[2,32,2048]{2,1,0:T(8,128)}) %reduce-scatter.19.cloned.1.call-update) | async-done | bytes 524304 | tf_op jit(solution)/shard_map/reduce_scatter | solution.py:423
  (1075 shorter events, 477.7 us)
Async XLA Ops:
  7.2 230.4 %all-gather.16.cloned.1.call-start = ((), (), s32[]{:S(2)}) async-start(), calls=%async_computation.13 | async-start | bytes 4456448 | tf_op jit(solution)/shard_map/all_gather | solution.py:320
  9.0 228.5 %all-gather.18.cloned.1.call-start = ((), (), s32[]{:S(2)}) async-start(), calls=%async_computation.14 | async-start | bytes 4456448 | tf_op jit(solution)/shard_map/all_gather | solution.py:321
  10.9 232.3 %all-gather.20.cloned.1.call-start = ((), (), s32[]{:S(2)}) async-start(), calls=%async_computation.15 | async-start | bytes 1671168 | tf_op jit(solution)/shard_map/all_gather | solution.py:322
  12.5 205.4 %copy-start.95 = (bf16[2,1,4096,80]{2,3,1,0:T(8,128)(2,1)S(1)}, bf16[2,1,4096,80]{2,3,1,0:T(8,128)(2,1)}, u32[]{:S(2)}) copy-start(bf16[2,1,4096,80]{2,3,1,0:T(8,128)(2,1)} %param.16) | copy-start | bytes 3932164
  12.6 245.9 %all-gather.22.cloned.1.call-start = ((), (), s32[]{:S(2)}) async-start(), calls=%async_computation.16 | async-start | bytes 1114112 | tf_op jit(solution)/shard_map/all_gather | solution.py:324
  14.3 353.6 %all-gather.14.cloned.1.call-start = ((), (), s32[]{:S(2)}) async-start(), calls=%async_computation.10 | async-start | bytes 1081344 | tf_op jit(solution)/shard_map/all_gather | solution.py:332
  15.8 803.6 %reduce-scatter.33.cloned.1.call-start = ((), (), s32[]{:S(2)}) async-start(), calls=%async_computation.24 | async-start | bytes 278528
  19.6 253.5 %copy-start.227 = (f32[1,1,512]{2,1,0:T(1,128)}, f32[1,1,512]{2,1,0:T(1,128)S(1)}, u32[]{:S(2)}) copy-start(f32[1,1,512]{2,1,0:T(1,128)S(1)} %get-tuple-element.221) | copy-start | bytes 6148
  19.7 299.4 %copy-start.229 = (f32[1,1,512]{2,1,0:T(1,128)}, f32[1,1,512]{2,1,0:T(1,128)S(1)}, u32[]{:S(2)}) copy-start(f32[1,1,512]{2,1,0:T(1,128)S(1)} %get-tuple-element.220) | copy-start | bytes 6148
  19.7 306.2 %copy-start.231 = (f32[1,1,512]{2,1,0:T(1,128)}, f32[1,1,512]{2,1,0:T(1,128)S(1)}, u32[]{:S(2)}) copy-start(f32[1,1,512]{2,1,0:T(1,128)S(1)} %get-tuple-element.219) | copy-start | bytes 6148
  19.7 306.7 %copy-start.204 = (f32[1,1,512]{2,1,0:T(1,128)}, f32[1,1,512]{2,1,0:T(1,128)S(1)}, u32[]{:S(2)}) copy-start(f32[1,1,512]{2,1,0:T(1,128)S(1)} %get-tuple-element.217) | copy-start | bytes 6148
  19.7 428.4 %copy-start.214 = (f32[1,1,512]{2,1,0:T(1,128)}, f32[1,1,512]{2,1,0:T(1,128)S(1)}, u32[]{:S(2)}) copy-start(f32[1,1,512]{2,1,0:T(1,128)S(1)} %get-tuple-element.218) | copy-start | bytes 6148
  274.3 14.4 collective-permute-start
  320.3 16.4 collective-permute-start.1
  338.3 105.0 %copy-start.212 = (f32[512]{0:T(512)}, f32[512]{0:T(512)S(1)}, u32[]{:S(2)}) copy-start(f32[512]{0:T(512)S(1)} %get-tuple-element.319) | copy-start | bytes 6148
  338.5 104.8 %copy-start.223 = (f32[512]{0:T(512)}, f32[512]{0:T(512)S(1)}, u32[]{:S(2)}) copy-start(f32[512]{0:T(512)S(1)} %add_rsqrt_fusion.17) | copy-start | bytes 6148
  341.9 93.8 %copy-start.241 = (f32[512]{0:T(512)}, f32[512]{0:T(512)S(1)}, u32[]{:S(2)}) copy-start(f32[512]{0:T(512)S(1)} %broadcast_multiply_fusion.52) | copy-start | bytes 6148
  342.5 93.2 %copy-start.251 = (f32[512]{0:T(512)}, f32[512]{0:T(512)S(1)}, u32[]{:S(2)}) copy-start(f32[512]{0:T(512)S(1)} %add_rsqrt_fusion.16) | copy-start | bytes 6148
  465.0 120.2 %copy-start.225 = (f32[512]{0:T(512)}, f32[512]{0:T(512)S(1)}, u32[]{:S(2)}) copy-start(f32[512]{0:T(512)S(1)} %add_rsqrt_fusion.11) | copy-start | bytes 6148
  465.0 49.5 %collective-permute-start.2 = (bf16[512,512]{0,1:T(8,128)(2,1)}, bf16[512,512]{0,1:T(8,128)(2,1)}, u32[]{:S(2)}, u32[]{:S(2)}) collective-permute-start(bf16[512,512]{0,1:T(8,128)(2,1)} %get-tuple-element.191), channel_id=1, source_target_pairs={{16,0},{17,1},{18,2},{19,3},{20,4},{21,5},{22,6},{23,7},{24,8},{25... | collective-permute-start | bytes 1572872 | tf_op jit(solution)/shard_map/ppermute | solution.py:18
  485.4 49.7 %copy-start.237 = (f32[512]{0:T(512)}, f32[512]{0:T(512)S(1)}, u32[]{:S(2)}) copy-start(f32[512]{0:T(512)S(1)} %broadcast_multiply_fusion.33) | copy-start | bytes 6148
  587.4 52.0 %collective-permute-start.3 = (bf16[512,512]{0,1:T(8,128)(2,1)}, bf16[512,512]{0,1:T(8,128)(2,1)}, u32[]{:S(2)}, u32[]{:S(2)}) collective-permute-start(bf16[512,512]{0,1:T(8,128)(2,1)} %get-tuple-element.185), channel_id=1, source_target_pairs={{16,0},{17,1},{18,2},{19,3},{20,4},{21,5},{22,6},{23,7},{24,8},{25... | collective-permute-start | bytes 1572872 | tf_op jit(solution)/shard_map/ppermute | solution.py:18
  713.0 114.7 %reduce-scatter.31.cloned.1.call-start = ((), (), s32[]{:S(2)}) async-start(), calls=%async_computation.23 | async-start | bytes 278528
  714.1 246.6 %all-reduce.12.cloned.1.call-start = ((), (), s32[]{:S(2)}) async-start(), calls=%async_computation.25 | async-start | bytes 1310720
  720.1 376.4 %reduce-scatter.15.cloned.1.call-start = ((), (), s32[]{:S(2)}) async-start(), calls=%async_computation.11 | async-start | bytes 540672 | tf_op jit(solution)/shard_map/reduce_scatter | solution.py:437
  724.8 429.5 %reduce-scatter.29.cloned.1.call-start = ((), (), s32[]{:S(2)}) async-start(), calls=%async_computation.22 | async-start | bytes 1114112 | tf_op jit(solution)/shard_map/reduce_scatter | solution.py:429
  730.2 485.1 %reduce-scatter.25.cloned.1.call-start = ((), (), s32[]{:S(2)}) async-start(), calls=%async_computation.20 | async-start | bytes 1114112 | tf_op jit(solution)/shard_map/reduce_scatter | solution.py:426
  735.6 544.6 %reduce-scatter.27.cloned.1.call-start = ((), (), s32[]{:S(2)}) async-start(), calls=%async_computation.21 | async-start | bytes 2228224 | tf_op jit(solution)/shard_map/reduce_scatter | solution.py:427
  740.8 678.3 %reduce-scatter.17.cloned.1.call-start = ((), (), s32[]{:S(2)}) async-start(), calls=%async_computation.12 | async-start | bytes 2162688 | tf_op jit(solution)/shard_map/reduce_scatter | solution.py:438
  746.7 738.8 %reduce-scatter.23.cloned.1.call-start = ((), (), s32[]{:S(2)}) async-start(), calls=%async_computation.19 | async-start | bytes 3342336 | tf_op jit(solution)/shard_map/reduce_scatter | solution.py:425
  754.4 839.3 %reduce-scatter.21.cloned.1.call-start = ((), (), s32[]{:S(2)}) async-start(), calls=%async_computation.18 | async-start | bytes 8912896 | tf_op jit(solution)/shard_map/reduce_scatter | solution.py:424
  780.4 922.2 %reduce-scatter.19.cloned.1.call-start = ((), (), s32[]{:S(2)}) async-start(), calls=%async_computation.17 | async-start | bytes 8912896 | tf_op jit(solution)/shard_map/reduce_scatter | solution.py:423
  (299 other events, 1620.3 us)
Sparse Core Ops, SparseCore 0:
  10.2 53.9 all-gather.15
  67.0 50.2 all-gather.17
  120.1 38.4 all-gather.19
  161.2 37.0 all-gather.21
  201.7 53.2 all-gather.13
  713.2 56.5 reduce-scatter.32
  773.3 54.3 reduce-scatter.30
  832.9 127.7 all-reduce.11
  963.6 132.8 reduce-scatter.14
  1100.6 53.6 reduce-scatter.28
  1158.9 56.4 reduce-scatter.24
  1219.5 60.5 reduce-scatter.26
  1283.1 135.9 reduce-scatter.16
  1423.3 62.2 reduce-scatter.22
  1490.0 103.5 reduce-scatter.20
  1598.2 104.3 reduce-scatter.18
where the time goes:
time: 1720 us; the launch traced here: 1710 us
  waiting for transfers between devices  896 us (52%)
  matrix products  355 us (21%)
  blocking collectives  164 us (10%)
  other arithmetic  141 us (8%)
  local copies, waits for them, and re-layouts  120 us (7%)
  between operations  18.6 us (1%)
    reduce_scatter x1, waiting for transfers between devices, on_device(): lax.psum_scatter(head_sum, ('section', 'dp'), scatter_dimension=1, tiled=...  139 us
    unnamed x19, waiting for transfers between devices  139 us
    reduce_scatter x1, waiting for transfers between devices, on_device(): lax.psum_scatter(stem_out_sum, ('section', 'dp'), scatter_dimension=0, ti...  134 us
    reduce_scatter x1, waiting for transfers between devices, on_device(): lax.psum_scatter(layer_grads[0], 'dp', scatter_dimension=1, tiled=True)  109 us
    reduce_scatter x1, waiting for transfers between devices, on_device(): lax.psum_scatter(layer_grads[1], 'dp', scatter_dimension=1, tiled=True)  108 us
    dot_general x53, matrix products, matmul(): return jnp.dot(left, right, preferred_element_type=jnp.float32)  101 us
    dot_general x33, matrix products, matmul_left(): lax.dot_general(left, right, (((0,), (0,)), ((), ())), preferred_element_...  73.9 us
    reduce_scatter x1, waiting for transfers between devices, on_device(): lax.psum_scatter(layer_grads[2], 'dp', scatter_dimension=0, tiled=True)  66.5 us
  transfers between devices with their start and end apart: 20, of which 12 were waited for; matrix products, arithmetic and copies ran while one was open for 20% of the time, Pallas kernels for 0%

commit v1 on v0

v1 whole, which is shorter than its diff:
```python
import types

import jax
import jax.numpy as jnp
from jax import lax
from jax.experimental import pallas as pl
from jax.experimental.pallas import tpu as pltpu
from jax.sharding import PartitionSpec as P

D = 512
HEADS = 8
HDIM = 64
FF = 2048
TAPS = 9
EPS = 1e-05
MASKED = -1e30
RB = 512
BOTH = ("section", "dp")
BF = jnp.bfloat16
F32 = jnp.float32

FEED, ATTN, CONV = 256, 128, 96
FLAT = 32
SMALL = 16


def dotn(a, b):
    return lax.dot_general(a, b, (((1,), (0,)), ((), ())), preferred_element_type=F32)


def dotr(a, b):
    return lax.dot_general(a, b, (((1,), (1,)), ((), ())), preferred_element_type=F32)


def dotl(a, b):
    return lax.dot_general(a, b, (((0,), (0,)), ((), ())), preferred_element_type=F32)


def sigmoid(v):
    return 0.5 * jnp.tanh(0.5 * v) + 0.5


def unit_rows(v):
    c = v - jnp.mean(v, axis=-1, keepdims=True)
    r = lax.rsqrt(jnp.mean(c * c, axis=-1, keepdims=True) + EPS)
    return c * r, r


def unit_back(dn, u, r, gain):
    du = dn * gain
    dv = r * (du - jnp.mean(du, axis=-1, keepdims=True) - u * jnp.mean(du * u, axis=-1, keepdims=True))
    return dv, jnp.sum(dn * u, axis=0, keepdims=True)


def row_mask(length, start, rows, columns):
    return (lax.broadcasted_iota(jnp.int32, (rows, columns), 0) + start < length).astype(F32)


def row_loop(body):
    for i in range(512 // RB):
        body(slice(i * RB, i * RB + RB), i * RB)


def piece_of(ids, cr, a, b, zk):
    pc = ids[3] ^ cr
    px = ids[0] ^ (a + pc * (b - a))
    py = ids[2] ^ (b + pc * (a - b))
    pz = ids[1] ^ zk
    return px, pz * 4 + py * 2 + pc


def pieces():
    return [(cr, a, b, zk) for cr in range(2) for a in range(2) for b in range(2) for zk in range(4)]


def start_load(ids, bufs, row, rows, scr, sem, flat=False):
    for cr, a, b, zk in pieces():
        px, d = piece_of(ids, cr, a, b, zk)
        src = bufs[cr * 4 + a * 2 + b].at[zk, row : row + rows]
        if flat:
            dst = scr.at[px * 16 + d]
        else:
            dst = scr.at[d, pl.ds(pl.multiple_of(px * rows, 16), rows)]
        pltpu.make_async_copy(src, dst, sem).start()


def wait_load(scr, sem):
    pltpu.make_async_copy(scr, scr, sem).wait()


def start_store(ids, scr, keep, send, row, rows, sem, flat=False):
    for cr, a, b, zk in pieces():
        px, d = piece_of(ids, cr, a, b, zk)
        if flat:
            src = scr.at[px * 16 + d]
        else:
            src = scr.at[d, pl.ds(pl.multiple_of(px * rows, 16), rows)]
        dst = (send if cr else keep).at[a * 8 + b * 4 + zk, row : row + rows]
        pltpu.make_async_copy(src, dst, sem).start()


def wait_store(scr, sem):
    pltpu.make_async_copy(scr, scr, sem).wait()


def in_block(w, j):
    return w[:, 32 * j : 32 * j + 32, :].reshape(512, 512)


def out_block(w, j):
    return w[4 * j : 4 * j + 4, 128:256, :].reshape(512, 512)


def feed_fwd(x, w, gain, hid, out):
    def body(rs, start):
        v = x[rs, :].astype(F32)
        u, _ = unit_rows(v)
        n = (u * gain).astype(BF)
        total = jnp.zeros((RB, 512), F32)
        for j in range(4):
            h = dotn(n, in_block(w, j))
            hid[rs, 512 * j : 512 * j + 512] = h.astype(BF)
            total = total + dotn((h * sigmoid(h)).astype(BF), out_block(w, j))
        out[rs, :] = v + 0.5 * total

    row_loop(body)


def feed_bwd(dx, x, hid, w, gain, out, gw, small, row, s):
    def body(rs, start):
        g = dx[rs, :]
        v = x[rs, :].astype(F32)
        u, r = unit_rows(v)
        s.n[rs, :] = (u * gain).astype(BF)
        d = (0.5 * g).astype(BF)
        s.d[rs, :] = d
        dn = jnp.zeros((RB, 512), F32)
        for j in range(4):
            h = hid[rs, 512 * j : 512 * j + 512].astype(F32)
            sg = sigmoid(h)
            s.act[rs, 512 * j : 512 * j + 512] = (h * sg).astype(BF)
            dh = (dotr(d, out_block(w, j)) * (sg * (1.0 + h * (1.0 - sg)))).astype(BF)
            s.dh[rs, 512 * j : 512 * j + 512] = dh
            dn = dn + dotr(dh, in_block(w, j))
        dv, gg = unit_back(dn, u, r, gain)
        out[rs, :] = g + dv
        small[row : row + 1, :] += gg

    row_loop(body)
    for j in range(4):
        cols = slice(512 * j, 512 * j + 512)
        gw[:, 32 * j : 32 * j + 32, :] = dotl(s.n[...], s.dh[:, cols]).astype(BF).reshape(16, 32, 512)
        gw[4 * j : 4 * j + 4, 128:256, :] = dotl(s.act[:, cols], s.d[...]).astype(BF).reshape(4, 128, 512)


def lanes_of(half, axis=1, count=1):
    shape = (count, 128) if axis else (128, count)
    return (lax.broadcasted_iota(jnp.int32, shape, axis) + 64 * half) % 128 - 64


def attn_fwd(x, w, gain, length, qkv, ls, mixt, out):
    def project(rs, start):
        u, _ = unit_rows(x[rs, :])
        n = (u * gain).astype(BF)
        for j in range(3):
            qkv[rs, 512 * j : 512 * j + 512] = dotn(n, in_block(w, j)).astype(BF)

    row_loop(project)

    for hp in range(4):
        at = hp * 128
        k = qkv[:, pl.ds(512 + at, 128)].astype(F32)
        vt = qkv[:, pl.ds(1024 + at, 128)].astype(F32).T
        outside = jnp.where(lax.broadcasted_iota(jnp.int32, (512, 128), 0) < length, 0.0, MASKED)
        kx, vx = [], []
        for hh in range(2):
            free = lanes_of(hh)
            kx.append(jnp.where(free < 0, k, jnp.where(free == 0, outside, 0.0)).astype(BF))
            free = lanes_of(hh, 0, 512)
            vx.append(jnp.where(free < 0, vt, jnp.where(free == 0, 1.0, 0.0)).astype(BF))

        def body(rs, start):
            q = qkv[rs, pl.ds(at, 128)].astype(F32) * HDIM**-0.5
            parts = []
            for hh in range(2):
                free = lanes_of(hh)
                qx = jnp.where(free < 0, q, jnp.where(free == 0, 1.0, 0.0)).astype(BF)
                sc = dotr(kx[hh], qx)
                top = jnp.max(sc, axis=0, keepdims=True)
                both = dotn(vx[hh], jnp.exp(sc - top).astype(BF))
                tot = both[64 * (1 - hh) : 64 * (1 - hh) + 1, :]
                parts.append(both * (1.0 / tot))
                ls[pl.ds(hp * 2 + hh, 1), rs] = top + jnp.log(tot)
            mixt[pl.ds(at, 128), rs] = jnp.where(lanes_of(0, 0, RB) < 0, parts[0], parts[1]).astype(BF)

        row_loop(body)

    def project_out(rs, start):
        out[rs, :] = x[rs, :] + dotl(mixt[:, rs], w[:, 96:128, :].reshape(512, 512))

    row_loop(project_out)


def attn_bwd(dx, x, qkv, ls, mixt, w, gain, length, out, gw, small, row, s):
    def first(rs, start):
        u, _ = unit_rows(x[rs, :])
        s.n[rs, :] = (u * gain).astype(BF)
        d = dx[rs, :].astype(BF)
        s.d[rs, :] = d
        s.dm[:, rs] = dotr(w[:, 96:128, :].reshape(512, 512), d).astype(BF)

    row_loop(first)
    gw[:, 96:128, :] = dotn(mixt[...], s.d[...]).astype(BF).reshape(16, 32, 512)

    for hp in range(4):
        at = hp * 128
        s.dq[...] = jnp.zeros((128, 512), F32)
        q = qkv[:, pl.ds(at, 128)].astype(F32) * HDIM**-0.5
        kt = qkv[:, pl.ds(512 + at, 128)].astype(F32).T * HDIM**-0.5
        dmt = s.dm[pl.ds(at, 128), :].astype(F32)
        prod = dmt * mixt[pl.ds(at, 128), :].astype(F32)
        qx, qs, dms, deltas, sums = [], [], [], [], []
        for hh in range(2):
            free = lanes_of(hh)
            qs.append(jnp.where(free < 0, q, 0.0).astype(BF))
            qx.append(jnp.where(free < 0, q, jnp.where(free == 0, 1.0, 0.0)).astype(BF))
            free = lanes_of(hh, 0, 512)
            dms.append(jnp.where(free < 0, dmt, 0.0).astype(BF))
            deltas.append(jnp.sum(prod[64 * hh : 64 * hh + 64, :], axis=0, keepdims=True))
            s.kt[128 * hh : 128 * hh + 128, :] = jnp.where(free < 0, kt, 0.0).astype(BF)
            sums.append(ls[pl.ds(hp * 2 + hh, 1), :])

        def body(rs, start):
            k = qkv[rs, pl.ds(512 + at, 128)].astype(F32)
            v = qkv[rs, pl.ds(1024 + at, 128)]
            outside = jnp.where(lax.broadcasted_iota(jnp.int32, (RB, 128), 0) + start < length, 0.0, MASKED)
            dk = jnp.zeros((RB, 128), F32)
            dv = jnp.zeros((RB, 128), F32)
            for hh in range(2):
                free = lanes_of(hh)
                kx = jnp.where(free < 0, k, jnp.where(free == 0, outside, 0.0)).astype(BF)
                p = jnp.exp(dotr(kx, qx[hh]) - sums[hh])
                ds = (p * (dotn(v, dms[hh]) - deltas[hh])).astype(BF)
                dv = dv + dotr(p.astype(BF), dms[hh])
                dk = dk + dotn(ds, qs[hh])
                s.dq[...] += dotn(s.kt[128 * hh : 128 * hh + 128, rs], ds)
            s.dpk[rs, pl.ds(512 + at, 128)] = dk.astype(BF)
            s.dpk[rs, pl.ds(1024 + at, 128)] = dv.astype(BF)

        row_loop(body)
        s.dpk[:, pl.ds(at, 128)] = s.dq[...].T.astype(BF)

    def last(rs, start):
        u, r = unit_rows(x[rs, :])
        dn = jnp.zeros((RB, 512), F32)
        for j in range(3):
            dn = dn + dotr(s.dpk[rs, 512 * j : 512 * j + 512], in_block(w, j))
        dv, gg = unit_back(dn, u, r, gain)
        out[rs, :] = dx[rs, :] + dv
        small[row : row + 1, :] += gg

    row_loop(last)
    for j in range(3):
        gw[:, 32 * j : 32 * j + 32, :] = (
            dotl(s.n[...], s.dpk[:, 512 * j : 512 * j + 512]).astype(BF).reshape(16, 32, 512)
        )


PAD = 8


def conv_fwd(x, w, prm, length, gated, deep, out, pad):
    pad[0:PAD, :] = jnp.zeros((PAD, 512), F32)
    pad[PAD + 512 : 2 * PAD + 512, :] = jnp.zeros((PAD, 512), F32)

    def first(rs, start):
        u, _ = unit_rows(x[rs, :])
        n = (u * prm[TAPS + 2 : TAPS + 3, :]).astype(BF)
        a = dotn(n, in_block(w, 0))
        b = dotn(n, in_block(w, 1))
        gated[rs, 0:512] = a
        gated[rs, 512:1024] = b
        pad[pl.ds(start + PAD, RB), :] = a * sigmoid(b) * row_mask(length, start, RB, 512)

    row_loop(first)
    for i in range(512 // RB):
        total = jnp.zeros((RB, 512), F32)
        for t in range(TAPS):
            begin = i * RB + PAD - TAPS // 2 + t
            total = total + prm[t : t + 1, :] * pad[begin : begin + RB, :]
        deep[i * RB : i * RB + RB, :] = total

    def last(rs, start):
        u, _ = unit_rows(deep[rs, :])
        m = u * prm[TAPS + 3 : TAPS + 4, :]
        act = (m * sigmoid(m)).astype(BF)
        out[rs, :] = x[rs, :] + dotn(act, w[:, 64:96, :].reshape(512, 512))

    row_loop(last)


def conv_bwd(dx, x, gated, deep, w, prm, length, out, gw, small, s):
    for pad in (s.pad, s.back):
        pad[0:PAD, :] = jnp.zeros((PAD, 512), F32)
        pad[PAD + 512 : 2 * PAD + 512, :] = jnp.zeros((PAD, 512), F32)
    gain_in = prm[TAPS + 2 : TAPS + 3, :]
    gain_mid = prm[TAPS + 3 : TAPS + 4, :]

    def first(rs, start):
        padded = pl.ds(start + PAD, RB)
        d = dx[rs, :].astype(BF)
        s.d[rs, :] = d
        u3, r3 = unit_rows(deep[rs, :])
        m = u3 * gain_mid
        sg = sigmoid(m)
        s.act[rs, :] = (m * sg).astype(BF)
        dmid = dotr(d, w[:, 64:96, :].reshape(512, 512)) * (sg * (1.0 + m * (1.0 - sg)))
        ddeep, gg = unit_back(dmid, u3, r3, gain_mid)
        s.back[padded, :] = ddeep
        small[TAPS + 3 : TAPS + 4, :] += gg
        s.pad[padded, :] = (
            gated[rs, 0:512] * sigmoid(gated[rs, 512:1024]) * row_mask(length, start, RB, 512)
        )

    row_loop(first)
    gw[:, 64:96, :] = dotl(s.act[...], s.d[...]).astype(BF).reshape(16, 32, 512)
    for i in range(512 // RB):
        rows = slice(i * RB, i * RB + RB)
        ddeep = s.back[PAD + i * RB : PAD + i * RB + RB, :]
        dglu = jnp.zeros((RB, 512), F32)
        for t in range(TAPS):
            begin = i * RB + PAD - TAPS // 2 + t
            small[t : t + 1, :] += jnp.sum(ddeep * s.pad[begin : begin + RB, :], axis=0, keepdims=True)
            begin = i * RB + PAD + TAPS // 2 - t
            dglu = dglu + prm[t : t + 1, :] * s.back[begin : begin + RB, :]
        dglu = dglu * row_mask(length, i * RB, RB, 512)
        sg = sigmoid(gated[rows, 512:1024])
        ga = dglu * sg
        s.dga[rows, :] = ga.astype(BF)
        s.dgb[rows, :] = (ga * gated[rows, 0:512] * (1.0 - sg)).astype(BF)

    def last(rs, start):
        u, r = unit_rows(x[rs, :])
        s.n[rs, :] = (u * gain_in).astype(BF)
        dn = dotr(s.dga[rs, :], in_block(w, 0)) + dotr(s.dgb[rs, :], in_block(w, 1))
        dv, gg = unit_back(dn, u, r, gain_in)
        out[rs, :] = dx[rs, :] + dv
        small[TAPS + 2 : TAPS + 3, :] += gg

    row_loop(last)
    gw[:, 0:32, :] = dotl(s.n[...], s.dga[...]).astype(BF).reshape(16, 32, 512)
    gw[:, 32:64, :] = dotl(s.n[...], s.dgb[...]).astype(BF).reshape(16, 32, 512)


def finish_fwd(x4, prm, length, sent):
    def body(rs, start):
        u, _ = unit_rows(x4[rs, :])
        sent[rs, :] = (u * prm[TAPS + 5 : TAPS + 6, :] * row_mask(length, start, RB, 512)).astype(BF)

    row_loop(body)


def head_rows(sent, w, permit):
    logits = dotr(sent, w)
    top = jnp.max(jnp.where(permit, logits, MASKED), axis=-1, keepdims=True)
    e = jnp.exp(jnp.where(permit, logits - top, MASKED))
    return logits, top + jnp.log(jnp.sum(e, axis=-1, keepdims=True))


def head_bwd(x4, sent, w, allowed, cot, prm, length, extra, out, gl, gsent, small):
    permit = allowed[...] > 0
    gain = prm[TAPS + 5 : TAPS + 6, :]

    def body(rs, start):
        hw = w[...].reshape(1024, 512)
        logits, logsum = head_rows(sent[rs, :], hw, permit)
        weighted = jnp.where(permit, cot[rs, :].astype(F32), 0.0) * row_mask(length, start, RB, 1024)
        probs = jnp.exp(jnp.where(permit, logits - logsum, MASKED))
        g = (weighted - probs * jnp.sum(weighted, axis=-1, keepdims=True)).astype(BF)
        gl[rs, :] = g
        gs = dotn(g, hw)
        if extra is not None:
            gs = gs + extra[rs, :].astype(F32)
        u, r = unit_rows(x4[rs, :])
        dv, gg = unit_back(gs * row_mask(length, start, RB, 512), u, r, gain)
        out[rs, :] = dv
        small[TAPS + 5 : TAPS + 6, :] += gg

    row_loop(body)


ANY, VMEM, SMEM = pl.ANY, pltpu.VMEM, pltpu.SMEM


def run(body, micros, ins, outs, scratch):
    flat = []
    for value, space in ins.values():
        flat += [(array, space) for array in (value if isinstance(value, list) else [value])]

    def kernel(*refs):
        left = list(refs)
        ns = types.SimpleNamespace()
        for key, (value, _) in ins.items():
            if isinstance(value, list):
                setattr(ns, key, [left.pop(0) for _ in value])
            else:
                setattr(ns, key, left.pop(0))
        for key in [*outs, *scratch]:
            setattr(ns, key, left.pop(0))
        ns.sems = left.pop(0)
        body(ns)

    result = pl.pallas_call(
        kernel,
        out_shape=[jax.ShapeDtypeStruct(shape, dtype) for shape, dtype, _ in outs.values()],
        in_specs=[pl.BlockSpec(memory_space=space) for _, space in flat],
        out_specs=[pl.BlockSpec(memory_space=space) for _, _, space in outs.values()],
        scratch_shapes=[pltpu.VMEM(shape, dtype) for shape, dtype in scratch.values()] + [pltpu.SemaphoreType.DMA((8,))],
        compiler_params=pltpu.CompilerParams(vmem_limit_bytes=58 * 2**20),
        cost_estimate=pl.CostEstimate(flops=int(micros * 1.1e9), bytes_accessed=2**20, transcendentals=0),
        name=body.__name__,
    )(*[array for array, _ in flat])
    return types.SimpleNamespace(**dict(zip(outs, result)))


ROWS = (512, 512)


def kernel_stem_feed(ids, bufs, frames):
    def stem_feed(k):
        start_load(k.ids, k.bufs, 0, FLAT, k.stem, k.sems.at[0], flat=True)
        start_load(k.ids, k.bufs, FLAT, FEED // 2, k.w, k.sems.at[1])
        wait_load(k.stem, k.sems.at[0])
        stem = k.stem[...].astype(F32)
        for layer in range(2):
            for z in range(4):
                part = jnp.zeros((8, 512), F32)
                for q in range(4):
                    part = part + stem[layer * 16 + z * 4 + q, 24:32, :]
                k.prm[layer, 0:8, 128 * z : 128 * z + 128] = part[:, 0:128]
                k.prm[layer, 8:16, 128 * z : 128 * z + 128] = part[:, 128:256]
        k.win_a[...] = stem[:, 0:8, :].reshape(256, 512).astype(BF)
        k.win_b[...] = stem[:, 8:16, 0:128].reshape(256, 128).astype(BF)
        k.wout[...] = stem[:, 16:24, :].reshape(256, 512).astype(BF)

        def rows(rs, start):
            pre = dotr(k.frames[rs, 0:512], k.win_a[...]) + dotr(k.frames[rs, 512:640], k.win_b[...])
            k.pre[rs, :] = pre
            x = dotn((pre * sigmoid(pre)).astype(BF), k.wout[...])
            k.x0[rs, :] = (x * row_mask(k.ids[4], start, RB, 512)).astype(BF)

        row_loop(rows)
        wait_load(k.w, k.sems.at[1])
        feed_fwd(k.x0, k.w, k.prm[0, TAPS : TAPS + 1, :], k.hid, k.x1)

    return run(
        stem_feed,
        9,
        dict(ids=(ids, SMEM), bufs=(bufs, ANY), frames=(frames, VMEM)),
        dict(
            prm=((2, SMALL, 512), F32, VMEM),
            pre=((512, 256), F32, VMEM),
            win_a=((256, 512), BF, VMEM),
            win_b=((256, 128), BF, VMEM),
            wout=((256, 512), BF, VMEM),
            x0=(ROWS, BF, VMEM),
            hid=((512, FF), BF, VMEM),
            x1=(ROWS, F32, VMEM),
        ),
        dict(stem=((32, FLAT, 512), BF), w=((16, FEED, 512), BF)),
    )


ATTN_OUTS = dict(
    qkv=((512, 1536), BF, VMEM),
    ls=((8, 512), F32, VMEM),
    mixed=(ROWS, BF, VMEM),
    x2=(ROWS, F32, VMEM),
)
CONV_OUTS = dict(
    gated=((512, 1024), F32, VMEM),
    deep=(ROWS, F32, VMEM),
    x3=(ROWS, F32, VMEM),
)


def kernel_rest_first(ids, bufs, prm, x1):
    def rest_first(k):
        start_load(k.ids, k.bufs, 0, ATTN // 2, k.wa, k.sems.at[0])
        start_load(k.ids, k.bufs, ATTN // 2, CONV // 2, k.wc, k.sems.at[1])
        start_load(k.ids, k.bufs, ATTN // 2 + CONV // 2, FEED // 2, k.wf, k.sems.at[2])
        prm = k.prm.at[0]
        wait_load(k.wa, k.sems.at[0])
        attn_fwd(k.x1, k.wa, prm[TAPS + 1 : TAPS + 2, :], k.ids[4], k.qkv, k.ls, k.mixed, k.x2)
        wait_load(k.wc, k.sems.at[1])
        conv_fwd(k.x2, k.wc, prm, k.ids[4], k.gated, k.deep, k.x3, k.pad)
        wait_load(k.wf, k.sems.at[2])
        feed_fwd(k.x3, k.wf, prm[TAPS + 4 : TAPS + 5, :], k.hid, k.x4)
        finish_fwd(k.x4, prm, k.ids[4], k.sent)

    return run(
        rest_first,
        24,
        dict(ids=(ids, SMEM), bufs=(bufs, ANY), prm=(prm, VMEM), x1=(x1, VMEM)),
        ATTN_OUTS
        | CONV_OUTS
        | dict(hid=((512, FF), BF, VMEM), x4=(ROWS, F32, VMEM), sent=(ROWS, BF, VMEM)),
        dict(
            wa=((16, ATTN, 512), BF),
            wc=((16, CONV, 512), BF),
            wf=((16, FEED, 512), BF),
            pad=((512 + 2 * PAD, 512), F32),
        ),
    )


def kernel_first_second(ids, bufs, prm, x0):
    def first_second(k):
        start_load(k.ids, k.bufs, 0, FEED // 2, k.wf, k.sems.at[2])
        start_load(k.ids, k.bufs, FEED // 2, ATTN // 2, k.wa, k.sems.at[0])
        start_load(k.ids, k.bufs, FEED // 2 + ATTN // 2, CONV // 2, k.wc, k.sems.at[1])
        prm = k.prm.at[1]
        wait_load(k.wf, k.sems.at[2])
        feed_fwd(k.x0, k.wf, prm[TAPS : TAPS + 1, :], k.hid, k.x1)
        wait_load(k.wa, k.sems.at[0])
        attn_fwd(k.x1, k.wa, prm[TAPS + 1 : TAPS + 2, :], k.ids[4], k.qkv, k.ls, k.mixed, k.x2)
        wait_load(k.wc, k.sems.at[1])
        conv_fwd(k.x2, k.wc, prm, k.ids[4], k.gated, k.deep, k.x3, k.pad)

    return run(
        first_second,
        24,
        dict(ids=(ids, SMEM), bufs=(bufs, ANY), prm=(prm, VMEM), x0=(x0, VMEM)),
        dict(hid=((512, FF), BF, VMEM), x1=(ROWS, F32, VMEM)) | ATTN_OUTS | CONV_OUTS,
        dict(
            wa=((16, ATTN, 512), BF),
            wc=((16, CONV, 512), BF),
            wf=((16, FEED, 512), BF),
            pad=((512 + 2 * PAD, 512), F32),
        ),
    )


def kernel_turn(ids, feed_bufs, conv_bufs, prm, x3, cot, allowed, x2, gated, deep):
    def turn(k):
        start_load(k.ids, k.fbufs, 0, FEED // 2, k.wf, k.sems.at[0])
        start_load(k.ids, k.fbufs, FEED // 2, FLAT, k.wh, k.sems.at[1], flat=True)
        start_load(k.ids, k.cbufs, FEED // 2 + ATTN // 2, CONV // 2, k.wc, k.sems.at[2])
        prm = k.prm.at[1]
        k.small[...] = jnp.zeros((SMALL, 512), F32)
        wait_load(k.wf, k.sems.at[0])
        feed_fwd(k.x3, k.wf, prm[TAPS + 4 : TAPS + 5, :], k.hid, k.x4)
        finish_fwd(k.x4, prm, k.ids[4], k.sent)
        wait_load(k.wh, k.sems.at[1])
        head_bwd(k.x4, k.sent, k.wh, k.allowed, k.cot, prm, k.ids[4], None, k.dx4, k.gl, None, k.small)
        k.ghead[...] = dotl(k.gl[...], k.sent[...])
        feed_bwd(
            k.dx4,
            k.x3,
            k.hid,
            k.wf,
            prm[TAPS + 4 : TAPS + 5, :],
            k.dx3,
            k.gf,
            k.small,
            TAPS + 4,
            k,
        )
        start_store(k.ids, k.gf, k.keep, k.send, 0, FEED // 2, k.sems.at[3])
        wait_load(k.wc, k.sems.at[2])
        s = types.SimpleNamespace(
            n=k.n, d=k.d, act=k.act.at[:, 0:512], dga=k.dh.at[:, 0:512], dgb=k.dh.at[:, 512:1024], pad=k.pad, back=k.back
        )
        conv_bwd(k.dx3, k.x2, k.gated, k.deep, k.wc, prm, k.ids[4], k.dx2, k.gc, k.small, s)
        start_store(k.ids, k.gc, k.keep, k.send, FEED // 2, CONV // 2, k.sems.at[4])
        wait_store(k.gf, k.sems.at[3])
        wait_store(k.gc, k.sems.at[4])

    rows = FEED // 2 + CONV // 2
    return run(
        turn,
        32,
        dict(
            ids=(ids, SMEM),
            fbufs=(feed_bufs, ANY),
            cbufs=(conv_bufs, ANY),
            prm=(prm, VMEM),
            x3=(x3, VMEM),
            cot=(cot, VMEM),
            allowed=(allowed, VMEM),
            x2=(x2, VMEM),
            gated=(gated, VMEM),
            deep=(deep, VMEM),
        ),
        dict(
            sent=(ROWS, BF, VMEM),
            ghead=((1024, 512), F32, VMEM),
            dx2=(ROWS, F32, VMEM),
            small=((SMALL, 512), F32, VMEM),
            keep=((16, rows, 512), BF, ANY),
            send=((16, rows, 512), BF, ANY),
        ),
        dict(
            wf=((16, FEED, 512), BF),
            wh=((32, FLAT, 512), BF),
            wc=((16, CONV, 512), BF),
            gf=((16, FEED, 512), BF),
            gc=((16, CONV, 512), BF),
            hid=((512, FF), BF),
            x4=(ROWS, F32),
            gl=((512, 1024), BF),
            dx4=(ROWS, F32),
            dx3=(ROWS, F32),
            n=(ROWS, BF),
            d=(ROWS, BF),
            act=((512, FF), BF),
            dh=((512, FF), BF),
            pad=((512 + 2 * PAD, 512), F32),
            back=((512 + 2 * PAD, 512), F32),
        ),
    )


def kernel_back_late(ids, feed_bufs, conv_bufs, head_bufs, prm, x4, sent, cot, allowed, ig, x3, hid, x2, gated, deep, ghead):
    def back_late(k):
        start_load(k.ids, k.hbufs, FEED // 2, FLAT, k.wh, k.sems.at[1], flat=True)
        start_load(k.ids, k.fbufs, ATTN // 2 + CONV // 2, FEED // 2, k.wf, k.sems.at[0])
        start_load(k.ids, k.cbufs, ATTN // 2, CONV // 2, k.wc, k.sems.at[2])
        prm = k.prm.at[0]
        k.small[...] = jnp.zeros((SMALL, 512), F32)
        wait_load(k.wh, k.sems.at[1])
        head_bwd(k.x4, k.sent, k.wh, k.allowed, k.cot, prm, k.ids[4], k.ig, k.dx4, k.gl, None, k.small)
        k.gh[...] = (k.ghead[...] + dotl(k.gl[...], k.sent[...])).astype(BF).reshape(32, FLAT, 512)
        start_store(k.ids, k.gh, k.keep, k.send, FEED // 2 + CONV // 2, FLAT, k.sems.at[5], flat=True)
        wait_load(k.wf, k.sems.at[0])
        feed_bwd(
            k.dx4,
            k.x3,
            k.hid,
            k.wf,
            prm[TAPS + 4 : TAPS + 5, :],
            k.dx3,
            k.gf,
            k.small,
            TAPS + 4,
            k,
        )
        start_store(k.ids, k.gf, k.keep, k.send, 0, FEED // 2, k.sems.at[3])
        wait_load(k.wc, k.sems.at[2])
        s = types.SimpleNamespace(
            n=k.n, d=k.d, act=k.act.at[:, 0:512], dga=k.dh.at[:, 0:512], dgb=k.dh.at[:, 512:1024], pad=k.pad, back=k.back
        )
        conv_bwd(k.dx3, k.x2, k.gated, k.deep, k.wc, prm, k.ids[4], k.dx2, k.gc, k.small, s)
        start_store(k.ids, k.gc, k.keep, k.send, FEED // 2, CONV // 2, k.sems.at[4])
        wait_store(k.gh, k.sems.at[5])
        wait_store(k.gf, k.sems.at[3])
        wait_store(k.gc, k.sems.at[4])

    rows = FEED // 2 + CONV // 2 + FLAT
    return run(
        back_late,
        28,
        dict(
            ids=(ids, SMEM),
            fbufs=(feed_bufs, ANY),
            cbufs=(conv_bufs, ANY),
            hbufs=(head_bufs, ANY),
            prm=(prm, VMEM),
            x4=(x4, VMEM),
            sent=(sent, VMEM),
            cot=(cot, VMEM),
            allowed=(allowed, VMEM),
            ig=(ig, VMEM),
            x3=(x3, VMEM),
            hid=(hid, VMEM),
            x2=(x2, VMEM),
            gated=(gated, VMEM),
            deep=(deep, VMEM),
            ghead=(ghead, VMEM),
        ),
        dict(
            dx2=(ROWS, F32, VMEM),
            small=((SMALL, 512), F32, VMEM),
            keep=((16, rows, 512), BF, ANY),
            send=((16, rows, 512), BF, ANY),
        ),
        dict(
            wf=((16, FEED, 512), BF),
            wh=((32, FLAT, 512), BF),
            wc=((16, CONV, 512), BF),
            gf=((16, FEED, 512), BF),
            gc=((16, CONV, 512), BF),
            gh=((32, FLAT, 512), BF),
            gl=((512, 1024), BF),
            dx4=(ROWS, F32),
            dx3=(ROWS, F32),
            n=(ROWS, BF),
            d=(ROWS, BF),
            act=((512, FF), BF),
            dh=((512, FF), BF),
            pad=((512 + 2 * PAD, 512), F32),
            back=((512 + 2 * PAD, 512), F32),
        ),
    )


def kernel_back_early(layer, ids, attn_bufs, attn_row, feed_bufs, feed_row, prm, dx2, x1, qkv, ls, mixed, x0, hid, stem):
    def back_early_stem(k):
        start_load(k.ids, k.abufs, attn_row, ATTN // 2, k.wa, k.sems.at[0])
        start_load(k.ids, k.fbufs, feed_row, FEED // 2, k.wf, k.sems.at[1])
        prm = k.prm.at[layer]
        k.small[...] = jnp.zeros((SMALL, 512), F32)
        wait_load(k.wa, k.sems.at[0])
        s = types.SimpleNamespace(n=k.n, d=k.d, dm=k.dm, dpk=k.act.at[:, 0:1536], dq=k.dq, kt=k.kt)
        attn_bwd(
            k.dx2, k.x1, k.qkv, k.ls, k.mixed, k.wa, prm[TAPS + 1 : TAPS + 2, :], k.ids[4], k.dx1, k.ga, k.small, TAPS + 1, s
        )
        start_store(k.ids, k.ga, k.keep, k.send, 0, ATTN // 2, k.sems.at[2])
        wait_load(k.wf, k.sems.at[1])
        feed_bwd(
            k.dx1,
            k.x0,
            k.hid,
            k.wf,
            prm[TAPS : TAPS + 1, :],
            k.ig,
            k.gf,
            k.small,
            TAPS,
            k,
        )
        start_store(k.ids, k.gf, k.keep, k.send, ATTN // 2, FEED // 2, k.sems.at[3])
        if stem is not None:

            def rows(rs, start):
                d = (k.ig[rs, :] * row_mask(k.ids[4], start, RB, 512)).astype(BF)
                k.d[rs, :] = d
                pre = k.pre[rs, :]
                sg = sigmoid(pre)
                k.n[rs, 0:256] = (pre * sg).astype(BF)
                k.n[rs, 256:512] = (dotr(d, k.wout[...]) * (sg * (1.0 + pre * (1.0 - sg)))).astype(BF)

            row_loop(rows)
            k.gs[:, 0:8, :] = dotl(k.n[:, 256:512], k.frames[:, 0:512]).reshape(32, 8, 512)
            k.gs[:, 8:16, 0:128] = dotl(k.n[:, 256:512], k.frames[:, 512:640]).reshape(32, 8, 128)
            k.gs[:, 8:16, 128:512] = jnp.zeros((32, 8, 384), F32)
            k.gs[:, 16:24, :] = dotl(k.n[:, 0:256], k.d[...]).reshape(32, 8, 512)
            first = k.small[...] + k.small_first[...]
            for number, total in enumerate((first, k.small_second[...])):
                for z in range(4):
                    lanes = slice(128 * z, 128 * z + 128)
                    block = jnp.concatenate([total[0:8, lanes], total[8:16, lanes], jnp.zeros((8, 256), F32)], axis=1)
                    for q in range(4):
                        k.gs[number * 16 + z * 4 + q, 24:32, :] = block
            k.gsb[...] = k.gs[...].astype(BF)
            start_store(k.ids, k.gsb, k.keep, k.send, ATTN // 2 + FEED // 2, FLAT, k.sems.at[4], flat=True)
            wait_store(k.gsb, k.sems.at[4])
        wait_store(k.ga, k.sems.at[2])
        wait_store(k.gf, k.sems.at[3])

    rows = ATTN // 2 + FEED // 2 + (0 if stem is None else FLAT)
    ins = dict(
        ids=(ids, SMEM),
        abufs=(attn_bufs, ANY),
        fbufs=(feed_bufs, ANY),
        prm=(prm, VMEM),
        dx2=(dx2, VMEM),
        x1=(x1, VMEM),
        qkv=(qkv, VMEM),
        ls=(ls, VMEM),
        mixed=(mixed, VMEM),
        x0=(x0, VMEM),
        hid=(hid, VMEM),
    )
    scratch = dict(
        wf=((16, FEED, 512), BF),
        wa=((16, ATTN, 512), BF),
        gf=((16, FEED, 512), BF),
        ga=((16, ATTN, 512), BF),
        dx1=(ROWS, F32),
        n=(ROWS, BF),
        d=(ROWS, BF),
        dm=(ROWS, BF),
        act=((512, FF), BF),
        dh=((512, FF), BF),
        dq=((128, 512), F32),
        kt=((256, 512), BF),
    )
    if stem is not None:
        ins |= {key: (value, VMEM) for key, value in stem.items()}
        scratch |= dict(gs=((32, FLAT, 512), F32), gsb=((32, FLAT, 512), BF))
    return run(
        back_early_stem,
        31,
        ins,
        dict(
            ig=(ROWS, F32, VMEM),
            small=((SMALL, 512), F32, VMEM),
            keep=((16, rows, 512), BF, ANY),
            send=((16, rows, 512), BF, ANY),
        ),
        scratch,
    )


def kernel_outputs(ids, head_bufs, own, other, allowed, lengths):
    def outputs(k):
        start_load(k.ids, k.hbufs, FEED // 2, FLAT, k.wh, k.sems.at[0], flat=True)
        wait_load(k.wh, k.sems.at[0])

        @pl.loop(0, 2)
        def _(batch):
            length = k.lengths[batch]
            permit = k.allowed[pl.ds(batch, 1), :] > 0

            def rows(rs, start):
                mine = (batch == k.ids[0]).astype(F32)
                sent = (k.own[rs, :].astype(F32) * mine + k.other[rs, :].astype(F32) * (1.0 - mine)).astype(BF)
                logits, logsum = head_rows(sent, k.wh[...].reshape(1024, 512), permit)
                ok = row_mask(length, start, RB, 1024)
                k.logp[batch, rs, :] = jnp.where(permit, logits - logsum, 0.0) * ok
                k.acts[batch, rs, :] = sent.astype(F32)

            row_loop(rows)

    return run(
        outputs,
        9,
        dict(
            ids=(ids, SMEM),
            lengths=(lengths, SMEM),
            hbufs=(head_bufs, ANY),
            own=(own, VMEM),
            other=(other, VMEM),
            allowed=(allowed, VMEM),
        ),
        dict(logp=((2, 512, 1024), F32, VMEM), acts=((2, 512, 512), F32, VMEM)),
        dict(wh=((32, FLAT, 512), BF)),
    )


def pack_feed(w_in, w_out):
    return jnp.concatenate([w_in.reshape(32, 4, 512).transpose(1, 0, 2).reshape(128, 512), w_out])


def pack_attn(w_in, w_out):
    return jnp.concatenate([w_in.reshape(32, 3, 512).transpose(1, 0, 2).reshape(96, 512), w_out])


def pack_conv(w_in, w_out):
    return jnp.concatenate([w_in.reshape(32, 2, 512).transpose(1, 0, 2).reshape(64, 512), w_out])


def unpack_in(rows, blocks):
    return rows[: 32 * blocks].reshape(blocks, 32, 512).transpose(1, 0, 2).reshape(32, 512 * blocks)


def pack_stem(stem_in, stem_out, depth, gains, quarter):
    turned = stem_in.T
    small = jnp.concatenate([depth, gains, jnp.zeros((1, 32), depth.dtype)])
    spread = lax.dynamic_update_slice(jnp.zeros((16, 128), depth.dtype), small, (0, 32 * quarter))
    return jnp.concatenate(
        [
            turned[:, :512],
            jnp.pad(turned[:, 512:], ((0, 0), (0, 384))),
            stem_out,
            jnp.concatenate([spread[:8], spread[8:], jnp.zeros((8, 256), depth.dtype)], axis=1),
        ]
    )


def unpack_stem(rows, quarter):
    turned = jnp.concatenate([rows[0:8], rows[8:16, :128]], axis=1)
    spread = jnp.concatenate([rows[24:32, 0:128], rows[24:32, 128:256]])
    small = lax.dynamic_slice(spread, (0, 32 * quarter), (16, 32))
    return turned.T, rows[16:24], small[:TAPS], small[TAPS : TAPS + 6]


def permutation(target):
    pairs = []
    for x in range(2):
        for d in range(16):
            tx, tz, ty, tc = target(x, d // 4, (d // 2) % 2, d % 2)
            pairs.append((x * 16 + d, tx * 16 + tz * 4 + ty * 2 + tc))
    return pairs


def across(value, target):
    return lax.ppermute(value, BOTH, permutation(target))


def over_x(value):
    return across(value, lambda x, z, y, c: (1 - x, z, y, c))


def over_core(value):
    return across(value, lambda x, z, y, c: (x, z, y, 1 - c))


def over_z(value, k):
    return across(value, lambda x, z, y, c: (x, z ^ k, y, c))


def over_a(value):
    return across(value, lambda x, z, y, c: (1 - x, z, y, c) if c == 0 else (x, z, 1 - y, c))


def over_b(value):
    return across(value, lambda x, z, y, c: (1 - x, z, y, c) if c == 1 else (x, z, 1 - y, c))


def fence(*values):
    return lax.optimization_barrier(values)


def z_parts(own):
    return [own] + [over_z(own, k) for k in (1, 2, 3)]


def ab_parts(quad):
    return over_a(quad), over_b(quad)


def core_parts(quad, ra, rb, rab):
    return [quad, rb, ra, rab] + [over_core(v) for v in (quad, rb, ra, rab)]


def add(*values):
    total = values[0].astype(F32)
    for value in values[1:]:
        total = total + value.astype(F32)
    return total


def halves(kept, came):
    cut = kept.shape[0] // 2
    return add(kept[:cut], came[:cut]).astype(BF), add(kept[cut:], came[cut:]).astype(BF)


def quarters(kept, came):
    return [add(kept[k], came[k]).astype(BF) for k in range(4)]


def z_sum(parts):
    return add(parts[0], *[over_z(parts[k], k) for k in (1, 2, 3)])


def pick(first, own, other):
    return jnp.where(first, own, other), jnp.where(first, other, own)


def on_device(fast, *args):
    (spectra, lengths, languages, token_masks, cotangent) = args[:5]
    masters = args[5:]
    sec = lax.axis_index("section")
    dp = lax.axis_index("dp")
    first = sec == 0
    low = [m.astype(BF) for m in masters]
    if fast:
        ids = jnp.stack([sec, dp // 4, (dp // 2) % 2, dp % 2, lengths[sec, 0]]).astype(jnp.int32)
        own = own_pieces(low, sec, dp, first)
    else:
        ids = jnp.stack([sec * 0, sec * 0, sec * 0, sec * 0, lengths[sec, 0]]).astype(jnp.int32)
        chunks = gather_plain(low)
    frames = lax.dynamic_index_in_dim(spectra, sec, 0, keepdims=False).reshape(512, -1)
    allowed_both = jnp.concatenate(
        [lax.dynamic_slice_in_dim(token_masks, languages[m, 0], 1, 0) for m in range(2)]
    ).astype(F32)
    allowed = lax.dynamic_slice_in_dim(allowed_both, sec, 1, 0)
    swap = lambda v: lax.ppermute(v, "section", [(0, 1), (1, 0)])
    cots = cotangent[0, :, 0]
    cot_own = lax.dynamic_index_in_dim(cots, sec, 0, keepdims=False)
    cot_other = swap(lax.dynamic_index_in_dim(cots, 1 - sec, 0, keepdims=False))
    cot_first, cot_second = pick(first, cot_own, cot_other)

    if fast:
        chunks = [None] * 4
        quad0 = jnp.stack(z_parts(own[0]))
        a0, b0 = ab_parts(quad0)
        quad1 = jnp.stack(z_parts(own[1]))
        chunks[0] = core_parts(quad0, a0, b0, over_b(a0))
        quad1, own[2], *chunks[0] = fence(quad1, own[2], *chunks[0])
        a1, b1 = ab_parts(quad1)
        quad2 = jnp.stack(z_parts(own[2]))
    ka = kernel_stem_feed(ids, chunks[0], frames)
    prm = ka.prm
    if fast:
        ka.x1, quad1, a1, b1, quad2, own[3] = fence(ka.x1, quad1, a1, b1, quad2, own[3])
        chunks[1] = core_parts(quad1, a1, b1, over_b(a1))
        ka.x1, *chunks[1] = fence(ka.x1, *chunks[1])
        a2, b2 = ab_parts(quad2)
        quad3 = jnp.stack(z_parts(own[3]))
    kb = kernel_rest_first(ids, chunks[1], prm, ka.x1)
    if fast:
        kb.sent, quad2, a2, b2, quad3 = fence(kb.sent, quad2, a2, b2, quad3)
        chunks[2] = core_parts(quad2, a2, b2, over_b(a2))
        kb.sent, *chunks[2] = fence(kb.sent, *chunks[2])
        a3, b3 = ab_parts(quad3)
    kc = kernel_first_second(ids, chunks[2], prm, kb.sent)
    if fast:
        kc.x3, quad3, a3, b3 = fence(kc.x3, quad3, a3, b3)
        chunks[3] = core_parts(quad3, a3, b3, over_b(a3))
    kd = kernel_turn(ids, chunks[3], chunks[2], prm, kc.x3, cot_second, allowed, kc.x2, kc.gated, kc.deep)
    to_send = jnp.where(first, kd.sent, kb.sent)
    own_sent = jnp.where(first, kb.sent, kd.sent)
    other_sent = swap(to_send)
    if fast:
        came0 = over_core(kd.send)
    ke = kernel_back_early(
        1, ids, chunks[2], FEED // 2, chunks[2], 0, prm, kd.dx2, kc.x1, kc.qkv, kc.ls, kc.mixed,
        kb.sent, kc.hid, None,
    )
    ig_second = ke.ig.astype(BF)
    if fast:
        other_sent, came0, ke.send, ig_second = fence(other_sent, came0, ke.send, ig_second)
        near0, far0 = halves(kd.keep, came0)
        came0 = over_a(far0)
        came1 = over_core(ke.send)
    kf = kernel_back_late(
        ids, chunks[1], chunks[1], chunks[3], prm, kb.x4, kb.sent, cot_first, allowed, ig_second,
        kb.x3, kb.hid, kb.x2, kb.gated, kb.deep, kd.ghead,
    )
    if fast:
        came0, came1, kf.send, kf.dx2 = fence(came0, came1, kf.send, kf.dx2)
        near0, far0 = halves(near0, came0)
        near1, far1 = halves(ke.keep, came1)
        came0 = over_b(far0)
        came1 = over_a(far1)
        came2 = over_core(kf.send)
    stem = dict(
        pre=ka.pre,
        wout=ka.wout,
        frames=frames,
        small_first=kf.small,
        small_second=kd.small + ke.small,
    )
    kg = kernel_back_early(
        0, ids, chunks[1], 0, chunks[0], FLAT, prm, kf.dx2, ka.x1, kb.qkv, kb.ls, kb.mixed, ka.x0,
        ka.hid, stem,
    )
    if fast:
        came0, came1, came2, kg.send = fence(came0, came1, came2, kg.send)
        near2, far2 = halves(kf.keep, came2)
        near1, far1 = halves(near1, came1)
        came3 = over_core(kg.send)
        came2 = over_a(far2)
        came1 = over_b(far1)
        sum0 = z_sum(quarters(near0, came0))
        near3, far3 = halves(kg.keep, came3)
        near2, far2 = halves(near2, came2)
        came3 = over_a(far3)
        came2 = over_b(far2)
        sum1 = z_sum(quarters(near1, came1))
        sum2 = z_sum(quarters(near2, came2))
        near3, far3 = halves(near3, came3)
        came3 = over_b(far3)
        sum3 = z_sum(quarters(near3, came3))
    other_grad = swap(jnp.where(first, ke.ig, kg.ig).astype(BF)).astype(F32)
    own_grad = jnp.where(first, kg.ig, ke.ig)
    input_grads = jnp.stack(pick(first, own_grad, other_grad))[None, :, None]
    ko = kernel_outputs_of(fast, ids, sec, chunks[3], own_sent, other_sent, allowed_both, lengths)
    activations = ko.acts[None, :, None]
    log_probs = ko.logp[None, :, None]
    if fast:
        shards = own_shards(sum0, sum1, sum2, sum3, dp, first)
    else:
        shards = reduce_plain([(k.keep, k.send) for k in (kd, ke, kf, kg)])
    return (activations, log_probs, input_grads, *shards)


def kernel_outputs_of(fast, ids, sec, head_bufs, own, other, allowed, lengths):
    if not fast:
        mine, theirs = own, other
        flip = sec == 1
        own, other = jnp.where(flip, theirs, mine), jnp.where(flip, mine, theirs)
    return kernel_outputs(ids, head_bufs, own, other, allowed, lengths[:, 0])


def own_pieces(low, sec, dp, first):
    feed_in, feed_out, attend_in, attend_out, conv_in, depth, conv_out, gains, stem_in, stem_out, head = low
    feeds = [pack_feed(feed_in[0, j], feed_out[0, j]).reshape(2, FEED // 2, 512) for j in range(2)]
    attn = pack_attn(attend_in[0], attend_out[0]).reshape(2, ATTN // 2, 512)
    conv = pack_conv(conv_in[0], conv_out[0]).reshape(2, CONV // 2, 512)
    stem = pack_stem(stem_in, stem_out, depth[0], gains[0], dp % 4)

    def spread(both):
        mine = lax.dynamic_index_in_dim(both, sec, 0, keepdims=False)
        theirs = over_x(lax.dynamic_index_in_dim(both, 1 - sec, 0, keepdims=False))
        return pick(first, mine, theirs)

    feed_first, feed_second = spread(feeds[0])
    rest_first, rest_second = spread(jnp.concatenate([attn, conv, feeds[1]], axis=1))
    edge = ATTN // 2 + CONV // 2
    return [
        jnp.concatenate([stem, feed_first]),
        rest_first,
        jnp.concatenate([feed_second, rest_second[:edge]]),
        jnp.concatenate([rest_second[edge:], head.T]),
    ]


def own_shards(second_late, second_early, first_late, first_early, dp, first):
    edge, early = FEED // 2 + CONV // 2, ATTN // 2 + FEED // 2

    def join(of_first, of_second):
        own = jnp.where(first, of_first, of_second)
        other = over_x(jnp.where(first, of_second, of_first).astype(BF)).astype(F32)
        return jnp.stack(pick(first, own, other))

    late = join(first_late[:edge], second_late)
    earlier = join(first_early[:early], second_early)
    half = lambda part, begin, rows: part[:, begin : begin + rows].reshape(2 * rows, 512)
    feeds = [half(earlier, ATTN // 2, FEED // 2), half(late, 0, FEED // 2)]
    attn = half(earlier, 0, ATTN // 2)
    conv = half(late, FEED // 2, CONV // 2)
    head = first_late[edge:]
    g_stem_in, g_stem_out, g_depth, g_gains = unpack_stem(first_early[early:], dp % 4)
    return (
        jnp.stack([unpack_in(f, 4) for f in feeds])[None],
        jnp.stack([f[128:] for f in feeds])[None],
        unpack_in(attn, 3)[None],
        attn[96:][None],
        unpack_in(conv, 2)[None],
        g_depth[None],
        conv[64:][None],
        g_gains[None],
        g_stem_in,
        g_stem_out,
        head.T,
    )


def spread_order():
    order = []
    for cr, a, b, zk in pieces():
        px, py = (b, a) if cr else (a, b)
        order.append(px * 16 + zk * 4 + py * 2 + cr)
    return order


def gather_plain(low):
    axes = (2, 2, 1, 1, 1, 2, 1, 2)
    whole = []
    for weight, axis in zip(low[:8], axes):
        axis = 2 if weight.ndim == 4 else axis
        part = lax.all_gather(weight[0], "dp", axis=axis - 1, tiled=True)
        whole.append(lax.all_gather(part, "section", axis=0))
    feed_in, feed_out, attend_in, attend_out, conv_in, depth, conv_out, gains = whole
    stem_in = lax.all_gather(low[8], BOTH, axis=1, tiled=True)
    stem_out = lax.all_gather(low[9], BOTH, axis=0, tiled=True)
    head = lax.all_gather(low[10], BOTH, axis=1, tiled=True)
    order = spread_order()

    def layer(l):
        rows = lambda w, n: w.reshape(16, n, w.shape[-1])
        feeds = [jax.vmap(pack_feed)(rows(feed_in[l, j], 32), rows(feed_out[l, j], 128)) for j in range(2)]
        attn = jax.vmap(pack_attn)(rows(attend_in[l], 32), rows(attend_out[l], 32))
        conv = jax.vmap(pack_conv)(rows(conv_in[l], 32), rows(conv_out[l], 32))
        cut = lambda w: w.reshape(16, 2, w.shape[1] // 2, 512).transpose(1, 0, 2, 3).reshape(32, w.shape[1] // 2, 512)
        return [cut(w) for w in (feeds[0], attn, conv, feeds[1])]

    one, two = layer(0), layer(1)
    columns = lambda w, n: w.reshape(*w.shape[:-1], n, w.shape[-1] // n)
    small = lambda w: jnp.moveaxis(columns(w, 16), 2, 1).reshape(32, w.shape[1], 32)
    stem = jax.vmap(pack_stem)(
        jnp.moveaxis(columns(stem_in, 32), 1, 0),
        stem_out.reshape(32, 8, 512),
        small(depth),
        small(gains),
        jnp.arange(32) % 4,
    )
    head = head.T.reshape(32, 32, 512)
    chunks = ([stem, one[0]], one[1:], [two[0], two[1], two[2]], [two[3], head])
    placed = []
    for parts in chunks:
        joined = jnp.concatenate(parts, axis=1)
        placed.append([jnp.stack([joined[p] for p in order[4 * i : 4 * i + 4]]) for i in range(8)])
    return placed


def reduce_plain(grads):
    order = spread_order()
    place = [order.index(p) for p in range(32)]
    chunks = []
    for keep, send in grads:
        both = jnp.concatenate([keep, send])
        chunks.append(jnp.stack([both[q] for q in place]).astype(F32))
    edge, early = FEED // 2 + CONV // 2, ATTN // 2 + FEED // 2
    whole = []
    for late, earlier in ((chunks[2], chunks[3]), (chunks[0], chunks[1])):
        glue = lambda part, begin, rows: (
            part[:, begin : begin + rows].reshape(2, 16, rows, 512).transpose(1, 0, 2, 3).reshape(16, 2 * rows, 512)
        )
        feeds = [glue(earlier, ATTN // 2, FEED // 2), glue(late, 0, FEED // 2)]
        attn, conv = glue(earlier, 0, ATTN // 2), glue(late, FEED // 2, CONV // 2)
        spread = lambda w, n: jax.vmap(lambda rows: unpack_in(rows, n))(w).reshape(512, 512 * n)
        whole.append(
            (
                jnp.stack([spread(f, 4) for f in feeds]),
                jnp.stack([f[:, 128:].reshape(FF, 512) for f in feeds]),
                spread(attn, 3),
                attn[:, 96:].reshape(512, 512),
                spread(conv, 2),
                conv[:, 64:].reshape(512, 512),
            )
        )
    head = chunks[2][:, edge:].reshape(1024, 512).T
    g_stem_in, g_stem_out, g_depth, g_gains = jax.vmap(unpack_stem)(chunks[3][:, early:], jnp.arange(32) % 4)
    g_stem_in = jnp.moveaxis(g_stem_in, 0, 1).reshape(640, 256)
    g_stem_out = g_stem_out.reshape(256, 512)
    lanes = lambda w: jnp.moveaxis(w.reshape(2, 16, w.shape[1], 32), 1, 2).reshape(2, w.shape[1], 512)
    g_depth, g_gains = lanes(g_depth), lanes(g_gains)
    stacked = [jnp.stack([whole[0][i], whole[1][i]]) for i in range(6)]

    def shard(value, axis):
        value = lax.psum_scatter(value, "section", scatter_dimension=0, tiled=True)
        return lax.psum_scatter(value, "dp", scatter_dimension=axis, tiled=True)

    return (
        shard(stacked[0], 2),
        shard(stacked[1], 2),
        shard(stacked[2], 1),
        shard(stacked[3], 1),
        shard(stacked[4], 1),
        shard(g_depth, 2),
        shard(stacked[5], 1),
        shard(g_gains, 2),
        lax.psum_scatter(g_stem_in, BOTH, scatter_dimension=1, tiled=True),
        lax.psum_scatter(g_stem_out, BOTH, scatter_dimension=0, tiled=True),
        lax.psum_scatter(head, BOTH, scatter_dimension=1, tiled=True),
    )


def solution(mesh):
    fast = dict(mesh.shape) == {"section": 2, "dp": 16}

    def body(*args):
        return on_device(fast, *args)

    layer_specs = (
        P("section", None, "dp", None),
        P("section", None, "dp", None),
        P("section", "dp", None),
        P("section", "dp", None),
        P("section", "dp", None),
        P("section", None, "dp"),
        P("section", "dp", None),
        P("section", None, "dp"),
        P(None, BOTH),
        P(BOTH, None),
        P(None, BOTH),
    )
    rows = P("section", None, "dp", None, None)
    return jax.shard_map(
        body,
        mesh=mesh,
        in_specs=(P(None, "dp", None, None), P(None, "dp"), P(None, "dp"), P(), rows) + layer_specs,
        out_specs=(rows, rows, rows) + layer_specs,
        check_vma=False,
    )
```

time: 1720 us -> 493 us (0.29)
  waiting for transfers between devices: 896 us -> 195 us
  matrix products: 355 us -> 0 us
  blocking collectives: 164 us -> 0 us
  Pallas kernels: 0 us -> 141 us
  local copies, waits for them, and re-layouts: 120 us -> 21.6 us
  other arithmetic: 141 us -> 44.3 us
  starting transfers between devices: 13.8 us -> 81.8 us
    reduce_scatter x8 -> x0, waiting for transfers between devices: 741 us -> none  [the longest x1 139 us: on_device(): lax.psum_scatter(head_sum, ('section', 'dp'), scatter_dimension=1, tiled=...]
    dot_general x138 -> x0, matrix products: 355 us -> none  [the longest x53 101 us: matmul(): return jnp.dot(left, right, preferred_element_type=jnp.float32)]
    ppermute x4 -> x71, waiting for transfers between devices: 16.8 us -> 195 us  [the longest x68 180 us: across(): return lax.ppermute(value, BOTH, permutation(target))]
    all_gather x6 -> x0, blocking collectives: 164 us -> none  [the longest x1 42.7 us: on_device(): lax.all_gather(stem_out.astype(jnp.bfloat16), ('section', 'dp'), axis=0,...]
    pallas_call x0 -> x8, Pallas kernels: none -> 141 us  [run(): pl.pallas_call(kernel, out_shape=[jax.ShapeDtypeStruct(shape, dtype) for...]
    unnamed x19 -> x0, waiting for transfers between devices: 139 us -> none
    ppermute x4 -> x71, starting transfers between devices: 12.5 us -> 81.8 us  [the longest x68 77.2 us: across(): return lax.ppermute(value, BOTH, permutation(target))]
    reduce_sum x59 -> x0, other arithmetic: 58.3 us -> none  [the longest x7 20.4 us: norm_forward(): centered = x_rows - jnp.mean(x_rows, axis=-1, keepdims=True)]
  transfers between devices with their start and end apart: 20 -> 71, of which waited for: 12 -> 31; matrix products, arithmetic and copies ran while one was open for 20% -> 9% of each run, Pallas kernels for 0% -> 24%
where the time goes in v1:
time: 493 us; the launch traced here: 490 us
  waiting for transfers between devices  195 us (40%)
  Pallas kernels  141 us (29%)
  starting transfers between devices  81.8 us (17%)
  other arithmetic  44.3 us (9%)
  local copies, waits for them, and re-layouts  21.6 us (4%)
  between operations  5.87 us (1%)
    ppermute x68, waiting for transfers between devices, across(): return lax.ppermute(value, BOTH, permutation(target))  180 us
    pallas_call x8, Pallas kernels, run(): pl.pallas_call(kernel, out_shape=[jax.ShapeDtypeStruct(shape, dtype) for...  141 us
    ppermute x68, starting transfers between devices, across(): return lax.ppermute(value, BOTH, permutation(target))  77.2 us
    convert_element_type x8, other arithmetic, halves(): add(kept[:cut], came[:cut]).astype(BF)  23 us
    ppermute x3, waiting for transfers between devices, on_device(): swap = lambda v: lax.ppermute(v, 'section', [(0, 1), (1, 0)])  15.1 us
  transfers between devices with their start and end apart: 71, of which 31 were waited for; matrix products, arithmetic and copies ran while one was open for 9% of the time, Pallas kernels for 24%

profile of v1, /device:TPU:0, one launch (start us, length us, event | category | flops | bytes accessed | tf_op | source)
XLA Modules:
  0.0 489.5 jit_solution(10459878926773155208)
XLA Ops:
  18.0 7.8 %collective-permute-done.6 = bf16[160,512]{1,0:T(8,128)(2,1)S(1)} collective-permute-done((bf16[160,512]{1,0:T(8,128)(2,1)S(1)}, bf16[160,512]{1,0:T(8,128)(2,1)S(1)}, u32[]{:S(2)}, u32[]{:S(2)}) %collective-permute-start.6) | collective-permute-done | bytes 163872 | tf_op jit(solution)/shard_map/ppermute | solution.py:889
  31.5 13.9 %collective-permute-done.9.refs_3_.refs_11_ = bf16[4,160,512]{2,1,0:T(8,128)(2,1)} collective-permute-done((bf16[4,160,512]{2,1,0:T(8,128)(2,1)S(1)}, bf16[4,160,512]{2,1,0:T(8,128)(2,1)}, u32[]{:S(2)}, u32[]{:S(2)}) %collective-permute-start.9) | collective-permute-done | bytes 655392 | tf_op jit(solution)/shard_map/ppermute | solution.py:889
  53.3 5.5 %collective-permute-done.3 = bf16[240,512]{1,0:T(8,128)(2,1)S(1)} collective-permute-done((bf16[240,512]{1,0:T(8,128)(2,1)S(1)}, bf16[240,512]{1,0:T(8,128)(2,1)S(1)}, u32[]{:S(2)}, u32[]{:S(2)}) %collective-permute-start.3) | collective-permute-done | bytes 245792 | tf_op jit(solution)/shard_map/ppermute | solution.py:889
  59.4 4.7 collective-permute-done.2
  79.7 7.9 %stem_feed.1 = (f32[2,16,512]{2,1,0:T(8,128)}, f32[512,256]{1,0:T(8,128)}, bf16[256,512]{1,0:T(8,128)(2,1)}, bf16[256,128]{1,0:T(8,128)(2,1)}, bf16[256,512]{1,0...) custom-call(s32[5]{0:T(128)} %stack.114.refs_0_, ...), custom_call_target="tpu_custom_call" | custom-call | flops 9900000256 | bytes 1048576 | tf_op jit(solution)/shard_map/stem_feed/pallas_call | solution.py:413
  91.5 4.7 collective-permute-done.16.refs_2_.refs_10_
  98.5 12.0 %collective-permute-done.20.refs_4_.refs_12_ = bf16[4,240,512]{2,1,0:T(8,128)(2,1)S(1)} collective-permute-done((bf16[4,240,512]{2,1,0:T(8,128)(2,1)S(1)}, bf16[4,240,512]{2,1,0:T(8,128)(2,1)S(1)}, u32[]{:S(2)}, u32[]{:S(2)}) %collective-permute-start.20) | collective-permute-done | bytes 983072 | tf_op jit(solution)/shard_map/ppermute | solution.py:889
  113.0 6.0 %collective-permute-done.29 = bf16[160,512]{1,0:T(8,128)(2,1)S(1)} collective-permute-done((bf16[160,512]{1,0:T(8,128)(2,1)S(1)}, bf16[160,512]{1,0:T(8,128)(2,1)S(1)}, u32[]{:S(2)}, u32[]{:S(2)}) %collective-permute-start.29) | collective-permute-done | bytes 163872 | tf_op jit(solution)/shard_map/ppermute | solution.py:889
  121.8 7.6 %collective-permute-done.28 = bf16[160,512]{1,0:T(8,128)(2,1)S(1)} collective-permute-done((bf16[160,512]{1,0:T(8,128)(2,1)S(1)}, bf16[160,512]{1,0:T(8,128)(2,1)S(1)}, u32[]{:S(2)}, u32[]{:S(2)}) %collective-permute-start.28) | collective-permute-done | bytes 163872 | tf_op jit(solution)/shard_map/ppermute | solution.py:889
  129.4 5.3 %collective-permute-done.27 = bf16[160,512]{1,0:T(8,128)(2,1)S(1)} collective-permute-done((bf16[160,512]{1,0:T(8,128)(2,1)S(1)}, bf16[160,512]{1,0:T(8,128)(2,1)S(1)}, u32[]{:S(2)}, u32[]{:S(2)}) %collective-permute-start.27) | collective-permute-done | bytes 163872 | tf_op jit(solution)/shard_map/ppermute | solution.py:889
  141.7 16.8 %rest_first.1 = (bf16[512,1536]{1,0:T(8,128)(2,1)}, f32[8,512]{1,0:T(8,128)}, bf16[512,512]{1,0:T(8,128)(2,1)}, f32[512,512]{1,0:T(8,128)}, f32[512,1024]{1,0:T(...) custom-call(s32[5]{0:T(128)} %stack.114.refs_0_, ...), custom_call_target="tpu_custom_call" | custom-call | flops 26400000000 | bytes 1048576 | tf_op jit(solution)/shard_map/rest_first/pallas_call | solution.py:413
  161.3 12.1 %collective-permute-done.30.refs_4_.refs_12_ = bf16[4,240,512]{2,1,0:T(8,128)(2,1)S(1)} collective-permute-done((bf16[4,240,512]{2,1,0:T(8,128)(2,1)S(1)}, bf16[4,240,512]{2,1,0:T(8,128)(2,1)S(1)}, u32[]{:S(2)}, u32[]{:S(2)}) %collective-permute-start.30) | collective-permute-done | bytes 983072 | tf_op jit(solution)/shard_map/ppermute | solution.py:889
  177.2 15.9 %first_second.1 = (bf16[512,2048]{1,0:T(8,128)(2,1)}, f32[512,512]{1,0:T(8,128)}, bf16[512,1536]{1,0:T(8,128)(2,1)}, f32[8,512]{1,0:T(8,128)}, bf16[512,512]{1,0...) custom-call(s32[5]{0:T(128)} %stack.114.refs_0_, ...), custom_call_target="tpu_custom_call" | custom-call | flops 26400000000 | bytes 1048576 | tf_op jit(solution)/shard_map/first_second/pallas_call | solution.py:413
  197.0 7.1 %collective-permute-done.37.refs_4_.refs_5_.refs_20_ = bf16[4,160,512]{2,1,0:T(8,128)(2,1)} collective-permute-done((bf16[4,160,512]{2,1,0:T(8,128)(2,1)}, bf16[4,160,512]{2,1,0:T(8,128)(2,1)}, u32[]{:S(2)}, u32[]{:S(2)}) %collective-permute-start.37) | collective-permute-done | bytes 655392 | tf_op jit(solution)/shard_map/ppermute | solution.py:889
  213.5 7.6 %collective-permute-done.42 = bf16[512,1024]{1,0:T(8,128)(2,1)S(1)} collective-permute-done((bf16[512,1024]{1,0:T(8,128)(2,1)}, bf16[512,1024]{1,0:T(8,128)(2,1)S(1)}, u32[]{:S(2)}, u32[]{:S(2)}) %collective-permute-start.42) | collective-permute-done | bytes 1048608 | tf_op jit(solution)/shard_map/ppermute | solution.py:970
  222.6 25.7 %turn.1 = (bf16[512,512]{1,0:T(8,128)(2,1)}, f32[1024,512]{1,0:T(8,128)}, f32[512,512]{1,0:T(8,128)}, f32[16,512]{1,0:T(8,128)}, bf16[16,176,512]{2,1,0:T(8,128)(2,1)}, /*index=5*/bf16[16,176,512]{2,1,0:T(8,128)(2,1)}) custom-call(s32[5]{0:T(128)} %stack.114.refs_0_, bf16[4,160,512]{2,1,0:T(8,128)(2,1)} %pad_maximum_fusion.3.refs_1_.refs_2_.refs_17_, ...), custom_call_target="tpu_custom_call" | custom-call | flops 35200000000 | bytes 1048576 | tf_op jit(solution)/shard_map/turn/pallas_call | solution.py:413
  255.9 22.2 %back_early_stem.2 = (f32[512,512]{1,0:T(8,128)}, f32[16,512]{1,0:T(8,128)}, bf16[16,192,512]{2,1,0:T(8,128)(2,1)}, bf16[16,192,512]{2,1,0:T(8,128)(2,1)}) custom-call(s32[5]{0:T(128)} %stack.114.refs_0_, bf16[4,240,512]{2,1,0:T(8,128)(2,1)} %copy-done.11, bf16[4,240,512]{2,1,0:T(8,128)(2,1)} %collective-permute-done.26.refs_2_.refs_10_, ...), custom_call_target="tpu_custom_call" | custom-call | flops 34100000768 | bytes 1048576 | tf_op jit(solution)/shard_map/back_early_stem/pallas_call | solution.py:413
  281.6 4.8 add_convert_fusion.6
  286.8 22.6 %back_late.1 = (f32[512,512]{1,0:T(8,128)}, f32[16,512]{1,0:T(8,128)}, bf16[16,208,512]{2,1,0:T(8,128)(2,1)}, bf16[16,208,512]{2,1,0:T(8,128)(2,1)}) custom-call(s32[5]{0:T(128)} %stack.114.refs_0_, bf16[4,240,512]{2,1,0:T(8,128)(2,1)} %copy-done.10, bf16[4,240,512]{2,1,0:T(8,128)(2,1)} %copy-done.34, bf16[4,240,512]{2,1,0:T(8,128)(2,1)} %copy-done.35, ...), custom_call_target="tpu_custom_call" | custom-call | flops 30799998976 | bytes 1048576 | tf_op jit(solution)/shard_map/back_late/pallas_call | solution.py:413
  317.4 22.7 %back_early_stem.3 = (f32[512,512]{1,0:T(8,128)}, f32[16,512]{1,0:T(8,128)}, bf16[16,224,512]{2,1,0:T(8,128)(2,1)}, bf16[16,224,512]{2,1,0:T(8,128)(2,1)}) custom-call(s32[5]{0:T(128)} %stack.114.refs_0_, bf16[4,240,512]{2,1,0:T(8,128)(2,1)} %copy-done.10, bf16[4,240,512]{2,1,0:T(8,128)(2,1)} %copy-done.34, bf16[4,240,512]{2,1,0:T(8,128)(2,1)} %copy-done.35, ...), custom_call_target="tpu_custom_call" | custom-call | flops 34100000768 | bytes 1048576 | tf_op jit(solution)/shard_map/back_early_stem/pallas_call | solution.py:413
  341.3 5.2 %add_convert_fusion.3 = (bf16[8,208,512]{2,1,0:T(8,128)(2,1)S(1)}, bf16[8,208,512]{2,1,0:T(8,128)(2,1)}) fusion(bf16[16,208,512]{2,1,0:T(8,128)(2,1)} %collective-permute-done.50, bf16[16,208,512]{2,1,0:T(8,128)(2,1)} %get-tuple-element.209), kind=kLoop, calls=%fused_computation.3 | loop fusion | flops 6815744 | bytes 10223616 | tf_op jit(solution)/shard_map/convert_element_type | solution.py:937
  347.6 7.4 %outputs.1 = (f32[2,512,1024]{2,1,0:T(8,128)}, f32[2,512,512]{2,1,0:T(8,128)}) custom-call(s32[5]{0:T(128)} %stack.114.refs_0_, s32[2]{0:T(128)} %bitcast.216, bf16[4,160,512]{2,1,0:T(8,128)(2,1)} %pad_maximum_fusion.3.refs_1_.refs_2_.refs_17_, bf16[4,160,512]{2,1,0:T(8,128)(2,1)} %collective-permute-done.36.refs_2_.refs_3_.refs_18_, ...), custom_call_target="tpu_custom_call" | custom-call | flops 9900000256 | bytes 1048576 | tf_op jit(solution)/shard_map/outputs/pallas_call | solution.py:413
  356.4 4.4 add_convert_fusion.1
  363.3 16.1 %collective-permute-done.62 = bf16[8,208,512]{2,1,0:T(8,128)(2,1)} collective-permute-done((bf16[8,208,512]{2,1,0:T(8,128)(2,1)}, bf16[8,208,512]{2,1,0:T(8,128)(2,1)}, u32[]{:S(2)}, u32[]{:S(2)}) %collective-permute-start.62) | collective-permute-done | bytes 1703968 | tf_op jit(solution)/shard_map/ppermute | solution.py:889
  383.0 7.5 %collective-permute-done.47 = bf16[512,512]{1,0:T(8,128)(2,1)S(1)} collective-permute-done((bf16[512,512]{1,0:T(8,128)(2,1)S(1)}, bf16[512,512]{1,0:T(8,128)(2,1)S(1)}, u32[]{:S(2)}, u32[]{:S(2)}) %collective-permute-start.47) | collective-permute-done | bytes 524320 | tf_op jit(solution)/shard_map/ppermute | solution.py:970
  396.5 6.7 %collective-permute-done.63 = bf16[4,208,512]{2,1,0:T(8,128)(2,1)S(1)} collective-permute-done((bf16[4,208,512]{2,1,0:T(8,128)(2,1)S(1)}, bf16[4,208,512]{2,1,0:T(8,128)(2,1)S(1)}, u32[]{:S(2)}, u32[]{:S(2)}) %collective-permute-start.63) | collective-permute-done | bytes 852000 | tf_op jit(solution)/shard_map/ppermute | solution.py:889
  406.0 11.1 %collective-permute-done.52 = bf16[8,224,512]{2,1,0:T(8,128)(2,1)S(1)} collective-permute-done((bf16[8,224,512]{2,1,0:T(8,128)(2,1)S(1)}, bf16[8,224,512]{2,1,0:T(8,128)(2,1)S(1)}, u32[]{:S(2)}, u32[]{:S(2)}) %collective-permute-start.52) | collective-permute-done | bytes 1835040 | tf_op jit(solution)/shard_map/ppermute | solution.py:889
  420.7 4.8 collective-permute-start.58
  425.5 5.2 %collective-permute-done.65 = bf16[208,512]{1,0:T(8,128)(2,1)S(1)} collective-permute-done((bf16[208,512]{1,0:T(8,128)(2,1)S(1)}, bf16[208,512]{1,0:T(8,128)(2,1)S(1)}, u32[]{:S(2)}, u32[]{:S(2)}) %collective-permute-start.65) | collective-permute-done | bytes 213024 | tf_op jit(solution)/shard_map/ppermute | solution.py:889
  435.9 6.8 %collective-permute-done.70 = bf16[176,512]{1,0:T(8,128)(2,1)S(1)} collective-permute-done((bf16[176,512]{1,0:T(8,128)(2,1)S(1)}, bf16[176,512]{1,0:T(8,128)(2,1)S(1)}, u32[]{:S(2)}, u32[]{:S(2)}) %collective-permute-start.70) | collective-permute-done | bytes 180256 | tf_op jit(solution)/shard_map/ppermute | solution.py:889
  456.8 15.8 %collective-permute-done.55 = bf16[224,512]{1,0:T(8,128)(2,1)} collective-permute-done((bf16[224,512]{1,0:T(8,128)(2,1)}, bf16[224,512]{1,0:T(8,128)(2,1)}, u32[]{:S(2)}, u32[]{:S(2)}) %collective-permute-start.55) | collective-permute-done | bytes 229408 | tf_op jit(solution)/shard_map/ppermute | solution.py:889
  480.6 4.9 %collective-permute-done.61 = bf16[192,512]{1,0:T(8,128)(2,1)S(1)} collective-permute-done((bf16[192,512]{1,0:T(8,128)(2,1)S(1)}, bf16[192,512]{1,0:T(8,128)(2,1)S(1)}, u32[]{:S(2)}, u32[]{:S(2)}) %collective-permute-start.61) | collective-permute-done | bytes 196640 | tf_op jit(solution)/shard_map/ppermute | solution.py:889
  (326 shorter events, 154.8 us)
Async XLA Ops:
  29.4 21.2 %collective-permute-start = (bf16[240,512]{1,0:T(8,128)(2,1)S(1)}, bf16[240,512]{1,0:T(8,128)(2,1)S(1)}, u32[]{:S(2)}, u32[]{:S(2)}) collective-permute-start(bf16[240,512]{1,0:T(8,128)(2,1)S(1)} %dynamic-slice_bitcast_fusion.1), channel_id=1, source_target_pairs={{0,16},{1,17},{2,18},{3,19},{4,20},{5,21},{6,22},{7,23},{8,24},{9,... | collective-permute-start | bytes 737288 | tf_op jit(solution)/shard_map/ppermute | solution.py:889
  30.0 28.8 %collective-permute-start.8 = (bf16[4,160,512]{2,1,0:T(8,128)(2,1)S(1)}, bf16[4,160,512]{2,1,0:T(8,128)(2,1)}, u32[]{:S(2)}, u32[]{:S(2)}) collective-permute-start(bf16[4,160,512]{2,1,0:T(8,128)(2,1)S(1)} %pad_maximum_fusion.2.refs_1_.refs_9_), channel_id=1, source_target_pairs={{0,2},{1,17},{2,0},{3,19},{4,6},{5,21},{6,4},{7,23},{8,10},{9,25},... | collective-permute-start | bytes 1966088 | tf_op jit(solution)/shard_map/ppermute | solution.py:889
  76.7 19.5 %collective-permute-start.16 = (bf16[4,240,512]{2,1,0:T(8,128)(2,1)S(1)}, bf16[4,240,512]{2,1,0:T(8,128)(2,1)S(1)}, u32[]{:S(2)}, u32[]{:S(2)}) collective-permute-start(bf16[4,240,512]{2,1,0:T(8,128)(2,1)S(1)} %pad_maximum_fusion.refs_1_.refs_9_), channel_id=1, source_target_pairs={{0,2},{1,17},{2,0},{3,19},{4,6},{5,21},{6,4},{7,23},{8,10},{9,25},... | collective-permute-start | bytes 2949128 | tf_op jit(solution)/shard_map/ppermute | solution.py:889
  97.9 41.6 %collective-permute-start.23 = (bf16[4,240,512]{2,1,0:T(8,128)(2,1)S(1)}, bf16[4,240,512]{2,1,0:T(8,128)(2,1)S(1)}, u32[]{:S(2)}, u32[]{:S(2)}) collective-permute-start(bf16[4,240,512]{2,1,0:T(8,128)(2,1)S(1)} %collective-permute-done.15.refs_3_.refs_11_), channel_id=1, source_target_pairs={{0,1},{1,0},{2,3},{3,2},{4,5},{5,4},{6,7},{7,6},{8,9},{9,8},{10,11... | collective-permute-start | bytes 2949128 | tf_op jit(solution)/shard_map/ppermute | solution.py:889
  97.9 39.2 %collective-permute-start.21 = (bf16[4,240,512]{2,1,0:T(8,128)(2,1)S(1)}, bf16[4,240,512]{2,1,0:T(8,128)(2,1)S(1)}, u32[]{:S(2)}, u32[]{:S(2)}) collective-permute-start(bf16[4,240,512]{2,1,0:T(8,128)(2,1)S(1)} %pad_maximum_fusion.refs_1_.refs_9_), channel_id=1, source_target_pairs={{0,1},{1,0},{2,3},{3,2},{4,5},{5,4},{6,7},{7,6},{8,9},{9,8},{10,11... | collective-permute-start | bytes 2949128 | tf_op jit(solution)/shard_map/ppermute | solution.py:889
  98.5 41.1 %collective-permute-start.22 = (bf16[4,240,512]{2,1,0:T(8,128)(2,1)S(1)}, bf16[4,240,512]{2,1,0:T(8,128)(2,1)S(1)}, u32[]{:S(2)}, u32[]{:S(2)}) collective-permute-start(bf16[4,240,512]{2,1,0:T(8,128)(2,1)S(1)} %collective-permute-done.16.refs_2_.refs_10_), channel_id=1, source_target_pairs={{0,1},{1,0},{2,3},{3,2},{4,5},{5,4},{6,7},{7,6},{8,9},{9,8},{10,11... | collective-permute-start | bytes 2949128 | tf_op jit(solution)/shard_map/ppermute | solution.py:889
  110.5 29.1 %collective-permute-start.24 = (bf16[4,240,512]{2,1,0:T(8,128)(2,1)S(1)}, bf16[4,240,512]{2,1,0:T(8,128)(2,1)S(1)}, u32[]{:S(2)}, u32[]{:S(2)}) collective-permute-start(bf16[4,240,512]{2,1,0:T(8,128)(2,1)S(1)} %collective-permute-done.20.refs_4_.refs_12_), channel_id=1, source_target_pairs={{0,1},{1,0},{2,3},{3,2},{4,5},{5,4},{6,7},{7,6},{8,9},{9,8},{10,11... | collective-permute-start | bytes 2949128 | tf_op jit(solution)/shard_map/ppermute | solution.py:889
  134.7 24.5 %collective-permute-start.26 = (bf16[4,240,512]{2,1,0:T(8,128)(2,1)S(1)}, bf16[4,240,512]{2,1,0:T(8,128)(2,1)}, u32[]{:S(2)}, u32[]{:S(2)}) collective-permute-start(bf16[4,240,512]{2,1,0:T(8,128)(2,1)S(1)} %pad_maximum_fusion.1.refs_1_.refs_9_), channel_id=1, source_target_pairs={{0,2},{1,17},{2,0},{3,19},{4,6},{5,21},{6,4},{7,23},{8,10},{9,25},... | collective-permute-start | bytes 2949128 | tf_op jit(solution)/shard_map/ppermute | solution.py:889
  137.2 22.0 %collective-permute-start.25 = (bf16[4,240,512]{2,1,0:T(8,128)(2,1)S(1)}, bf16[4,240,512]{2,1,0:T(8,128)(2,1)S(1)}, u32[]{:S(2)}, u32[]{:S(2)}) collective-permute-start(bf16[4,240,512]{2,1,0:T(8,128)(2,1)S(1)} %pad_maximum_fusion.1.refs_1_.refs_9_), channel_id=1, source_target_pairs={{0,16},{1,3},{2,18},{3,1},{4,20},{5,7},{6,22},{7,5},{8,24},{9,11},... | collective-permute-start | bytes 2949128 | tf_op jit(solution)/shard_map/ppermute | solution.py:889
  173.4 19.7 %collective-permute-start.36 = (bf16[4,160,512]{2,1,0:T(8,128)(2,1)}, bf16[4,160,512]{2,1,0:T(8,128)(2,1)}, u32[]{:S(2)}, u32[]{:S(2)}) collective-permute-start(bf16[4,160,512]{2,1,0:T(8,128)(2,1)} %pad_maximum_fusion.3.refs_1_.refs_2_.refs_17_), channel_id=1, source_target_pairs={{0,2},{1,17},{2,0},{3,19},{4,6},{5,21},{6,4},{7,23},{8,10},{9,25},... | collective-permute-start | bytes 1966088 | tf_op jit(solution)/shard_map/ppermute | solution.py:889
  194.8 26.3 %collective-permute-start.42 = (bf16[512,1024]{1,0:T(8,128)(2,1)}, bf16[512,1024]{1,0:T(8,128)(2,1)S(1)}, u32[]{:S(2)}, u32[]{:S(2)}) collective-permute-start(bf16[512,1024]{1,0:T(8,128)(2,1)} %dynamic-slice_bitcast_fusion), channel_id=1, source_target_pairs={{0,16},{16,0},{1,17},{17,1},{2,18},{18,2},{3,19},{19,3},{4,20},{20... | collective-permute-start | bytes 3145736 | tf_op jit(solution)/shard_map/ppermute | solution.py:970
  196.5 26.1 %collective-permute-start.40 = (bf16[4,160,512]{2,1,0:T(8,128)(2,1)}, bf16[4,160,512]{2,1,0:T(8,128)(2,1)}, u32[]{:S(2)}, u32[]{:S(2)}) collective-permute-start(bf16[4,160,512]{2,1,0:T(8,128)(2,1)} %collective-permute-done.35.refs_3_.refs_4_.refs_19_), channel_id=1, source_target_pairs={{0,1},{1,0},{2,3},{3,2},{4,5},{5,4},{6,7},{7,6},{8,9},{9,8},{10,11... | collective-permute-start | bytes 1966088 | tf_op jit(solution)/shard_map/ppermute | solution.py:889
  196.5 26.1 %collective-permute-start.38 = (bf16[4,160,512]{2,1,0:T(8,128)(2,1)}, bf16[4,160,512]{2,1,0:T(8,128)(2,1)}, u32[]{:S(2)}, u32[]{:S(2)}) collective-permute-start(bf16[4,160,512]{2,1,0:T(8,128)(2,1)} %pad_maximum_fusion.3.refs_1_.refs_2_.refs_17_), channel_id=1, source_target_pairs={{0,1},{1,0},{2,3},{3,2},{4,5},{5,4},{6,7},{7,6},{8,9},{9,8},{10,11... | collective-permute-start | bytes 1966088 | tf_op jit(solution)/shard_map/ppermute | solution.py:889
  197.0 25.6 %collective-permute-start.39 = (bf16[4,160,512]{2,1,0:T(8,128)(2,1)}, bf16[4,160,512]{2,1,0:T(8,128)(2,1)}, u32[]{:S(2)}, u32[]{:S(2)}) collective-permute-start(bf16[4,160,512]{2,1,0:T(8,128)(2,1)} %collective-permute-done.36.refs_2_.refs_3_.refs_18_), channel_id=1, source_target_pairs={{0,1},{1,0},{2,3},{3,2},{4,5},{5,4},{6,7},{7,6},{8,9},{9,8},{10,11... | collective-permute-start | bytes 1966088 | tf_op jit(solution)/shard_map/ppermute | solution.py:889
  250.3 31.3 %collective-permute-start.43 = (bf16[512,512]{1,0:T(8,128)(2,1)S(1)}, bf16[512,512]{1,0:T(8,128)(2,1)S(1)}, u32[]{:S(2)}, u32[]{:S(2)}) collective-permute-start(bf16[512,512]{1,0:T(8,128)(2,1)S(1)} %get-tuple-element.292), channel_id=1, source_target_pairs={{0,16},{16,0},{1,17},{17,1},{2,18},{18,2},{3,19},{19,3},{4,20},{20... | collective-permute-start | bytes 1572872 | tf_op jit(solution)/shard_map/ppermute | solution.py:970
  252.0 29.6 %collective-permute-start.44 = (bf16[16,176,512]{2,1,0:T(8,128)(2,1)}, bf16[16,176,512]{2,1,0:T(8,128)(2,1)}, u32[]{:S(2)}, u32[]{:S(2)}) collective-permute-start(bf16[16,176,512]{2,1,0:T(8,128)(2,1)} %get-tuple-element.164), channel_id=1, source_target_pairs={{0,1},{1,0},{2,3},{3,2},{4,5},{5,4},{6,7},{7,6},{8,9},{9,8},{10,11... | collective-permute-start | bytes 8650760 | tf_op jit(solution)/shard_map/ppermute | solution.py:889
  281.6 27.9 %collective-permute-start.46 = (bf16[16,192,512]{2,1,0:T(8,128)(2,1)}, bf16[16,192,512]{2,1,0:T(8,128)(2,1)S(1)}, u32[]{:S(2)}, u32[]{:S(2)}) collective-permute-start(bf16[16,192,512]{2,1,0:T(8,128)(2,1)} %get-tuple-element.178), channel_id=1, source_target_pairs={{0,1},{1,0},{2,3},{3,2},{4,5},{5,4},{6,7},{7,6},{8,9},{9,8},{10,11... | collective-permute-start | bytes 9437192 | tf_op jit(solution)/shard_map/ppermute | solution.py:889
  286.4 23.0 %collective-permute-start.45 = (bf16[8,176,512]{2,1,0:T(8,128)(2,1)}, bf16[8,176,512]{2,1,0:T(8,128)(2,1)}, u32[]{:S(2)}, u32[]{:S(2)}) collective-permute-start(bf16[8,176,512]{2,1,0:T(8,128)(2,1)} %get-tuple-element.265), channel_id=1, source_target_pairs={{0,16},{1,3},{2,18},{3,1},{4,20},{5,7},{6,22},{7,5},{8,24},{9,11},... | collective-permute-start | bytes 4325384 | tf_op jit(solution)/shard_map/ppermute | solution.py:889
  312.4 27.7 %collective-permute-start.48 = (bf16[4,176,512]{2,1,0:T(8,128)(2,1)}, bf16[4,176,512]{2,1,0:T(8,128)(2,1)S(1)}, u32[]{:S(2)}, u32[]{:S(2)}) collective-permute-start(bf16[4,176,512]{2,1,0:T(8,128)(2,1)} %get-tuple-element.275), channel_id=1, source_target_pairs={{0,2},{1,17},{2,0},{3,19},{4,6},{5,21},{6,4},{7,23},{8,10},{9,25},... | collective-permute-start | bytes 2162696 | tf_op jit(solution)/shard_map/ppermute | solution.py:889
  313.0 27.2 %collective-permute-start.50 = (bf16[16,208,512]{2,1,0:T(8,128)(2,1)}, bf16[16,208,512]{2,1,0:T(8,128)(2,1)}, u32[]{:S(2)}, u32[]{:S(2)}) collective-permute-start(bf16[16,208,512]{2,1,0:T(8,128)(2,1)} %get-tuple-element.205), channel_id=1, source_target_pairs={{0,1},{1,0},{2,3},{3,2},{4,5},{5,4},{6,7},{7,6},{8,9},{9,8},{10,11... | collective-permute-start | bytes 10223624 | tf_op jit(solution)/shard_map/ppermute | solution.py:889
  315.6 24.5 %collective-permute-start.49 = (bf16[8,192,512]{2,1,0:T(8,128)(2,1)}, bf16[8,192,512]{2,1,0:T(8,128)(2,1)S(1)}, u32[]{:S(2)}, u32[]{:S(2)}) collective-permute-start(bf16[8,192,512]{2,1,0:T(8,128)(2,1)} %get-tuple-element.263), channel_id=1, source_target_pairs={{0,16},{1,3},{2,18},{3,1},{4,20},{5,7},{6,22},{7,5},{8,24},{9,11},... | collective-permute-start | bytes 4718600 | tf_op jit(solution)/shard_map/ppermute | solution.py:889
  346.6 32.8 %collective-permute-start.62 = (bf16[8,208,512]{2,1,0:T(8,128)(2,1)}, bf16[8,208,512]{2,1,0:T(8,128)(2,1)}, u32[]{:S(2)}, u32[]{:S(2)}) collective-permute-start(bf16[8,208,512]{2,1,0:T(8,128)(2,1)} %get-tuple-element.261), channel_id=1, source_target_pairs={{0,16},{1,3},{2,18},{3,1},{4,20},{5,7},{6,22},{7,5},{8,24},{9,11},... | collective-permute-start | bytes 5111816 | tf_op jit(solution)/shard_map/ppermute | solution.py:889
  355.2 35.3 %collective-permute-start.47 = (bf16[512,512]{1,0:T(8,128)(2,1)S(1)}, bf16[512,512]{1,0:T(8,128)(2,1)S(1)}, u32[]{:S(2)}, u32[]{:S(2)}) collective-permute-start(bf16[512,512]{1,0:T(8,128)(2,1)S(1)} %select_convert_fusion), channel_id=1, source_target_pairs={{0,16},{16,0},{1,17},{17,1},{2,18},{18,2},{3,19},{19,3},{4,20},{20... | collective-permute-start | bytes 1572872 | tf_op jit(solution)/shard_map/ppermute | solution.py:970
  360.8 56.2 %collective-permute-start.52 = (bf16[8,224,512]{2,1,0:T(8,128)(2,1)S(1)}, bf16[8,224,512]{2,1,0:T(8,128)(2,1)S(1)}, u32[]{:S(2)}, u32[]{:S(2)}) collective-permute-start(bf16[8,224,512]{2,1,0:T(8,128)(2,1)S(1)} %get-tuple-element.259), channel_id=1, source_target_pairs={{0,16},{1,3},{2,18},{3,1},{4,20},{5,7},{6,22},{7,5},{8,24},{9,11},... | collective-permute-start | bytes 5505032 | tf_op jit(solution)/shard_map/ppermute | solution.py:889
  362.3 33.1 %collective-permute-start.57 = (bf16[4,192,512]{2,1,0:T(8,128)(2,1)S(1)}, bf16[4,192,512]{2,1,0:T(8,128)(2,1)S(1)}, u32[]{:S(2)}, u32[]{:S(2)}) collective-permute-start(bf16[4,192,512]{2,1,0:T(8,128)(2,1)S(1)} %get-tuple-element.271), channel_id=1, source_target_pairs={{0,2},{1,17},{2,0},{3,19},{4,6},{5,21},{6,4},{7,23},{8,10},{9,25},... | collective-permute-start | bytes 2359304 | tf_op jit(solution)/shard_map/ppermute | solution.py:889
  381.3 21.9 %collective-permute-start.63 = (bf16[4,208,512]{2,1,0:T(8,128)(2,1)S(1)}, bf16[4,208,512]{2,1,0:T(8,128)(2,1)S(1)}, u32[]{:S(2)}, u32[]{:S(2)}) collective-permute-start(bf16[4,208,512]{2,1,0:T(8,128)(2,1)S(1)} %get-tuple-element.269), channel_id=1, source_target_pairs={{0,2},{1,17},{2,0},{3,19},{4,6},{5,21},{6,4},{7,23},{8,10},{9,25},... | collective-permute-start | bytes 2555912 | tf_op jit(solution)/shard_map/ppermute | solution.py:889
  392.9 39.6 %collective-permute-start.67 = (bf16[176,512]{1,0:T(8,128)(2,1)S(1)}, bf16[176,512]{1,0:T(8,128)(2,1)S(1)}, u32[]{:S(2)}, u32[]{:S(2)}) collective-permute-start(bf16[176,512]{1,0:T(8,128)(2,1)S(1)} %get-tuple-element.287), channel_id=1, source_target_pairs={{0,4},{1,5},{2,6},{3,7},{4,0},{5,1},{6,2},{7,3},{8,12},{9,13},{10,... | collective-permute-start | bytes 540680 | tf_op jit(solution)/shard_map/ppermute | solution.py:889
  393.2 41.8 %collective-permute-start.69 = (bf16[176,512]{1,0:T(8,128)(2,1)S(1)}, bf16[176,512]{1,0:T(8,128)(2,1)S(1)}, u32[]{:S(2)}, u32[]{:S(2)}) collective-permute-start(bf16[176,512]{1,0:T(8,128)(2,1)S(1)} %get-tuple-element.288), channel_id=1, source_target_pairs={{0,12},{1,13},{2,14},{3,15},{4,8},{5,9},{6,10},{7,11},{8,4},{9,5},... | collective-permute-start | bytes 540680 | tf_op jit(solution)/shard_map/ppermute | solution.py:889
  420.7 53.7 %collective-permute-start.58 = (bf16[192,512]{1,0:T(8,128)(2,1)}, bf16[192,512]{1,0:T(8,128)(2,1)}, u32[]{:S(2)}, u32[]{:S(2)}) collective-permute-start(bf16[192,512]{1,0:T(8,128)(2,1)} %get-tuple-element.284), channel_id=1, source_target_pairs={{0,4},{1,5},{2,6},{3,7},{4,0},{5,1},{6,2},{7,3},{8,12},{9,13},{10,... | collective-permute-start | bytes 589832 | tf_op jit(solution)/shard_map/ppermute | solution.py:889
  432.5 41.9 %collective-permute-start.60 = (bf16[192,512]{1,0:T(8,128)(2,1)}, bf16[192,512]{1,0:T(8,128)(2,1)}, u32[]{:S(2)}, u32[]{:S(2)}) collective-permute-start(bf16[192,512]{1,0:T(8,128)(2,1)} %get-tuple-element.285), channel_id=1, source_target_pairs={{0,12},{1,13},{2,14},{3,15},{4,8},{5,9},{6,10},{7,11},{8,4},{9,5},... | collective-permute-start | bytes 589832 | tf_op jit(solution)/shard_map/ppermute | solution.py:889
  447.4 25.2 %collective-permute-start.55 = (bf16[224,512]{1,0:T(8,128)(2,1)}, bf16[224,512]{1,0:T(8,128)(2,1)}, u32[]{:S(2)}, u32[]{:S(2)}) collective-permute-start(bf16[224,512]{1,0:T(8,128)(2,1)} %get-tuple-element.280), channel_id=1, source_target_pairs={{0,8},{1,9},{2,10},{3,11},{4,12},{5,13},{6,14},{7,15},{8,0},{9,1},... | collective-permute-start | bytes 688136 | tf_op jit(solution)/shard_map/ppermute | solution.py:889
  451.7 25.0 %collective-permute-start.59 = (bf16[192,512]{1,0:T(8,128)(2,1)}, bf16[192,512]{1,0:T(8,128)(2,1)S(1)}, u32[]{:S(2)}, u32[]{:S(2)}) collective-permute-start(bf16[192,512]{1,0:T(8,128)(2,1)} %get-tuple-element.286), channel_id=1, source_target_pairs={{0,8},{1,9},{2,10},{3,11},{4,12},{5,13},{6,14},{7,15},{8,0},{9,1},... | collective-permute-start | bytes 589832 | tf_op jit(solution)/shard_map/ppermute | solution.py:889
  (87 other events, 1213.1 us)

commit v2 on v1

--- a/solution.py
+++ b/solution.py
@@ -367,7 +367,7 @@
     return logits, top + jnp.log(jnp.sum(e, axis=-1, keepdims=True))
 
 
-def head_bwd(x4, sent, w, allowed, cot, prm, length, extra, out, gl, gsent, small):
+def head_bwd(x4, sent, w, allowed, cot, prm, length, extra, out, gl, small):
     permit = allowed[...] > 0
     gain = prm[TAPS + 5 : TAPS + 6, :]
 
@@ -380,7 +380,7 @@
         gl[rs, :] = g
         gs = dotn(g, hw)
         if extra is not None:
-            gs = gs + extra[rs, :].astype(F32)
+            gs = gs + extra[rs, :].astype(BF).astype(F32)
         u, r = unit_rows(x4[rs, :])
         dv, gg = unit_back(gs * row_mask(length, start, RB, 512), u, r, gain)
         out[rs, :] = dv
@@ -390,32 +390,81 @@
 
 
 ANY, VMEM, SMEM = pl.ANY, pltpu.VMEM, pltpu.SMEM
+LATE = object()
+
+
+class Late:
+    def __init__(self, source, held, sem):
+        self.copy, self.held, self.going, self.here = pltpu.make_async_copy(source, held, sem), held, False, False
+
+    def go(self):
+        self.going = True
+        self.copy.start()
+
+    def get(self):
+        if not self.going:
+            self.go()
+        if not self.here:
+            self.copy.wait()
+        self.here = True
+        return self.held
+
+
+class Soon:
+    def __init__(self, held, target, sem):
+        self.copy, self.held, self.going = pltpu.make_async_copy(held, target, sem), held, False
+
+    def go(self):
+        self.going = True
+        self.copy.start()
+
+    def end(self):
+        if not self.going:
+            self.go()
+        self.copy.wait()
 
 
 def run(body, micros, ins, outs, scratch):
-    flat = []
+    flat, held = [], []
     for value, space in ins.values():
-        flat += [(array, space) for array in (value if isinstance(value, list) else [value])]
+        flat += [(array, ANY if space is LATE else space) for array in (value if isinstance(value, list) else [value])]
+        if space is LATE:
+            held.append((value.shape, value.dtype))
+    held += [(shape, dtype) for shape, dtype, space in outs.values() if space is LATE]
 
     def kernel(*refs):
         left = list(refs)
         ns = types.SimpleNamespace()
-        for key, (value, _) in ins.items():
+        waiting, soon = [], []
+        for key, (value, space) in ins.items():
             if isinstance(value, list):
                 setattr(ns, key, [left.pop(0) for _ in value])
             else:
                 setattr(ns, key, left.pop(0))
         for key in [*outs, *scratch]:
             setattr(ns, key, left.pop(0))
-        ns.sems = left.pop(0)
+        ns.sems = left.pop()
+        number = 8
+        for key, (_, space) in ins.items():
+            if space is LATE:
+                setattr(ns, key, Late(getattr(ns, key), left.pop(0), ns.sems.at[number]))
+                number += 1
+        for key, (_, _, space) in outs.items():
+            if space is LATE:
+                soon.append(Soon(left.pop(0), getattr(ns, key), ns.sems.at[number]))
+                setattr(ns, key, soon[-1])
+                number += 1
         body(ns)
+        for result in soon:
+            result.end()
 
     result = pl.pallas_call(
         kernel,
         out_shape=[jax.ShapeDtypeStruct(shape, dtype) for shape, dtype, _ in outs.values()],
         in_specs=[pl.BlockSpec(memory_space=space) for _, space in flat],
-        out_specs=[pl.BlockSpec(memory_space=space) for _, _, space in outs.values()],
-        scratch_shapes=[pltpu.VMEM(shape, dtype) for shape, dtype in scratch.values()] + [pltpu.SemaphoreType.DMA((8,))],
+        out_specs=[pl.BlockSpec(memory_space=ANY if space is LATE else space) for _, _, space in outs.values()],
+        scratch_shapes=[pltpu.VMEM(shape, dtype) for shape, dtype in [*scratch.values(), *held]]
+        + [pltpu.SemaphoreType.DMA((8 + len(held),))],
         compiler_params=pltpu.CompilerParams(vmem_limit_bytes=58 * 2**20),
         cost_estimate=pl.CostEstimate(flops=int(micros * 1.1e9), bytes_accessed=2**20, transcendentals=0),
         name=body.__name__,
@@ -424,11 +473,19 @@
 
 
 ROWS = (512, 512)
+WF, WA, WC, WH = ((16, FEED, 512), BF), ((16, ATTN, 512), BF), ((16, CONV, 512), BF), ((32, FLAT, 512), BF)
+PADDED = ((512 + 2 * PAD, 512), F32)
+LATE_ROWS = ATTN // 2 + CONV // 2
+
+
+def gain_of(prm, number):
+    return prm[TAPS + number : TAPS + number + 1, :]
 
 
 def kernel_stem_feed(ids, bufs, frames):
     def stem_feed(k):
         start_load(k.ids, k.bufs, 0, FLAT, k.stem, k.sems.at[0], flat=True)
+        k.frames.go()
         start_load(k.ids, k.bufs, FLAT, FEED // 2, k.w, k.sems.at[1])
         wait_load(k.stem, k.sems.at[0])
         stem = k.stem[...].astype(F32)
@@ -439,78 +496,74 @@
                     part = part + stem[layer * 16 + z * 4 + q, 24:32, :]
                 k.prm[layer, 0:8, 128 * z : 128 * z + 128] = part[:, 0:128]
                 k.prm[layer, 8:16, 128 * z : 128 * z + 128] = part[:, 128:256]
-        k.win_a[...] = stem[:, 0:8, :].reshape(256, 512).astype(BF)
-        k.win_b[...] = stem[:, 8:16, 0:128].reshape(256, 128).astype(BF)
+        win_a = stem[:, 0:8, :].reshape(256, 512).astype(BF)
+        win_b = stem[:, 8:16, 0:128].reshape(256, 128).astype(BF)
         k.wout[...] = stem[:, 16:24, :].reshape(256, 512).astype(BF)
+        frames, x0, x1, hid, pre = k.frames.get(), k.x0.held, k.x1.held, k.hid.held, k.pre.held
 
         def rows(rs, start):
-            pre = dotr(k.frames[rs, 0:512], k.win_a[...]) + dotr(k.frames[rs, 512:640], k.win_b[...])
-            k.pre[rs, :] = pre
-            x = dotn((pre * sigmoid(pre)).astype(BF), k.wout[...])
-            k.x0[rs, :] = (x * row_mask(k.ids[4], start, RB, 512)).astype(BF)
+            p = dotr(frames[rs, 0:512], win_a) + dotr(frames[rs, 512:640], win_b)
+            pre[rs, :] = p
+            x = dotn((p * sigmoid(p)).astype(BF), k.wout[...])
+            x0[rs, :] = (x * row_mask(k.ids[4], start, RB, 512)).astype(BF)
 
         row_loop(rows)
+        k.pre.go()
+        k.x0.go()
         wait_load(k.w, k.sems.at[1])
-        feed_fwd(k.x0, k.w, k.prm[0, TAPS : TAPS + 1, :], k.hid, k.x1)
+        feed_fwd(x0, k.w, gain_of(k.prm.at[0], 0), hid, x1)
 
     return run(
         stem_feed,
         9,
-        dict(ids=(ids, SMEM), bufs=(bufs, ANY), frames=(frames, VMEM)),
+        dict(ids=(ids, SMEM), bufs=(bufs, ANY), frames=(frames, LATE)),
         dict(
             prm=((2, SMALL, 512), F32, VMEM),
-            pre=((512, 256), F32, VMEM),
-            win_a=((256, 512), BF, VMEM),
-            win_b=((256, 128), BF, VMEM),
+            pre=((512, 256), F32, LATE),
             wout=((256, 512), BF, VMEM),
-            x0=(ROWS, BF, VMEM),
-            hid=((512, FF), BF, VMEM),
-            x1=(ROWS, F32, VMEM),
+            x0=(ROWS, BF, LATE),
+            hid=((512, FF), BF, LATE),
+            x1=(ROWS, F32, LATE),
         ),
-        dict(stem=((32, FLAT, 512), BF), w=((16, FEED, 512), BF)),
-    )
-
-
-ATTN_OUTS = dict(
-    qkv=((512, 1536), BF, VMEM),
-    ls=((8, 512), F32, VMEM),
-    mixed=(ROWS, BF, VMEM),
-    x2=(ROWS, F32, VMEM),
-)
-CONV_OUTS = dict(
-    gated=((512, 1024), F32, VMEM),
-    deep=(ROWS, F32, VMEM),
-    x3=(ROWS, F32, VMEM),
-)
+        dict(stem=WH, w=WF),
+    )
+
+
+ATTN_OUTS = dict(qkv=((512, 1536), BF, LATE), ls=((8, 512), F32, VMEM), mixed=(ROWS, BF, LATE), x2=(ROWS, F32, LATE))
+CONV_OUTS = dict(gated=((512, 1024), F32, LATE), deep=(ROWS, F32, LATE), x3=(ROWS, F32, LATE))
+
+
+def attn_conv(k, x1, prm):
+    wait_load(k.wa, k.sems.at[0])
+    attn_fwd(x1, k.wa, gain_of(prm, 1), k.ids[4], k.qkv.held, k.ls, k.mixed.held, k.x2.held)
+    for result in (k.qkv, k.mixed, k.x2):
+        result.go()
+    wait_load(k.wc, k.sems.at[1])
+    conv_fwd(k.x2.held, k.wc, prm, k.ids[4], k.gated.held, k.deep.held, k.x3.held, k.pad)
+    for result in (k.gated, k.deep, k.x3):
+        result.go()
 
 
 def kernel_rest_first(ids, bufs, prm, x1):
     def rest_first(k):
+        k.x1.go()
         start_load(k.ids, k.bufs, 0, ATTN // 2, k.wa, k.sems.at[0])
         start_load(k.ids, k.bufs, ATTN // 2, CONV // 2, k.wc, k.sems.at[1])
-        start_load(k.ids, k.bufs, ATTN // 2 + CONV // 2, FEED // 2, k.wf, k.sems.at[2])
+        start_load(k.ids, k.bufs, LATE_ROWS, FEED // 2, k.wf, k.sems.at[2])
         prm = k.prm.at[0]
-        wait_load(k.wa, k.sems.at[0])
-        attn_fwd(k.x1, k.wa, prm[TAPS + 1 : TAPS + 2, :], k.ids[4], k.qkv, k.ls, k.mixed, k.x2)
-        wait_load(k.wc, k.sems.at[1])
-        conv_fwd(k.x2, k.wc, prm, k.ids[4], k.gated, k.deep, k.x3, k.pad)
+        attn_conv(k, k.x1.get(), prm)
         wait_load(k.wf, k.sems.at[2])
-        feed_fwd(k.x3, k.wf, prm[TAPS + 4 : TAPS + 5, :], k.hid, k.x4)
-        finish_fwd(k.x4, prm, k.ids[4], k.sent)
+        feed_fwd(k.x3.held, k.wf, gain_of(prm, 4), k.hid.held, k.x4.held)
+        k.hid.go()
+        k.x4.go()
+        finish_fwd(k.x4.held, prm, k.ids[4], k.sent)
 
     return run(
         rest_first,
-        24,
-        dict(ids=(ids, SMEM), bufs=(bufs, ANY), prm=(prm, VMEM), x1=(x1, VMEM)),
-        ATTN_OUTS
-        | CONV_OUTS
-        | dict(hid=((512, FF), BF, VMEM), x4=(ROWS, F32, VMEM), sent=(ROWS, BF, VMEM)),
-        dict(
-            wa=((16, ATTN, 512), BF),
-            wc=((16, CONV, 512), BF),
-            wf=((16, FEED, 512), BF),
-            pad=((512 + 2 * PAD, 512), F32),
-        ),
+        20,
+        dict(ids=(ids, SMEM), bufs=(bufs, ANY), prm=(prm, VMEM), x1=(x1, LATE)),
+        ATTN_OUTS | CONV_OUTS | dict(hid=((512, FF), BF, LATE), x4=(ROWS, F32, LATE), sent=(ROWS, BF, VMEM)),
+        dict(wa=WA, wc=WC, wf=WF, pad=PADDED),
     )
 
 
@@ -521,280 +574,269 @@
         start_load(k.ids, k.bufs, FEED // 2 + ATTN // 2, CONV // 2, k.wc, k.sems.at[1])
         prm = k.prm.at[1]
         wait_load(k.wf, k.sems.at[2])
-        feed_fwd(k.x0, k.wf, prm[TAPS : TAPS + 1, :], k.hid, k.x1)
-        wait_load(k.wa, k.sems.at[0])
-        attn_fwd(k.x1, k.wa, prm[TAPS + 1 : TAPS + 2, :], k.ids[4], k.qkv, k.ls, k.mixed, k.x2)
-        wait_load(k.wc, k.sems.at[1])
-        conv_fwd(k.x2, k.wc, prm, k.ids[4], k.gated, k.deep, k.x3, k.pad)
+        feed_fwd(k.x0, k.wf, gain_of(prm, 0), k.hid.held, k.x1.held)
+        k.hid.go()
+        k.x1.go()
+        attn_conv(k, k.x1.held, prm)
 
     return run(
         first_second,
-        24,
+        20,
         dict(ids=(ids, SMEM), bufs=(bufs, ANY), prm=(prm, VMEM), x0=(x0, VMEM)),
-        dict(hid=((512, FF), BF, VMEM), x1=(ROWS, F32, VMEM)) | ATTN_OUTS | CONV_OUTS,
-        dict(
-            wa=((16, ATTN, 512), BF),
-            wc=((16, CONV, 512), BF),
-            wf=((16, FEED, 512), BF),
-            pad=((512 + 2 * PAD, 512), F32),
-        ),
-    )
-
-
-def kernel_turn(ids, feed_bufs, conv_bufs, prm, x3, cot, allowed, x2, gated, deep):
+        dict(hid=((512, FF), BF, LATE), x1=(ROWS, F32, LATE)) | ATTN_OUTS | CONV_OUTS,
+        dict(wa=WA, wc=WC, wf=WF, pad=PADDED),
+    )
+
+
+def start_cot(k, layer):
+    @pl.when(k.ids[5] == layer)
+    def _():
+        pltpu.make_async_copy(k.cots.at[k.ids[5]], k.cot, k.sems.at[2]).start()
+
+    @pl.when(k.ids[5] != layer)
+    def _():
+        for number, part in enumerate(k.cot_other):
+            pltpu.make_async_copy(part, k.cot.at[256 * number : 256 * number + 256], k.sems.at[2]).start()
+
+
+FEED_SCRATCH = dict(n=(ROWS, BF), d=(ROWS, BF), act=((512, FF), BF), dh=((512, FF), BF), wf=WF, gf=WF)
+HEAD_SCRATCH = dict(wh=WH, cot=((512, 1024), BF), gl=((512, 1024), BF), dx4=(ROWS, F32))
+
+
+def kernel_turn(ids, bufs, prm, x3, cots, cot_other, allowed):
     def turn(k):
-        start_load(k.ids, k.fbufs, 0, FEED // 2, k.wf, k.sems.at[0])
-        start_load(k.ids, k.fbufs, FEED // 2, FLAT, k.wh, k.sems.at[1], flat=True)
-        start_load(k.ids, k.cbufs, FEED // 2 + ATTN // 2, CONV // 2, k.wc, k.sems.at[2])
+        k.x3.go()
+        start_load(k.ids, k.bufs, 0, FEED // 2, k.wf, k.sems.at[0])
+        start_load(k.ids, k.bufs, FEED // 2, FLAT, k.wh, k.sems.at[1], flat=True)
+        start_cot(k, 1)
         prm = k.prm.at[1]
         k.small[...] = jnp.zeros((SMALL, 512), F32)
+        x3 = k.x3.get()
         wait_load(k.wf, k.sems.at[0])
-        feed_fwd(k.x3, k.wf, prm[TAPS + 4 : TAPS + 5, :], k.hid, k.x4)
+        feed_fwd(x3, k.wf, gain_of(prm, 4), k.hid, k.x4)
         finish_fwd(k.x4, prm, k.ids[4], k.sent)
         wait_load(k.wh, k.sems.at[1])
-        head_bwd(k.x4, k.sent, k.wh, k.allowed, k.cot, prm, k.ids[4], None, k.dx4, k.gl, None, k.small)
-        k.ghead[...] = dotl(k.gl[...], k.sent[...])
-        feed_bwd(
-            k.dx4,
-            k.x3,
-            k.hid,
-            k.wf,
-            prm[TAPS + 4 : TAPS + 5, :],
-            k.dx3,
-            k.gf,
-            k.small,
-            TAPS + 4,
-            k,
-        )
+        wait_load(k.cot, k.sems.at[2])
+        head_bwd(k.x4, k.sent, k.wh, k.allowed, k.cot, prm, k.ids[4], None, k.dx4, k.gl, k.small)
+        k.ghead.held[...] = dotl(k.gl[...], k.sent[...])
+        k.ghead.go()
+        feed_bwd(k.dx4, x3, k.hid, k.wf, gain_of(prm, 4), k.dx3.held, k.gf, k.small, TAPS + 4, k)
         start_store(k.ids, k.gf, k.keep, k.send, 0, FEED // 2, k.sems.at[3])
-        wait_load(k.wc, k.sems.at[2])
-        s = types.SimpleNamespace(
-            n=k.n, d=k.d, act=k.act.at[:, 0:512], dga=k.dh.at[:, 0:512], dgb=k.dh.at[:, 512:1024], pad=k.pad, back=k.back
-        )
-        conv_bwd(k.dx3, k.x2, k.gated, k.deep, k.wc, prm, k.ids[4], k.dx2, k.gc, k.small, s)
-        start_store(k.ids, k.gc, k.keep, k.send, FEED // 2, CONV // 2, k.sems.at[4])
         wait_store(k.gf, k.sems.at[3])
-        wait_store(k.gc, k.sems.at[4])
-
-    rows = FEED // 2 + CONV // 2
+
+    rows = FEED // 2
     return run(
         turn,
-        32,
+        22,
         dict(
             ids=(ids, SMEM),
-            fbufs=(feed_bufs, ANY),
-            cbufs=(conv_bufs, ANY),
+            bufs=(bufs, ANY),
             prm=(prm, VMEM),
-            x3=(x3, VMEM),
-            cot=(cot, VMEM),
+            x3=(x3, LATE),
+            cots=(cots, ANY),
+            cot_other=(cot_other, ANY),
             allowed=(allowed, VMEM),
-            x2=(x2, VMEM),
-            gated=(gated, VMEM),
-            deep=(deep, VMEM),
         ),
         dict(
             sent=(ROWS, BF, VMEM),
-            ghead=((1024, 512), F32, VMEM),
-            dx2=(ROWS, F32, VMEM),
+            ghead=((1024, 512), F32, LATE),
+            dx3=(ROWS, F32, LATE),
             small=((SMALL, 512), F32, VMEM),
             keep=((16, rows, 512), BF, ANY),
             send=((16, rows, 512), BF, ANY),
         ),
-        dict(
-            wf=((16, FEED, 512), BF),
-            wh=((32, FLAT, 512), BF),
-            wc=((16, CONV, 512), BF),
-            gf=((16, FEED, 512), BF),
-            gc=((16, CONV, 512), BF),
-            hid=((512, FF), BF),
-            x4=(ROWS, F32),
-            gl=((512, 1024), BF),
-            dx4=(ROWS, F32),
-            dx3=(ROWS, F32),
-            n=(ROWS, BF),
-            d=(ROWS, BF),
-            act=((512, FF), BF),
-            dh=((512, FF), BF),
-            pad=((512 + 2 * PAD, 512), F32),
-            back=((512 + 2 * PAD, 512), F32),
-        ),
-    )
-
-
-def kernel_back_late(ids, feed_bufs, conv_bufs, head_bufs, prm, x4, sent, cot, allowed, ig, x3, hid, x2, gated, deep, ghead):
-    def back_late(k):
+        FEED_SCRATCH | HEAD_SCRATCH | dict(hid=((512, FF), BF), x4=(ROWS, F32)),
+    )
+
+
+def kernel_late(ids, bufs, head_bufs, prm, x4, sent, cots, cot_other, allowed, ig, x3, hid, ghead):
+    def late(k):
         start_load(k.ids, k.hbufs, FEED // 2, FLAT, k.wh, k.sems.at[1], flat=True)
-        start_load(k.ids, k.fbufs, ATTN // 2 + CONV // 2, FEED // 2, k.wf, k.sems.at[0])
-        start_load(k.ids, k.cbufs, ATTN // 2, CONV // 2, k.wc, k.sems.at[2])
+        start_cot(k, 0)
+        k.x4.go()
+        k.ig.go()
+        start_load(k.ids, k.bufs, LATE_ROWS, FEED // 2, k.wf, k.sems.at[0])
+        for operand in (k.ghead, k.x3, k.hid):
+            operand.go()
         prm = k.prm.at[0]
         k.small[...] = jnp.zeros((SMALL, 512), F32)
         wait_load(k.wh, k.sems.at[1])
-        head_bwd(k.x4, k.sent, k.wh, k.allowed, k.cot, prm, k.ids[4], k.ig, k.dx4, k.gl, None, k.small)
-        k.gh[...] = (k.ghead[...] + dotl(k.gl[...], k.sent[...])).astype(BF).reshape(32, FLAT, 512)
-        start_store(k.ids, k.gh, k.keep, k.send, FEED // 2 + CONV // 2, FLAT, k.sems.at[5], flat=True)
+        wait_load(k.cot, k.sems.at[2])
+        head_bwd(k.x4.get(), k.sent, k.wh, k.allowed, k.cot, prm, k.ids[4], k.ig.get(), k.dx4, k.gl, k.small)
+        k.gh[...] = (k.ghead.get()[...] + dotl(k.gl[...], k.sent[...])).astype(BF).reshape(32, FLAT, 512)
+        start_store(k.ids, k.gh, k.keep, k.send, FEED // 2, FLAT, k.sems.at[4], flat=True)
         wait_load(k.wf, k.sems.at[0])
-        feed_bwd(
-            k.dx4,
-            k.x3,
-            k.hid,
-            k.wf,
-            prm[TAPS + 4 : TAPS + 5, :],
-            k.dx3,
-            k.gf,
-            k.small,
-            TAPS + 4,
-            k,
-        )
+        feed_bwd(k.dx4, k.x3.get(), k.hid.get(), k.wf, gain_of(prm, 4), k.dx3.held, k.gf, k.small, TAPS + 4, k)
         start_store(k.ids, k.gf, k.keep, k.send, 0, FEED // 2, k.sems.at[3])
-        wait_load(k.wc, k.sems.at[2])
-        s = types.SimpleNamespace(
-            n=k.n, d=k.d, act=k.act.at[:, 0:512], dga=k.dh.at[:, 0:512], dgb=k.dh.at[:, 512:1024], pad=k.pad, back=k.back
-        )
-        conv_bwd(k.dx3, k.x2, k.gated, k.deep, k.wc, prm, k.ids[4], k.dx2, k.gc, k.small, s)
-        start_store(k.ids, k.gc, k.keep, k.send, FEED // 2, CONV // 2, k.sems.at[4])
-        wait_store(k.gh, k.sems.at[5])
+        wait_store(k.gh, k.sems.at[4])
         wait_store(k.gf, k.sems.at[3])
-        wait_store(k.gc, k.sems.at[4])
-
-    rows = FEED // 2 + CONV // 2 + FLAT
+
+    rows = FEED // 2 + FLAT
     return run(
-        back_late,
-        28,
+        late,
+        17,
         dict(
             ids=(ids, SMEM),
-            fbufs=(feed_bufs, ANY),
-            cbufs=(conv_bufs, ANY),
+            bufs=(bufs, ANY),
             hbufs=(head_bufs, ANY),
             prm=(prm, VMEM),
-            x4=(x4, VMEM),
+            x4=(x4, LATE),
             sent=(sent, VMEM),
-            cot=(cot, VMEM),
+            cots=(cots, ANY),
+            cot_other=(cot_other, ANY),
             allowed=(allowed, VMEM),
-            ig=(ig, VMEM),
-            x3=(x3, VMEM),
-            hid=(hid, VMEM),
-            x2=(x2, VMEM),
-            gated=(gated, VMEM),
-            deep=(deep, VMEM),
-            ghead=(ghead, VMEM),
+            ig=(ig, LATE),
+            x3=(x3, LATE),
+            hid=(hid, LATE),
+            ghead=(ghead, LATE),
         ),
         dict(
-            dx2=(ROWS, F32, VMEM),
+            dx3=(ROWS, F32, LATE),
             small=((SMALL, 512), F32, VMEM),
             keep=((16, rows, 512), BF, ANY),
             send=((16, rows, 512), BF, ANY),
         ),
+        FEED_SCRATCH | HEAD_SCRATCH | dict(gh=WH),
+    )
+
+
+def kernel_mid(layer, ids, bufs, row, prm, dx3, x2, gated, deep, x1, qkv, ls, mixed):
+    def mid(k):
+        for operand in (k.dx3, k.deep):
+            operand.go()
+        start_load(k.ids, k.bufs, row + ATTN // 2, CONV // 2, k.wc, k.sems.at[1])
+        for operand in (k.gated, k.x2):
+            operand.go()
+        start_load(k.ids, k.bufs, row, ATTN // 2, k.wa, k.sems.at[0])
+        for operand in (k.x1, k.mixed, k.qkv):
+            operand.go()
+        prm = k.prm.at[layer]
+        k.small[...] = jnp.zeros((SMALL, 512), F32)
+        wait_load(k.wc, k.sems.at[1])
+        s = types.SimpleNamespace(
+            n=k.n, d=k.d, act=k.act.at[:, 0:512], dga=k.dh.at[:, 0:512], dgb=k.dh.at[:, 512:1024], pad=k.pad, back=k.back
+        )
+        conv_bwd(k.dx3.get(), k.x2.get(), k.gated.get(), k.deep.get(), k.wc, prm, k.ids[4], k.dx2, k.gc, k.small, s)
+        start_store(k.ids, k.gc, k.keep, k.send, ATTN // 2, CONV // 2, k.sems.at[3])
+        wait_load(k.wa, k.sems.at[0])
+        s = types.SimpleNamespace(n=k.n, d=k.d, dm=k.dm, dpk=k.act, dq=k.dq, kt=k.kt)
+        attn_bwd(
+            k.dx2, k.x1.get(), k.qkv.get(), k.ls, k.mixed.get(), k.wa, gain_of(prm, 1), k.ids[4], k.dx1.held, k.ga,
+            k.small, TAPS + 1, s,
+        )
+        start_store(k.ids, k.ga, k.keep, k.send, 0, ATTN // 2, k.sems.at[2])
+        wait_store(k.gc, k.sems.at[3])
+        wait_store(k.ga, k.sems.at[2])
+
+    return run(
+        mid,
+        21,
         dict(
-            wf=((16, FEED, 512), BF),
-            wh=((32, FLAT, 512), BF),
-            wc=((16, CONV, 512), BF),
-            gf=((16, FEED, 512), BF),
-            gc=((16, CONV, 512), BF),
-            gh=((32, FLAT, 512), BF),
-            gl=((512, 1024), BF),
-            dx4=(ROWS, F32),
-            dx3=(ROWS, F32),
+            ids=(ids, SMEM),
+            bufs=(bufs, ANY),
+            prm=(prm, VMEM),
+            dx3=(dx3, LATE),
+            x2=(x2, LATE),
+            gated=(gated, LATE),
+            deep=(deep, LATE),
+            x1=(x1, LATE),
+            qkv=(qkv, LATE),
+            ls=(ls, VMEM),
+            mixed=(mixed, LATE),
+        ),
+        dict(
+            dx1=(ROWS, F32, LATE),
+            small=((SMALL, 512), F32, VMEM),
+            keep=((16, LATE_ROWS, 512), BF, ANY),
+            send=((16, LATE_ROWS, 512), BF, ANY),
+        ),
+        dict(
+            wa=WA,
+            wc=WC,
+            ga=WA,
+            gc=WC,
+            dx2=(ROWS, F32),
             n=(ROWS, BF),
             d=(ROWS, BF),
-            act=((512, FF), BF),
-            dh=((512, FF), BF),
-            pad=((512 + 2 * PAD, 512), F32),
-            back=((512 + 2 * PAD, 512), F32),
+            dm=(ROWS, BF),
+            act=((512, 1536), BF),
+            dh=((512, 1024), BF),
+            pad=PADDED,
+            back=PADDED,
+            dq=((128, 512), F32),
+            kt=((256, 512), BF),
         ),
     )
 
 
-def kernel_back_early(layer, ids, attn_bufs, attn_row, feed_bufs, feed_row, prm, dx2, x1, qkv, ls, mixed, x0, hid, stem):
-    def back_early_stem(k):
-        start_load(k.ids, k.abufs, attn_row, ATTN // 2, k.wa, k.sems.at[0])
-        start_load(k.ids, k.fbufs, feed_row, FEED // 2, k.wf, k.sems.at[1])
+def kernel_early(layer, ids, bufs, row, prm, dx1, x0, hid, stem):
+    def early(k):
+        k.dx1.go()
+        k.x0.go()
+        start_load(k.ids, k.bufs, row, FEED // 2, k.wf, k.sems.at[1])
+        k.hid.go()
+        if stem is not None:
+            k.pre.go()
+            k.frames.go()
         prm = k.prm.at[layer]
         k.small[...] = jnp.zeros((SMALL, 512), F32)
-        wait_load(k.wa, k.sems.at[0])
-        s = types.SimpleNamespace(n=k.n, d=k.d, dm=k.dm, dpk=k.act.at[:, 0:1536], dq=k.dq, kt=k.kt)
-        attn_bwd(
-            k.dx2, k.x1, k.qkv, k.ls, k.mixed, k.wa, prm[TAPS + 1 : TAPS + 2, :], k.ids[4], k.dx1, k.ga, k.small, TAPS + 1, s
-        )
-        start_store(k.ids, k.ga, k.keep, k.send, 0, ATTN // 2, k.sems.at[2])
         wait_load(k.wf, k.sems.at[1])
-        feed_bwd(
-            k.dx1,
-            k.x0,
-            k.hid,
-            k.wf,
-            prm[TAPS : TAPS + 1, :],
-            k.ig,
-            k.gf,
-            k.small,
-            TAPS,
-            k,
-        )
-        start_store(k.ids, k.gf, k.keep, k.send, ATTN // 2, FEED // 2, k.sems.at[3])
+        ig = k.ig.held
+        feed_bwd(k.dx1.get(), k.x0.get(), k.hid.get(), k.wf, gain_of(prm, 0), ig, k.gf, k.small, TAPS, k)
+        k.ig.go()
+        start_store(k.ids, k.gf, k.keep, k.send, 0, FEED // 2, k.sems.at[3])
         if stem is not None:
+            pre, frames = k.pre.get(), k.frames.get()
 
             def rows(rs, start):
-                d = (k.ig[rs, :] * row_mask(k.ids[4], start, RB, 512)).astype(BF)
+                d = (ig[rs, :] * row_mask(k.ids[4], start, RB, 512)).astype(BF)
                 k.d[rs, :] = d
-                pre = k.pre[rs, :]
-                sg = sigmoid(pre)
-                k.n[rs, 0:256] = (pre * sg).astype(BF)
-                k.n[rs, 256:512] = (dotr(d, k.wout[...]) * (sg * (1.0 + pre * (1.0 - sg)))).astype(BF)
+                p = pre[rs, :]
+                sg = sigmoid(p)
+                k.n[rs, 0:256] = (p * sg).astype(BF)
+                k.n[rs, 256:512] = (dotr(d, k.wout[...]) * (sg * (1.0 + p * (1.0 - sg)))).astype(BF)
 
             row_loop(rows)
-            k.gs[:, 0:8, :] = dotl(k.n[:, 256:512], k.frames[:, 0:512]).reshape(32, 8, 512)
-            k.gs[:, 8:16, 0:128] = dotl(k.n[:, 256:512], k.frames[:, 512:640]).reshape(32, 8, 128)
+            k.gs[:, 0:8, :] = dotl(k.n[:, 256:512], frames[:, 0:512]).reshape(32, 8, 512)
+            k.gs[:, 8:16, 0:128] = dotl(k.n[:, 256:512], frames[:, 512:640]).reshape(32, 8, 128)
             k.gs[:, 8:16, 128:512] = jnp.zeros((32, 8, 384), F32)
             k.gs[:, 16:24, :] = dotl(k.n[:, 0:256], k.d[...]).reshape(32, 8, 512)
-            first = k.small[...] + k.small_first[...]
-            for number, total in enumerate((first, k.small_second[...])):
+            first, second = k.small[...], jnp.zeros((SMALL, 512), F32)
+            for part in k.smalls[:2]:
+                first = first + part[...]
+            for part in k.smalls[2:]:
+                second = second + part[...]
+            for number, total in enumerate((first, second)):
                 for z in range(4):
                     lanes = slice(128 * z, 128 * z + 128)
                     block = jnp.concatenate([total[0:8, lanes], total[8:16, lanes], jnp.zeros((8, 256), F32)], axis=1)
                     for q in range(4):
                         k.gs[number * 16 + z * 4 + q, 24:32, :] = block
             k.gsb[...] = k.gs[...].astype(BF)
-            start_store(k.ids, k.gsb, k.keep, k.send, ATTN // 2 + FEED // 2, FLAT, k.sems.at[4], flat=True)
+            start_store(k.ids, k.gsb, k.keep, k.send, FEED // 2, FLAT, k.sems.at[4], flat=True)
             wait_store(k.gsb, k.sems.at[4])
-        wait_store(k.ga, k.sems.at[2])
         wait_store(k.gf, k.sems.at[3])
 
-    rows = ATTN // 2 + FEED // 2 + (0 if stem is None else FLAT)
+    rows = FEED // 2 + (0 if stem is None else FLAT)
     ins = dict(
         ids=(ids, SMEM),
-        abufs=(attn_bufs, ANY),
-        fbufs=(feed_bufs, ANY),
+        bufs=(bufs, ANY),
         prm=(prm, VMEM),
-        dx2=(dx2, VMEM),
-        x1=(x1, VMEM),
-        qkv=(qkv, VMEM),
-        ls=(ls, VMEM),
-        mixed=(mixed, VMEM),
-        x0=(x0, VMEM),
-        hid=(hid, VMEM),
-    )
-    scratch = dict(
-        wf=((16, FEED, 512), BF),
-        wa=((16, ATTN, 512), BF),
-        gf=((16, FEED, 512), BF),
-        ga=((16, ATTN, 512), BF),
-        dx1=(ROWS, F32),
-        n=(ROWS, BF),
-        d=(ROWS, BF),
-        dm=(ROWS, BF),
-        act=((512, FF), BF),
-        dh=((512, FF), BF),
-        dq=((128, 512), F32),
-        kt=((256, 512), BF),
-    )
+        dx1=(dx1, LATE),
+        x0=(x0, LATE),
+        hid=(hid, LATE),
+    )
+    scratch = dict(FEED_SCRATCH)
     if stem is not None:
-        ins |= {key: (value, VMEM) for key, value in stem.items()}
-        scratch |= dict(gs=((32, FLAT, 512), F32), gsb=((32, FLAT, 512), BF))
+        pre, wout, frames, smalls = stem
+        ins |= dict(pre=(pre, LATE), wout=(wout, VMEM), frames=(frames, LATE), smalls=(smalls, VMEM))
+        scratch |= dict(gs=((32, FLAT, 512), F32), gsb=WH)
     return run(
-        back_early_stem,
-        31,
+        early,
+        13 if stem is not None else 10,
         ins,
         dict(
-            ig=(ROWS, F32, VMEM),
+            ig=(ROWS, F32, LATE),
             small=((SMALL, 512), F32, VMEM),
             keep=((16, rows, 512), BF, ANY),
             send=((16, rows, 512), BF, ANY),
@@ -803,25 +845,25 @@
     )
 
 
-def kernel_outputs(ids, head_bufs, own, other, allowed, lengths):
+def kernel_outputs(ids, head_bufs, sent_first, sent_second, other, allowed, lengths):
     def outputs(k):
         start_load(k.ids, k.hbufs, FEED // 2, FLAT, k.wh, k.sems.at[0], flat=True)
+        for sec in range(2):
+
+            @pl.when(k.ids[5] == sec)
+            def _():
+                pltpu.make_async_copy(k.second if sec else k.first, k.sent.at[sec], k.sems.at[1]).start()
+                pltpu.make_async_copy(k.other, k.sent.at[1 - sec], k.sems.at[1]).start()
+
+        wait_load(k.sent, k.sems.at[1])
         wait_load(k.wh, k.sems.at[0])
-
-        @pl.loop(0, 2)
-        def _(batch):
-            length = k.lengths[batch]
-            permit = k.allowed[pl.ds(batch, 1), :] > 0
-
-            def rows(rs, start):
-                mine = (batch == k.ids[0]).astype(F32)
-                sent = (k.own[rs, :].astype(F32) * mine + k.other[rs, :].astype(F32) * (1.0 - mine)).astype(BF)
-                logits, logsum = head_rows(sent, k.wh[...].reshape(1024, 512), permit)
-                ok = row_mask(length, start, RB, 1024)
-                k.logp[batch, rs, :] = jnp.where(permit, logits - logsum, 0.0) * ok
-                k.acts[batch, rs, :] = sent.astype(F32)
-
-            row_loop(rows)
+        for batch in range(2):
+            permit = k.allowed[batch : batch + 1, :] > 0
+            sent = k.sent[batch]
+            logits, logsum = head_rows(sent, k.wh[...].reshape(1024, 512), permit)
+            ok = row_mask(k.lengths[batch], 0, 512, 1024)
+            k.logp.held[batch] = jnp.where(permit, logits - logsum, 0.0) * ok
+            k.acts.held[batch] = sent.astype(F32)
 
     return run(
         outputs,
@@ -830,13 +872,36 @@
             ids=(ids, SMEM),
             lengths=(lengths, SMEM),
             hbufs=(head_bufs, ANY),
-            own=(own, VMEM),
-            other=(other, VMEM),
+            first=(sent_first, ANY),
+            second=(sent_second, ANY),
+            other=(other, ANY),
             allowed=(allowed, VMEM),
         ),
-        dict(logp=((2, 512, 1024), F32, VMEM), acts=((2, 512, 512), F32, VMEM)),
-        dict(wh=((32, FLAT, 512), BF)),
-    )
+        dict(logp=((2, 512, 1024), F32, LATE), acts=((2, 512, 512), F32, LATE)),
+        dict(wh=WH, sent=((2, 512, 512), BF)),
+    )
+
+
+def kernel_grads(ids, first, second, other):
+    def grads(k):
+        sec = k.ids[5]
+        k.out.held[1 - sec] = k.other[...].astype(F32)
+
+        @pl.when(sec == 0)
+        def _():
+            k.out.held[0] = k.first[...]
+
+        @pl.when(sec != 0)
+        def _():
+            k.out.held[1] = k.second[...]
+
+    return run(
+        grads,
+        3,
+        dict(ids=(ids, SMEM), first=(first, VMEM), second=(second, VMEM), other=(other, VMEM)),
+        dict(out=((2, 512, 512), F32, LATE)),
+        dict(),
+    ).out
 
 
 def pack_feed(w_in, w_out):
@@ -956,165 +1021,182 @@
     dp = lax.axis_index("dp")
     first = sec == 0
     low = [m.astype(BF) for m in masters]
-    if fast:
-        ids = jnp.stack([sec, dp // 4, (dp // 2) % 2, dp % 2, lengths[sec, 0]]).astype(jnp.int32)
-        own = own_pieces(low, sec, dp, first)
-    else:
-        ids = jnp.stack([sec * 0, sec * 0, sec * 0, sec * 0, lengths[sec, 0]]).astype(jnp.int32)
-        chunks = gather_plain(low)
+    swap = lambda v: lax.ppermute(v, "section", [(0, 1), (1, 0)])
+    cots = cotangent[0, :, 0]
+    cot_send = lax.dynamic_index_in_dim(cots, 1 - sec, 0, keepdims=False)
+    place = [sec, dp // 4, (dp // 2) % 2, dp % 2] if fast else [sec * 0] * 4
+    ids = jnp.stack(place + [lengths[sec, 0], sec]).astype(jnp.int32)
     frames = lax.dynamic_index_in_dim(spectra, sec, 0, keepdims=False).reshape(512, -1)
     allowed_both = jnp.concatenate(
         [lax.dynamic_slice_in_dim(token_masks, languages[m, 0], 1, 0) for m in range(2)]
     ).astype(F32)
     allowed = lax.dynamic_slice_in_dim(allowed_both, sec, 1, 0)
-    swap = lambda v: lax.ppermute(v, "section", [(0, 1), (1, 0)])
-    cots = cotangent[0, :, 0]
-    cot_own = lax.dynamic_index_in_dim(cots, sec, 0, keepdims=False)
-    cot_other = swap(lax.dynamic_index_in_dim(cots, 1 - sec, 0, keepdims=False))
-    cot_first, cot_second = pick(first, cot_own, cot_other)
-
     if fast:
         chunks = [None] * 4
-        quad0 = jnp.stack(z_parts(own[0]))
+        own_first, rest = own_pieces(low, sec, dp, first)
+        early_cot, late_cot = cot_send[:256], cot_send[256:]
+        own_first, rest, early_cot = fence(own_first, rest, early_cot)
+        z0 = z_parts(own_first)
+        own = own_rest(rest, low, sec, first)
+        early_cot = swap(early_cot)
+        *z0, own[0], early_cot = fence(*z0, own[0], early_cot)
+        quad0 = jnp.stack(z0)
         a0, b0 = ab_parts(quad0)
-        quad1 = jnp.stack(z_parts(own[1]))
-        chunks[0] = core_parts(quad0, a0, b0, over_b(a0))
-        quad1, own[2], *chunks[0] = fence(quad1, own[2], *chunks[0])
+        z1 = z_parts(own[0])
+        quad0, a0, b0, *z1 = fence(quad0, a0, b0, *z1)
+        ab0 = over_b(a0)
+        core0 = [over_core(v) for v in (quad0, b0, a0)]
+        quad1 = jnp.stack(z1)
+        quad1, ab0, frames, *core0 = fence(quad1, ab0, frames, *core0)
         a1, b1 = ab_parts(quad1)
-        quad2 = jnp.stack(z_parts(own[2]))
+        chunks[0] = [quad0, b0, a0, ab0] + core0 + [over_core(ab0)]
+        *chunks[0], own[1] = fence(*chunks[0], own[1])
+        z2 = z_parts(own[1])
+    else:
+        chunks = gather_plain(low)
+        early_cot, late_cot = swap(cot_send[:256]), swap(cot_send[256:])
     ka = kernel_stem_feed(ids, chunks[0], frames)
     prm = ka.prm
     if fast:
-        ka.x1, quad1, a1, b1, quad2, own[3] = fence(ka.x1, quad1, a1, b1, quad2, own[3])
-        chunks[1] = core_parts(quad1, a1, b1, over_b(a1))
-        ka.x1, *chunks[1] = fence(ka.x1, *chunks[1])
+        ka.x1, quad1, a1, b1, *z2 = fence(ka.x1, quad1, a1, b1, *z2)
+        ab1 = over_b(a1)
+        core1 = [over_core(v) for v in (quad1, b1, a1)]
+        quad2 = jnp.stack(z2)
+        ab1, quad2, *core1 = fence(ab1, quad2, *core1)
         a2, b2 = ab_parts(quad2)
-        quad3 = jnp.stack(z_parts(own[3]))
+        chunks[1] = [quad1, b1, a1, ab1] + core1 + [over_core(ab1)]
+        *chunks[1], own[2] = fence(*chunks[1], own[2])
+        z3 = z_parts(own[2])
     kb = kernel_rest_first(ids, chunks[1], prm, ka.x1)
     if fast:
-        kb.sent, quad2, a2, b2, quad3 = fence(kb.sent, quad2, a2, b2, quad3)
-        chunks[2] = core_parts(quad2, a2, b2, over_b(a2))
-        kb.sent, *chunks[2] = fence(kb.sent, *chunks[2])
+        kb.sent, quad2, a2, b2, *z3 = fence(kb.sent, quad2, a2, b2, *z3)
+        ab2 = over_b(a2)
+        core2 = [over_core(v) for v in (quad2, b2, a2)]
+        quad3 = jnp.stack(z3)
+        ab2, quad3, late_cot, *core2 = fence(ab2, quad3, late_cot, *core2)
         a3, b3 = ab_parts(quad3)
+        late_cot = swap(late_cot)
+        chunks[2] = [quad2, b2, a2, ab2] + core2 + [over_core(ab2)]
+        chunks[2] = list(fence(*chunks[2]))
     kc = kernel_first_second(ids, chunks[2], prm, kb.sent)
     if fast:
-        kc.x3, quad3, a3, b3 = fence(kc.x3, quad3, a3, b3)
-        chunks[3] = core_parts(quad3, a3, b3, over_b(a3))
-    kd = kernel_turn(ids, chunks[3], chunks[2], prm, kc.x3, cot_second, allowed, kc.x2, kc.gated, kc.deep)
-    to_send = jnp.where(first, kd.sent, kb.sent)
-    own_sent = jnp.where(first, kb.sent, kd.sent)
-    other_sent = swap(to_send)
+        kc.x3, quad3, a3, b3, late_cot = fence(kc.x3, quad3, a3, b3, late_cot)
+        chunks[3] = [quad3, b3, a3] + [over_b(a3)]
+        chunks[3] += [over_core(v) for v in chunks[3]]
+    cot_other = [early_cot, late_cot]
+    kd = kernel_turn(ids, chunks[3], prm, kc.x3, cots, cot_other, allowed)
+    other_sent = swap(jnp.where(first, kd.sent, kb.sent))
+    came = [None] * 6
+    near, far, parts = [None] * 6, [None] * 6, [None] * 6
+
+    def begin(n, kernel):
+        near[n], far[n] = halves(kernel.keep, over_core(kernel.send))
+        came[n] = over_a(far[n])
+
+    def go_on(n):
+        near[n], far[n] = halves(near[n], came[n])
+        came[n] = over_b(far[n])
+
+    def gather_parts(n):
+        parts[n] = quarters(near[n], came[n])
+
     if fast:
-        came0 = over_core(kd.send)
-    ke = kernel_back_early(
-        1, ids, chunks[2], FEED // 2, chunks[2], 0, prm, kd.dx2, kc.x1, kc.qkv, kc.ls, kc.mixed,
-        kb.sent, kc.hid, None,
-    )
-    ig_second = ke.ig.astype(BF)
+        begin(0, kd)
+    ke = kernel_mid(1, ids, chunks[2], FEED // 2, prm, kd.dx3, kc.x2, kc.gated, kc.deep, kc.x1, kc.qkv, kc.ls, kc.mixed)
     if fast:
-        other_sent, came0, ke.send, ig_second = fence(other_sent, came0, ke.send, ig_second)
-        near0, far0 = halves(kd.keep, came0)
-        came0 = over_a(far0)
-        came1 = over_core(ke.send)
-    kf = kernel_back_late(
-        ids, chunks[1], chunks[1], chunks[3], prm, kb.x4, kb.sent, cot_first, allowed, ig_second,
-        kb.x3, kb.hid, kb.x2, kb.gated, kb.deep, kd.ghead,
-    )
+        came[0], other_sent, ke.send, ke.dx1 = fence(came[0], other_sent, ke.send, ke.dx1)
+        go_on(0)
+        begin(1, ke)
+    kf = kernel_early(1, ids, chunks[2], 0, prm, ke.dx1, kb.sent, kc.hid, None)
     if fast:
-        came0, came1, kf.send, kf.dx2 = fence(came0, came1, kf.send, kf.dx2)
-        near0, far0 = halves(near0, came0)
-        near1, far1 = halves(ke.keep, came1)
-        came0 = over_b(far0)
-        came1 = over_a(far1)
-        came2 = over_core(kf.send)
-    stem = dict(
-        pre=ka.pre,
-        wout=ka.wout,
-        frames=frames,
-        small_first=kf.small,
-        small_second=kd.small + ke.small,
-    )
-    kg = kernel_back_early(
-        0, ids, chunks[1], 0, chunks[0], FLAT, prm, kf.dx2, ka.x1, kb.qkv, kb.ls, kb.mixed, ka.x0,
-        ka.hid, stem,
+        came[0], came[1], kf.send, kf.ig = fence(came[0], came[1], kf.send, kf.ig)
+        gather_parts(0)
+        go_on(1)
+        begin(2, kf)
+    kg = kernel_late(
+        ids, chunks[1], chunks[3], prm, kb.x4, kb.sent, cots, cot_other, allowed, kf.ig, kb.x3, kb.hid, kd.ghead
     )
     if fast:
-        came0, came1, came2, kg.send = fence(came0, came1, came2, kg.send)
-        near2, far2 = halves(kf.keep, came2)
-        near1, far1 = halves(near1, came1)
-        came3 = over_core(kg.send)
-        came2 = over_a(far2)
-        came1 = over_b(far1)
-        sum0 = z_sum(quarters(near0, came0))
-        near3, far3 = halves(kg.keep, came3)
-        near2, far2 = halves(near2, came2)
-        came3 = over_a(far3)
-        came2 = over_b(far2)
-        sum1 = z_sum(quarters(near1, came1))
-        sum2 = z_sum(quarters(near2, came2))
-        near3, far3 = halves(near3, came3)
-        came3 = over_b(far3)
-        sum3 = z_sum(quarters(near3, came3))
-    other_grad = swap(jnp.where(first, ke.ig, kg.ig).astype(BF)).astype(F32)
-    own_grad = jnp.where(first, kg.ig, ke.ig)
-    input_grads = jnp.stack(pick(first, own_grad, other_grad))[None, :, None]
-    ko = kernel_outputs_of(fast, ids, sec, chunks[3], own_sent, other_sent, allowed_both, lengths)
+        came[1], came[2], kg.send, kg.dx3 = fence(came[1], came[2], kg.send, kg.dx3)
+        gather_parts(1)
+        go_on(2)
+        begin(3, kg)
+        sums_a = z_sum([jnp.concatenate([p, q]) for p, q in zip(parts[0], parts[1])])
+    kh = kernel_mid(0, ids, chunks[1], 0, prm, kg.dx3, kb.x2, kb.gated, kb.deep, ka.x1, kb.qkv, kb.ls, kb.mixed)
+    if fast:
+        came[2], came[3], sums_a, kh.send, kh.dx1 = fence(came[2], came[3], sums_a, kh.send, kh.dx1)
+        gather_parts(2)
+        go_on(3)
+        begin(4, kh)
+        sum_2 = z_sum(parts[2])
+    stem = (ka.pre, ka.wout, frames, [kg.small, kh.small, kd.small, ke.small, kf.small])
+    ki = kernel_early(0, ids, chunks[0], FLAT, prm, kh.dx1, ka.x0, ka.hid, stem)
+    if fast:
+        came[3], came[4], sum_2, ki.send, ki.ig, other_sent = fence(came[3], came[4], sum_2, ki.send, ki.ig, other_sent)
+        gather_parts(3)
+        go_on(4)
+        begin(5, ki)
+        sum_3 = z_sum(parts[3])
+    ko = kernel_outputs(ids, chunks[3], kb.sent, kd.sent, other_sent, allowed_both, lengths[:, 0])
+    if fast:
+        came[4], came[5], sum_3, ki.ig, ko.acts, ko.logp = fence(came[4], came[5], sum_3, ki.ig, ko.acts, ko.logp)
+        gather_parts(4)
+        go_on(5)
+        sum_4 = z_sum(parts[4])
+        came[5], sum_4, ki.ig = fence(came[5], sum_4, ki.ig)
+        gather_parts(5)
+        shards = own_shards(sums_a, sum_2, sum_3, sum_4, z_sum(parts[5]), dp, first)
+    else:
+        shards = reduce_plain([(k.keep, k.send) for k in (kd, ke, kf, kg, kh, ki)])
+    other_grad = swap(jnp.where(first, kf.ig, ki.ig).astype(BF))
+    input_grads = kernel_grads(ids, ki.ig, kf.ig, other_grad)[None, :, None]
     activations = ko.acts[None, :, None]
     log_probs = ko.logp[None, :, None]
-    if fast:
-        shards = own_shards(sum0, sum1, sum2, sum3, dp, first)
-    else:
-        shards = reduce_plain([(k.keep, k.send) for k in (kd, ke, kf, kg)])
     return (activations, log_probs, input_grads, *shards)
 
 
-def kernel_outputs_of(fast, ids, sec, head_bufs, own, other, allowed, lengths):
-    if not fast:
-        mine, theirs = own, other
-        flip = sec == 1
-        own, other = jnp.where(flip, theirs, mine), jnp.where(flip, mine, theirs)
-    return kernel_outputs(ids, head_bufs, own, other, allowed, lengths[:, 0])
+def own_half(both, sec, first):
+    mine = lax.dynamic_index_in_dim(both, sec, 0, keepdims=False)
+    theirs = over_x(lax.dynamic_index_in_dim(both, 1 - sec, 0, keepdims=False))
+    return pick(first, mine, theirs)
 
 
 def own_pieces(low, sec, dp, first):
-    feed_in, feed_out, attend_in, attend_out, conv_in, depth, conv_out, gains, stem_in, stem_out, head = low
-    feeds = [pack_feed(feed_in[0, j], feed_out[0, j]).reshape(2, FEED // 2, 512) for j in range(2)]
+    feed_in, feed_out = low[:2]
+    stem = pack_stem(low[8], low[9], low[5][0], low[7][0], dp % 4)
+    feed_first, feed_second = own_half(pack_feed(feed_in[0, 0], feed_out[0, 0]).reshape(2, FEED // 2, 512), sec, first)
+    return jnp.concatenate([stem, feed_first]), feed_second
+
+
+def own_rest(feed_second, low, sec, first):
+    feed_in, feed_out, attend_in, attend_out, conv_in, _, conv_out = low[:7]
+    feed = pack_feed(feed_in[0, 1], feed_out[0, 1]).reshape(2, FEED // 2, 512)
     attn = pack_attn(attend_in[0], attend_out[0]).reshape(2, ATTN // 2, 512)
     conv = pack_conv(conv_in[0], conv_out[0]).reshape(2, CONV // 2, 512)
-    stem = pack_stem(stem_in, stem_out, depth[0], gains[0], dp % 4)
-
-    def spread(both):
-        mine = lax.dynamic_index_in_dim(both, sec, 0, keepdims=False)
-        theirs = over_x(lax.dynamic_index_in_dim(both, 1 - sec, 0, keepdims=False))
-        return pick(first, mine, theirs)
-
-    feed_first, feed_second = spread(feeds[0])
-    rest_first, rest_second = spread(jnp.concatenate([attn, conv, feeds[1]], axis=1))
-    edge = ATTN // 2 + CONV // 2
+    rest_first, rest_second = own_half(jnp.concatenate([attn, conv, feed], axis=1), sec, first)
     return [
-        jnp.concatenate([stem, feed_first]),
         rest_first,
-        jnp.concatenate([feed_second, rest_second[:edge]]),
-        jnp.concatenate([rest_second[edge:], head.T]),
+        jnp.concatenate([feed_second, rest_second[:LATE_ROWS]]),
+        jnp.concatenate([rest_second[LATE_ROWS:], low[10].T]),
     ]
 
 
-def own_shards(second_late, second_early, first_late, first_early, dp, first):
-    edge, early = FEED // 2 + CONV // 2, ATTN // 2 + FEED // 2
+def own_shards(sums_a, sum_2, sum_3, sum_4, sum_5, dp, first):
+    half = FEED // 2
+    head, early_first, stem = sum_3[half:], sum_5[:half], sum_5[half:]
 
     def join(of_first, of_second):
         own = jnp.where(first, of_first, of_second)
         other = over_x(jnp.where(first, of_second, of_first).astype(BF)).astype(F32)
         return jnp.stack(pick(first, own, other))
 
-    late = join(first_late[:edge], second_late)
-    earlier = join(first_early[:early], second_early)
-    half = lambda part, begin, rows: part[:, begin : begin + rows].reshape(2 * rows, 512)
-    feeds = [half(earlier, ATTN // 2, FEED // 2), half(late, 0, FEED // 2)]
-    attn = half(earlier, 0, ATTN // 2)
-    conv = half(late, FEED // 2, CONV // 2)
-    head = first_late[edge:]
-    g_stem_in, g_stem_out, g_depth, g_gains = unpack_stem(first_early[early:], dp % 4)
+    rest = join(jnp.concatenate([sum_3[:half], sum_4]), sums_a)
+    late, rest = rest[:, :half].reshape(FEED, 512), rest[:, half:]
+    early = join(early_first, sum_2).reshape(FEED, 512)
+    attn = rest[:, : ATTN // 2].reshape(ATTN, 512)
+    conv = rest[:, ATTN // 2 : LATE_ROWS].reshape(CONV, 512)
+    feeds = [early, late]
+    g_stem_in, g_stem_out, g_depth, g_gains = unpack_stem(stem, dp % 4)
     return (
         jnp.stack([unpack_in(f, 4) for f in feeds])[None],
         jnp.stack([f[128:] for f in feeds])[None],
@@ -1185,14 +1267,14 @@
     for keep, send in grads:
         both = jnp.concatenate([keep, send])
         chunks.append(jnp.stack([both[q] for q in place]).astype(F32))
-    edge, early = FEED // 2 + CONV // 2, ATTN // 2 + FEED // 2
+    half = FEED // 2
     whole = []
-    for late, earlier in ((chunks[2], chunks[3]), (chunks[0], chunks[1])):
+    for late, mid, early in (chunks[3:], chunks[:3]):
         glue = lambda part, begin, rows: (
             part[:, begin : begin + rows].reshape(2, 16, rows, 512).transpose(1, 0, 2, 3).reshape(16, 2 * rows, 512)
         )
-        feeds = [glue(earlier, ATTN // 2, FEED // 2), glue(late, 0, FEED // 2)]
-        attn, conv = glue(earlier, 0, ATTN // 2), glue(late, FEED // 2, CONV // 2)
+        feeds = [glue(early, 0, half), glue(late, 0, half)]
+        attn, conv = glue(mid, 0, ATTN // 2), glue(mid, ATTN // 2, CONV // 2)
         spread = lambda w, n: jax.vmap(lambda rows: unpack_in(rows, n))(w).reshape(512, 512 * n)
         whole.append(
             (
@@ -1204,8 +1286,8 @@
                 conv[:, 64:].reshape(512, 512),
             )
         )
-    head = chunks[2][:, edge:].reshape(1024, 512).T
-    g_stem_in, g_stem_out, g_depth, g_gains = jax.vmap(unpack_stem)(chunks[3][:, early:], jnp.arange(32) % 4)
+    head = chunks[3][:, half:].reshape(1024, 512).T
+    g_stem_in, g_stem_out, g_depth, g_gains = jax.vmap(unpack_stem)(chunks[5][:, half:], jnp.arange(32) % 4)
     g_stem_in = jnp.moveaxis(g_stem_in, 0, 1).reshape(640, 256)
     g_stem_out = g_stem_out.reshape(256, 512)
     lanes = lambda w: jnp.moveaxis(w.reshape(2, 16, w.shape[1], 32), 1, 2).reshape(2, w.shape[1], 512)

time: 493 us -> 417 us (0.85)
  waiting for transfers between devices: 195 us -> 118 us
  other arithmetic: 44.3 us -> 27.3 us
  Pallas kernels: 141 us -> 157 us
    ppermute x68 -> x77, waiting for transfers between devices: 180 us -> 109 us  [across(): return lax.ppermute(value, BOTH, permutation(target))]
    convert_element_type x8 -> x9, other arithmetic: 23 us -> 5.84 us  [halves(): add(kept[:cut], came[:cut]).astype(BF)]
    pallas_call x8 -> x11, Pallas kernels: 141 us -> 157 us  [run(): pl.pallas_call(kernel, out_shape=[jax.ShapeDtypeStruct(shape, dtype) for...]
    ppermute x3 -> x4, waiting for transfers between devices: 15.1 us -> 8.12 us  [on_device(): swap = lambda v: lax.ppermute(v, 'section', [(0, 1), (1, 0)])]
    ppermute x68 -> x77, starting transfers between devices: 77.2 us -> 82.2 us  [across(): return lax.ppermute(value, BOTH, permutation(target))]
  transfers between devices with their start and end apart: 71 -> 81, of which waited for: 31 -> 20; matrix products, arithmetic and copies ran while one was open for 9% -> 9% of each run, Pallas kernels for 24% -> 33%
where the time goes in v2:
time: 417 us; the launch traced here: 413 us
  Pallas kernels  157 us (38%)
  waiting for transfers between devices  118 us (28%)
  starting transfers between devices  85.2 us (20%)
  other arithmetic  27.3 us (7%)
  local copies, waits for them, and re-layouts  19.5 us (5%)
  between operations  6.3 us (2%)
    pallas_call x11, Pallas kernels, run(): pl.pallas_call(kernel, out_shape=[jax.ShapeDtypeStruct(shape, dtype) for...  157 us
    ppermute x77, waiting for transfers between devices, across(): return lax.ppermute(value, BOTH, permutation(target))  109 us
    ppermute x77, starting transfers between devices, across(): return lax.ppermute(value, BOTH, permutation(target))  82.2 us
  transfers between devices with their start and end apart: 81, of which 20 were waited for; matrix products, arithmetic and copies ran while one was open for 9% of the time, Pallas kernels for 33%

profile of v2, /device:TPU:0, one launch (start us, length us, event | category | flops | bytes accessed | tf_op | source)
XLA Modules:
  0.0 413.2 jit_solution(7362702266529048161)
XLA Ops:
  4.1 2.9 collective-permute-start
  16.4 2.6 collective-permute-start.2
  19.0 11.8 %collective-permute-done.4 = bf16[240,512]{1,0:T(8,128)(2,1)S(1)} collective-permute-done((bf16[240,512]{1,0:T(8,128)(2,1)S(1)}, bf16[240,512]{1,0:T(8,128)(2,1)S(1)}, u32[]{:S(2)}, u32[]{:S(2)}) %collective-permute-start.4) | collective-permute-done | bytes 245792 | tf_op jit(solution)/shard_map/ppermute | solution.py:954
  40.0 4.5 %collective-permute-done.8 = bf16[240,512]{1,0:T(8,128)(2,1)S(1)} collective-permute-done((bf16[240,512]{1,0:T(8,128)(2,1)S(1)}, bf16[240,512]{1,0:T(8,128)(2,1)S(1)}, u32[]{:S(2)}, u32[]{:S(2)}) %collective-permute-start.8) | collective-permute-done | bytes 245792 | tf_op jit(solution)/shard_map/ppermute | solution.py:954
  44.5 12.3 %collective-permute-done.9 = bf16[240,512]{1,0:T(8,128)(2,1)S(1)} collective-permute-done((bf16[240,512]{1,0:T(8,128)(2,1)S(1)}, bf16[240,512]{1,0:T(8,128)(2,1)S(1)}, u32[]{:S(2)}, u32[]{:S(2)}) %collective-permute-start.9) | collective-permute-done | bytes 245792 | tf_op jit(solution)/shard_map/ppermute | solution.py:954
  60.9 6.8 %collective-permute-done.11.refs_4_ = bf16[4,160,512]{2,1,0:T(8,128)(2,1)} collective-permute-done((bf16[4,160,512]{2,1,0:T(8,128)(2,1)}, bf16[4,160,512]{2,1,0:T(8,128)(2,1)}, u32[]{:S(2)}, u32[]{:S(2)}) %collective-permute-start.11) | collective-permute-done | bytes 655392 | tf_op jit(solution)/shard_map/ppermute | solution.py:954
  70.9 3.3 collective-permute-start.18
  76.7 9.4 %stem_feed.1 = (f32[2,16,512]{2,1,0:T(8,128)}, f32[512,256]{1,0:T(8,128)}, bf16[256,512]{1,0:T(8,128)(2,1)}, bf16[512,512]{1,0:T(8,128)(2,1)}, bf16[512,2048]{1,0:T(8,128)(2,1)}, /*index=5*/f32[512,512]{1,0:T(8,128)}) custom-call(s32[6]{0:T(128)} %stack.102.refs_0_, bf16[4,160,512]{2,1,0:T(8,128)(2,1)} %pad_maximum_fusion.2.refs_1_, ...), custom_call_target="tpu_custom_call" | custom-call | flops 9900000256 | bytes 1048576 | tf_op jit(solution)/shard_map/stem_feed/pallas_call | solution.py:461
  86.1 8.4 %collective-permute-done.19 = bf16[240,512]{1,0:T(8,128)(2,1)S(1)} collective-permute-done((bf16[240,512]{1,0:T(8,128)(2,1)S(1)}, bf16[240,512]{1,0:T(8,128)(2,1)S(1)}, u32[]{:S(2)}, u32[]{:S(2)}) %collective-permute-start.19) | collective-permute-done | bytes 245792 | tf_op jit(solution)/shard_map/ppermute | solution.py:954
  96.7 11.9 %collective-permute-done.21.refs_4_ = bf16[4,240,512]{2,1,0:T(8,128)(2,1)S(1)} collective-permute-done((bf16[4,240,512]{2,1,0:T(8,128)(2,1)S(1)}, bf16[4,240,512]{2,1,0:T(8,128)(2,1)S(1)}, u32[]{:S(2)}, u32[]{:S(2)}) %collective-permute-start.21) | collective-permute-done | bytes 983072 | tf_op jit(solution)/shard_map/ppermute | solution.py:954
  111.9 4.5 %collective-permute-start.28 = (bf16[160,512]{1,0:T(8,128)(2,1)S(1)}, bf16[160,512]{1,0:T(8,128)(2,1)S(1)}, u32[]{:S(2)}, u32[]{:S(2)}) collective-permute-start(bf16[160,512]{1,0:T(8,128)(2,1)S(1)} %pad_maximum_fusion.14), channel_id=1, source_target_pairs={{0,4},{1,5},{2,6},{3,7},{4,0},{5,1},{6,2},{7,3},{8,12},{9,13},{10,... | collective-permute-start | bytes 491528 | tf_op jit(solution)/shard_map/ppermute | solution.py:954
  119.0 16.4 %rest_first.1 = (bf16[512,1536]{1,0:T(8,128)(2,1)}, f32[8,512]{1,0:T(8,128)}, bf16[512,512]{1,0:T(8,128)(2,1)}, f32[512,512]{1,0:T(8,128)}, f32[512,1024]{1,0:T(...) custom-call(s32[6]{0:T(128)} %stack.102.refs_0_, ...), custom_call_target="tpu_custom_call" | custom-call | flops 22000001024 | bytes 1048576 | tf_op jit(solution)/shard_map/rest_first/pallas_call | solution.py:461
  137.1 12.5 %collective-permute-done.31.refs_4_ = bf16[4,240,512]{2,1,0:T(8,128)(2,1)S(1)} collective-permute-done((bf16[4,240,512]{2,1,0:T(8,128)(2,1)S(1)}, bf16[4,240,512]{2,1,0:T(8,128)(2,1)S(1)}, u32[]{:S(2)}, u32[]{:S(2)}) %collective-permute-start.31) | collective-permute-done | bytes 983072 | tf_op jit(solution)/shard_map/ppermute | solution.py:954
  153.8 16.6 %first_second.1 = (bf16[512,2048]{1,0:T(8,128)(2,1)}, f32[512,512]{1,0:T(8,128)}, bf16[512,1536]{1,0:T(8,128)(2,1)}, f32[8,512]{1,0:T(8,128)}, bf16[512,512]{1,0...) custom-call(s32[6]{0:T(128)} %stack.102.refs_0_, ...), custom_call_target="tpu_custom_call" | custom-call | flops 22000001024 | bytes 1048576 | tf_op jit(solution)/shard_map/first_second/pallas_call | solution.py:461
  170.5 8.1 %collective-permute-done.38.refs_13_.refs_22_ = bf16[256,1024]{1,0:T(8,128)(2,1)S(1)} collective-permute-done((bf16[256,1024]{1,0:T(8,128)(2,1)S(1)}, bf16[256,1024]{1,0:T(8,128)(2,1)S(1)}, u32[]{:S(2)}, u32[]{:S(2)}) %collective-permute-start.38) | collective-permute-done | bytes 524320 | tf_op jit(solution)/shard_map/ppermute | solution.py:1024
  180.0 9.3 %collective-permute-done.39.refs_4_.refs_12_.refs_5_ = bf16[4,160,512]{2,1,0:T(8,128)(2,1)S(1)} collective-permute-done((bf16[4,160,512]{2,1,0:T(8,128)(2,1)S(1)}, bf16[4,160,512]{2,1,0:T(8,128)(2,1)S(1)}, u32[]{:S(2)}, u32[]{:S(2)}) %collective-permute-start.39) | collective-permute-done | bytes 655392 | tf_op jit(solution)/shard_map/ppermute | solution.py:954
  196.1 18.9 %turn.1 = (bf16[512,512]{1,0:T(8,128)(2,1)}, f32[1024,512]{1,0:T(8,128)}, f32[512,512]{1,0:T(8,128)}, f32[16,512]{1,0:T(8,128)}, bf16[16,128,512]{2,1,0:T(8,128)(2,1)}, /*index=5*/bf16[16,128,512]{2,1,0:T(8,128)(2,1)}) custom-call(s32[6]{0:T(128)} %stack.102.refs_0_, bf16[4,160,512]{2,1,0:T(8,128)(2,1)} %copy-done.11, ...), custom_call_target="tpu_custom_call" | custom-call | flops 24199999488 | bytes 1048576 | tf_op jit(solution)/shard_map/turn/pallas_call | solution.py:461
  216.7 2.8 collective-permute-done.44
  222.1 21.2 %mid.2 = (f32[512,512]{1,0:T(8,128)}, f32[16,512]{1,0:T(8,128)}, bf16[16,112,512]{2,1,0:T(8,128)(2,1)}, bf16[16,112,512]{2,1,0:T(8,128)(2,1)}) custom-call(s32[6]{0:T(128)} %stack.102.refs_0_, bf16[4,240,512]{2,1,0:T(8,128)(2,1)} %copy-done.10, bf16[4,240,512]{2,1,0:T(8,128)(2,1)} %collective-permute-done.27.refs_2_, bf16[4,240,512]{2,1,0:T(8,128)(2,1)} %copy-done.35, ...), custom_call_target="tpu_custom_call" | custom-call | flops 23100000256 | bytes 1048576 | tf_op jit(solution)/shard_map/mid/pallas_call | solution.py:461
  249.8 12.5 %early.2 = (f32[512,512]{1,0:T(8,128)}, f32[16,512]{1,0:T(8,128)}, bf16[16,128,512]{2,1,0:T(8,128)(2,1)}, bf16[16,128,512]{2,1,0:T(8,128)(2,1)}) custom-call(s32[6]{0:T(128)} %stack.102.refs_0_, bf16[4,240,512]{2,1,0:T(8,128)(2,1)} %copy-done.10, bf16[4,240,512]{2,1,0:T(8,128)(2,1)} %collective-permute-done.27.refs_2_, bf16[4,240,512]{2,1,0:T(8,128)(2,1)} %copy-done.35, ...), custom_call_target="tpu_custom_call" | custom-call | flops 11000000512 | bytes 1048576 | tf_op jit(solution)/shard_map/early/pallas_call | solution.py:461
  269.9 16.2 %late.1 = (f32[512,512]{1,0:T(8,128)}, f32[16,512]{1,0:T(8,128)}, bf16[16,160,512]{2,1,0:T(8,128)(2,1)}, bf16[16,160,512]{2,1,0:T(8,128)(2,1)}) custom-call(s32[6]{0:T(128)} %stack.102.refs_0_, bf16[4,240,512]{2,1,0:T(8,128)(2,1)} %copy-done.9, bf16[4,240,512]{2,1,0:T(8,128)(2,1)} %collective-permute-done.17.refs_2_, bf16[4,240,512]{2,1,0:T(8,128)(2,1)} %copy-done.29, ...), custom_call_target="tpu_custom_call" | custom-call | flops 18699999232 | bytes 1048576 | tf_op jit(solution)/shard_map/late/pallas_call | solution.py:461
  296.1 21.3 %mid.3 = (f32[512,512]{1,0:T(8,128)}, f32[16,512]{1,0:T(8,128)}, bf16[16,112,512]{2,1,0:T(8,128)(2,1)}, bf16[16,112,512]{2,1,0:T(8,128)(2,1)}) custom-call(s32[6]{0:T(128)} %stack.102.refs_0_, bf16[4,240,512]{2,1,0:T(8,128)(2,1)} %copy-done.9, bf16[4,240,512]{2,1,0:T(8,128)(2,1)} %collective-permute-done.17.refs_2_, bf16[4,240,512]{2,1,0:T(8,128)(2,1)} %copy-done.29, ...), custom_call_target="tpu_custom_call" | custom-call | flops 23100000256 | bytes 1048576 | tf_op jit(solution)/shard_map/mid/pallas_call | solution.py:461
  327.1 13.1 %early.3 = (f32[512,512]{1,0:T(8,128)}, f32[16,512]{1,0:T(8,128)}, bf16[16,160,512]{2,1,0:T(8,128)(2,1)}, bf16[16,160,512]{2,1,0:T(8,128)(2,1)}) custom-call(s32[6]{0:T(128)} %stack.102.refs_0_, bf16[4,160,512]{2,1,0:T(8,128)(2,1)} %pad_maximum_fusion.2.refs_1_, bf16[4,160,512]{2,1,0:T(8,128)(2,1)} %collective-permute-done.7.refs_2_, ...), custom_call_target="tpu_custom_call" | custom-call | flops 14300000256 | bytes 1048576 | tf_op jit(solution)/shard_map/early/pallas_call | solution.py:461
  343.2 3.6 collective-permute-done.66
  353.5 8.3 %outputs.1 = (f32[2,512,1024]{2,1,0:T(8,128)}, f32[2,512,512]{2,1,0:T(8,128)}) custom-call(s32[6]{0:T(128)} %stack.102.refs_0_, s32[2]{0:T(128)} %bitcast.226, bf16[4,160,512]{2,1,0:T(8,128)(2,1)} %copy-done.11, bf16[4,160,512]{2,1,0:T(8,128)(2,1)} %collective-permute-done.37.refs_2_.refs_10_.refs_3_, bf16[4,160,512]{2,1,0:T(8,128)(2,1)} %copy-done.41, ...), custom_call_target="tpu_custom_call" | custom-call | flops 9900000256 | bytes 1048576 | tf_op jit(solution)/shard_map/outputs/pallas_call | solution.py:461
  361.8 4.3 %collective-permute-done.69 = bf16[160,512]{1,0:T(8,128)(2,1)S(1)} collective-permute-done((bf16[160,512]{1,0:T(8,128)(2,1)}, bf16[160,512]{1,0:T(8,128)(2,1)S(1)}, u32[]{:S(2)}, u32[]{:S(2)}) %collective-permute-start.69) | collective-permute-done | bytes 163872 | tf_op jit(solution)/shard_map/ppermute | solution.py:954
  375.4 2.8 collective-permute-done.74
  378.2 3.5 collective-permute-done.73
  385.6 2.6 collective-permute-start.76
  389.8 3.0 collective-permute-done.78
  392.8 6.2 %collective-permute-done.77 = bf16[160,512]{1,0:T(8,128)(2,1)S(1)} collective-permute-done((bf16[160,512]{1,0:T(8,128)(2,1)S(1)}, bf16[160,512]{1,0:T(8,128)(2,1)S(1)}, u32[]{:S(2)}, u32[]{:S(2)}) %collective-permute-start.77) | collective-permute-done | bytes 163872 | tf_op jit(solution)/shard_map/ppermute | solution.py:954
  409.6 3.3 grads.1
  (357 shorter events, 121.8 us)
Async XLA Ops:
  12.4 18.5 %collective-permute-start.5 = (bf16[256,1024]{1,0:T(8,128)(2,1)S(1)}, bf16[256,1024]{1,0:T(8,128)(2,1)S(1)}, u32[]{:S(2)}, u32[]{:S(2)}) collective-permute-start(bf16[256,1024]{1,0:T(8,128)(2,1)S(1)} %get-tuple-element.179), channel_id=1, source_target_pairs={{0,16},{16,0},{1,17},{17,1},{2,18},{18,2},{3,19},{19,3},{4,20},{20... | collective-permute-start | bytes 1572872 | tf_op jit(solution)/shard_map/ppermute | solution.py:1024
  32.7 24.1 %collective-permute-start.6 = (bf16[4,160,512]{2,1,0:T(8,128)(2,1)}, bf16[4,160,512]{2,1,0:T(8,128)(2,1)}, u32[]{:S(2)}, u32[]{:S(2)}) collective-permute-start(bf16[4,160,512]{2,1,0:T(8,128)(2,1)} %pad_maximum_fusion.2.refs_1_), channel_id=1, source_target_pairs={{0,16},{1,3},{2,18},{3,1},{4,20},{5,7},{6,22},{7,5},{8,24},{9,11},... | collective-permute-start | bytes 1966088 | tf_op jit(solution)/shard_map/ppermute | solution.py:954
  34.1 22.7 %collective-permute-start.7 = (bf16[4,160,512]{2,1,0:T(8,128)(2,1)}, bf16[4,160,512]{2,1,0:T(8,128)(2,1)}, u32[]{:S(2)}, u32[]{:S(2)}) collective-permute-start(bf16[4,160,512]{2,1,0:T(8,128)(2,1)} %pad_maximum_fusion.2.refs_1_), channel_id=1, source_target_pairs={{0,2},{1,17},{2,0},{3,19},{4,6},{5,21},{6,4},{7,23},{8,10},{9,25},... | collective-permute-start | bytes 1966088 | tf_op jit(solution)/shard_map/ppermute | solution.py:954
  37.4 19.4 %collective-permute-start.9 = (bf16[240,512]{1,0:T(8,128)(2,1)S(1)}, bf16[240,512]{1,0:T(8,128)(2,1)S(1)}, u32[]{:S(2)}, u32[]{:S(2)}) collective-permute-start(bf16[240,512]{1,0:T(8,128)(2,1)S(1)} %get-tuple-element.188), channel_id=1, source_target_pairs={{0,8},{1,9},{2,10},{3,11},{4,12},{5,13},{6,14},{7,15},{8,0},{9,1},... | collective-permute-start | bytes 737288 | tf_op jit(solution)/shard_map/ppermute | solution.py:954
  69.8 24.7 %collective-permute-start.16 = (bf16[4,240,512]{2,1,0:T(8,128)(2,1)S(1)}, bf16[4,240,512]{2,1,0:T(8,128)(2,1)S(1)}, u32[]{:S(2)}, u32[]{:S(2)}) collective-permute-start(bf16[4,240,512]{2,1,0:T(8,128)(2,1)S(1)} %pad_maximum_fusion.refs_1_), channel_id=1, source_target_pairs={{0,16},{1,3},{2,18},{3,1},{4,20},{5,7},{6,22},{7,5},{8,24},{9,11},... | collective-permute-start | bytes 2949128 | tf_op jit(solution)/shard_map/ppermute | solution.py:954
  70.4 24.1 %collective-permute-start.17 = (bf16[4,240,512]{2,1,0:T(8,128)(2,1)S(1)}, bf16[4,240,512]{2,1,0:T(8,128)(2,1)}, u32[]{:S(2)}, u32[]{:S(2)}) collective-permute-start(bf16[4,240,512]{2,1,0:T(8,128)(2,1)S(1)} %pad_maximum_fusion.refs_1_), channel_id=1, source_target_pairs={{0,2},{1,17},{2,0},{3,19},{4,6},{5,21},{6,4},{7,23},{8,10},{9,25},... | collective-permute-start | bytes 2949128 | tf_op jit(solution)/shard_map/ppermute | solution.py:954
  74.2 20.3 %collective-permute-start.19 = (bf16[240,512]{1,0:T(8,128)(2,1)S(1)}, bf16[240,512]{1,0:T(8,128)(2,1)S(1)}, u32[]{:S(2)}, u32[]{:S(2)}) collective-permute-start(bf16[240,512]{1,0:T(8,128)(2,1)S(1)} %pad_maximum_fusion.9), channel_id=1, source_target_pairs={{0,8},{1,9},{2,10},{3,11},{4,12},{5,13},{6,14},{7,15},{8,0},{9,1},... | collective-permute-start | bytes 737288 | tf_op jit(solution)/shard_map/ppermute | solution.py:954
  75.3 19.2 %collective-permute-start.20 = (bf16[240,512]{1,0:T(8,128)(2,1)S(1)}, bf16[240,512]{1,0:T(8,128)(2,1)S(1)}, u32[]{:S(2)}, u32[]{:S(2)}) collective-permute-start(bf16[240,512]{1,0:T(8,128)(2,1)S(1)} %pad_maximum_fusion.9), channel_id=1, source_target_pairs={{0,12},{1,13},{2,14},{3,15},{4,8},{5,9},{6,10},{7,11},{8,4},{9,5},... | collective-permute-start | bytes 737288 | tf_op jit(solution)/shard_map/ppermute | solution.py:954
  108.8 26.6 %collective-permute-start.26 = (bf16[4,240,512]{2,1,0:T(8,128)(2,1)S(1)}, bf16[4,240,512]{2,1,0:T(8,128)(2,1)S(1)}, u32[]{:S(2)}, u32[]{:S(2)}) collective-permute-start(bf16[4,240,512]{2,1,0:T(8,128)(2,1)S(1)} %pad_maximum_fusion.1.refs_1_), channel_id=1, source_target_pairs={{0,16},{1,3},{2,18},{3,1},{4,20},{5,7},{6,22},{7,5},{8,24},{9,11},... | collective-permute-start | bytes 2949128 | tf_op jit(solution)/shard_map/ppermute | solution.py:954
  110.4 25.0 %collective-permute-start.27 = (bf16[4,240,512]{2,1,0:T(8,128)(2,1)S(1)}, bf16[4,240,512]{2,1,0:T(8,128)(2,1)}, u32[]{:S(2)}, u32[]{:S(2)}) collective-permute-start(bf16[4,240,512]{2,1,0:T(8,128)(2,1)S(1)} %pad_maximum_fusion.1.refs_1_), channel_id=1, source_target_pairs={{0,2},{1,17},{2,0},{3,19},{4,6},{5,21},{6,4},{7,23},{8,10},{9,25},... | collective-permute-start | bytes 2949128 | tf_op jit(solution)/shard_map/ppermute | solution.py:954
  111.9 23.5 %collective-permute-start.28 = (bf16[160,512]{1,0:T(8,128)(2,1)S(1)}, bf16[160,512]{1,0:T(8,128)(2,1)S(1)}, u32[]{:S(2)}, u32[]{:S(2)}) collective-permute-start(bf16[160,512]{1,0:T(8,128)(2,1)S(1)} %pad_maximum_fusion.14), channel_id=1, source_target_pairs={{0,4},{1,5},{2,6},{3,7},{4,0},{5,1},{6,2},{7,3},{8,12},{9,13},{10,... | collective-permute-start | bytes 491528 | tf_op jit(solution)/shard_map/ppermute | solution.py:954
  116.4 19.1 %collective-permute-start.29 = (bf16[160,512]{1,0:T(8,128)(2,1)S(1)}, bf16[160,512]{1,0:T(8,128)(2,1)S(1)}, u32[]{:S(2)}, u32[]{:S(2)}) collective-permute-start(bf16[160,512]{1,0:T(8,128)(2,1)S(1)} %pad_maximum_fusion.14), channel_id=1, source_target_pairs={{0,8},{1,9},{2,10},{3,11},{4,12},{5,13},{6,14},{7,15},{8,0},{9,1},... | collective-permute-start | bytes 491528 | tf_op jit(solution)/shard_map/ppermute | solution.py:954
  117.5 17.9 %collective-permute-start.30 = (bf16[160,512]{1,0:T(8,128)(2,1)S(1)}, bf16[160,512]{1,0:T(8,128)(2,1)S(1)}, u32[]{:S(2)}, u32[]{:S(2)}) collective-permute-start(bf16[160,512]{1,0:T(8,128)(2,1)S(1)} %pad_maximum_fusion.14), channel_id=1, source_target_pairs={{0,12},{1,13},{2,14},{3,15},{4,8},{5,9},{6,10},{7,11},{8,4},{9,5},... | collective-permute-start | bytes 491528 | tf_op jit(solution)/shard_map/ppermute | solution.py:954
  149.8 28.8 %collective-permute-start.36 = (bf16[4,160,512]{2,1,0:T(8,128)(2,1)S(1)}, bf16[4,160,512]{2,1,0:T(8,128)(2,1)S(1)}, u32[]{:S(2)}, u32[]{:S(2)}) collective-permute-start(bf16[4,160,512]{2,1,0:T(8,128)(2,1)S(1)} %pad_maximum_fusion.3.refs_1_.refs_9_.refs_2_), channel_id=1, source_target_pairs={{0,16},{1,3},{2,18},{3,1},{4,20},{5,7},{6,22},{7,5},{8,24},{9,11},... | collective-permute-start | bytes 1966088 | tf_op jit(solution)/shard_map/ppermute | solution.py:954
  150.8 27.8 %collective-permute-start.37 = (bf16[4,160,512]{2,1,0:T(8,128)(2,1)S(1)}, bf16[4,160,512]{2,1,0:T(8,128)(2,1)}, u32[]{:S(2)}, u32[]{:S(2)}) collective-permute-start(bf16[4,160,512]{2,1,0:T(8,128)(2,1)S(1)} %pad_maximum_fusion.3.refs_1_.refs_9_.refs_2_), channel_id=1, source_target_pairs={{0,2},{1,17},{2,0},{3,19},{4,6},{5,21},{6,4},{7,23},{8,10},{9,25},... | collective-permute-start | bytes 1966088 | tf_op jit(solution)/shard_map/ppermute | solution.py:954
  152.3 26.3 %collective-permute-start.38 = (bf16[256,1024]{1,0:T(8,128)(2,1)S(1)}, bf16[256,1024]{1,0:T(8,128)(2,1)S(1)}, u32[]{:S(2)}, u32[]{:S(2)}) collective-permute-start(bf16[256,1024]{1,0:T(8,128)(2,1)S(1)} %get-tuple-element.255), channel_id=1, source_target_pairs={{0,16},{16,0},{1,17},{17,1},{2,18},{18,2},{3,19},{19,3},{4,20},{20... | collective-permute-start | bytes 1572872 | tf_op jit(solution)/shard_map/ppermute | solution.py:1024
  216.6 26.8 %collective-permute-start.46 = (bf16[512,512]{1,0:T(8,128)(2,1)S(1)}, bf16[512,512]{1,0:T(8,128)(2,1)S(1)}, u32[]{:S(2)}, u32[]{:S(2)}) collective-permute-start(bf16[512,512]{1,0:T(8,128)(2,1)S(1)} %broadcast_select_fusion), channel_id=1, source_target_pairs={{0,16},{16,0},{1,17},{17,1},{2,18},{18,2},{3,19},{19,3},{4,20},{20... | collective-permute-start | bytes 1572872 | tf_op jit(solution)/shard_map/ppermute | solution.py:1024
  221.7 21.7 %collective-permute-start.45 = (bf16[8,128,512]{2,1,0:T(8,128)(2,1)S(1)}, bf16[8,128,512]{2,1,0:T(8,128)(2,1)S(1)}, u32[]{:S(2)}, u32[]{:S(2)}) collective-permute-start(bf16[8,128,512]{2,1,0:T(8,128)(2,1)S(1)} %get-tuple-element.390), channel_id=1, source_target_pairs={{0,16},{1,3},{2,18},{3,1},{4,20},{5,7},{6,22},{7,5},{8,24},{9,11},... | collective-permute-start | bytes 3145736 | tf_op jit(solution)/shard_map/ppermute | solution.py:954
  244.5 17.9 %collective-permute-start.48 = (bf16[4,128,512]{2,1,0:T(8,128)(2,1)S(1)}, bf16[4,128,512]{2,1,0:T(8,128)(2,1)S(1)}, u32[]{:S(2)}, u32[]{:S(2)}) collective-permute-start(bf16[4,128,512]{2,1,0:T(8,128)(2,1)S(1)} %get-tuple-element.403), channel_id=1, source_target_pairs={{0,2},{1,17},{2,0},{3,19},{4,6},{5,21},{6,4},{7,23},{8,10},{9,25},... | collective-permute-start | bytes 1572872 | tf_op jit(solution)/shard_map/ppermute | solution.py:954
  263.7 22.4 %collective-permute-start.50 = (bf16[4,112,512]{2,1,0:T(8,128)(2,1)S(1)}, bf16[4,112,512]{2,1,0:T(8,128)(2,1)S(1)}, u32[]{:S(2)}, u32[]{:S(2)}) collective-permute-start(bf16[4,112,512]{2,1,0:T(8,128)(2,1)S(1)} %get-tuple-element.409), channel_id=1, source_target_pairs={{0,2},{1,17},{2,0},{3,19},{4,6},{5,21},{6,4},{7,23},{8,10},{9,25},... | collective-permute-start | bytes 1376264 | tf_op jit(solution)/shard_map/ppermute | solution.py:954
  268.3 17.9 %collective-permute-start.52 = (bf16[8,128,512]{2,1,0:T(8,128)(2,1)S(1)}, bf16[8,128,512]{2,1,0:T(8,128)(2,1)S(1)}, u32[]{:S(2)}, u32[]{:S(2)}) collective-permute-start(bf16[8,128,512]{2,1,0:T(8,128)(2,1)S(1)} %get-tuple-element.388), channel_id=1, source_target_pairs={{0,16},{1,3},{2,18},{3,1},{4,20},{5,7},{6,22},{7,5},{8,24},{9,11},... | collective-permute-start | bytes 3145736 | tf_op jit(solution)/shard_map/ppermute | solution.py:954
  287.8 29.8 %collective-permute-start.53 = (bf16[4,128,512]{2,1,0:T(8,128)(2,1)}, bf16[4,128,512]{2,1,0:T(8,128)(2,1)}, u32[]{:S(2)}, u32[]{:S(2)}) collective-permute-start(bf16[4,128,512]{2,1,0:T(8,128)(2,1)} %get-tuple-element.401), channel_id=1, source_target_pairs={{0,2},{1,17},{2,0},{3,19},{4,6},{5,21},{6,4},{7,23},{8,10},{9,25},... | collective-permute-start | bytes 1572872 | tf_op jit(solution)/shard_map/ppermute | solution.py:954
  288.4 29.0 %collective-permute-start.58 = (bf16[240,512]{1,0:T(8,128)(2,1)S(1)}, bf16[240,512]{1,0:T(8,128)(2,1)S(1)}, u32[]{:S(2)}, u32[]{:S(2)}) collective-permute-start(bf16[240,512]{1,0:T(8,128)(2,1)S(1)} %pad_maximum_fusion.12), channel_id=1, source_target_pairs={{0,12},{1,13},{2,14},{3,15},{4,8},{5,9},{6,10},{7,11},{8,4},{9,5},... | collective-permute-start | bytes 737288 | tf_op jit(solution)/shard_map/ppermute | solution.py:954
  290.9 26.5 %collective-permute-start.57 = (bf16[240,512]{1,0:T(8,128)(2,1)S(1)}, bf16[240,512]{1,0:T(8,128)(2,1)S(1)}, u32[]{:S(2)}, u32[]{:S(2)}) collective-permute-start(bf16[240,512]{1,0:T(8,128)(2,1)S(1)} %pad_maximum_fusion.11), channel_id=1, source_target_pairs={{0,8},{1,9},{2,10},{3,11},{4,12},{5,13},{6,14},{7,15},{8,0},{9,1},... | collective-permute-start | bytes 737288 | tf_op jit(solution)/shard_map/ppermute | solution.py:954
  293.5 24.0 %collective-permute-start.56 = (bf16[240,512]{1,0:T(8,128)(2,1)}, bf16[240,512]{1,0:T(8,128)(2,1)S(1)}, u32[]{:S(2)}, u32[]{:S(2)}) collective-permute-start(bf16[240,512]{1,0:T(8,128)(2,1)} %pad_maximum_fusion.10), channel_id=1, source_target_pairs={{0,4},{1,5},{2,6},{3,7},{4,0},{5,1},{6,2},{7,3},{8,12},{9,13},{10,... | collective-permute-start | bytes 737288 | tf_op jit(solution)/shard_map/ppermute | solution.py:954
  294.5 23.1 %collective-permute-start.55 = (bf16[8,160,512]{2,1,0:T(8,128)(2,1)S(1)}, bf16[8,160,512]{2,1,0:T(8,128)(2,1)S(1)}, u32[]{:S(2)}, u32[]{:S(2)}) collective-permute-start(bf16[8,160,512]{2,1,0:T(8,128)(2,1)S(1)} %get-tuple-element.387), channel_id=1, source_target_pairs={{0,16},{1,3},{2,18},{3,1},{4,20},{5,7},{6,22},{7,5},{8,24},{9,11},... | collective-permute-start | bytes 3932168 | tf_op jit(solution)/shard_map/ppermute | solution.py:954
  318.1 23.4 %collective-permute-start.60 = (bf16[4,160,512]{2,1,0:T(8,128)(2,1)S(1)}, bf16[4,160,512]{2,1,0:T(8,128)(2,1)S(1)}, u32[]{:S(2)}, u32[]{:S(2)}) collective-permute-start(bf16[4,160,512]{2,1,0:T(8,128)(2,1)S(1)} %get-tuple-element.399), channel_id=1, source_target_pairs={{0,2},{1,17},{2,0},{3,19},{4,6},{5,21},{6,4},{7,23},{8,10},{9,25},... | collective-permute-start | bytes 1966088 | tf_op jit(solution)/shard_map/ppermute | solution.py:954
  320.6 19.7 %collective-permute-start.64 = (bf16[128,512]{1,0:T(8,128)(2,1)}, bf16[128,512]{1,0:T(8,128)(2,1)S(1)}, u32[]{:S(2)}, u32[]{:S(2)}) collective-permute-start(bf16[128,512]{1,0:T(8,128)(2,1)} %get-tuple-element.419), channel_id=1, source_target_pairs={{0,12},{1,13},{2,14},{3,15},{4,8},{5,9},{6,10},{7,11},{8,4},{9,5},... | collective-permute-start | bytes 393224 | tf_op jit(solution)/shard_map/ppermute | solution.py:954
  323.0 17.3 %collective-permute-start.63 = (bf16[128,512]{1,0:T(8,128)(2,1)S(1)}, bf16[128,512]{1,0:T(8,128)(2,1)}, u32[]{:S(2)}, u32[]{:S(2)}) collective-permute-start(bf16[128,512]{1,0:T(8,128)(2,1)S(1)} %get-tuple-element.420), channel_id=1, source_target_pairs={{0,8},{1,9},{2,10},{3,11},{4,12},{5,13},{6,14},{7,15},{8,0},{9,1},... | collective-permute-start | bytes 393224 | tf_op jit(solution)/shard_map/ppermute | solution.py:954
  342.7 24.5 %collective-permute-start.65 = (bf16[4,112,512]{2,1,0:T(8,128)(2,1)}, bf16[4,112,512]{2,1,0:T(8,128)(2,1)}, u32[]{:S(2)}, u32[]{:S(2)}) collective-permute-start(bf16[4,112,512]{2,1,0:T(8,128)(2,1)} %get-tuple-element.407), channel_id=1, source_target_pairs={{0,2},{1,17},{2,0},{3,19},{4,6},{5,21},{6,4},{7,23},{8,10},{9,25},... | collective-permute-start | bytes 1376264 | tf_op jit(solution)/shard_map/ppermute | solution.py:954
  347.6 19.6 %collective-permute-start.67 = (bf16[8,160,512]{2,1,0:T(8,128)(2,1)S(1)}, bf16[8,160,512]{2,1,0:T(8,128)(2,1)S(1)}, u32[]{:S(2)}, u32[]{:S(2)}) collective-permute-start(bf16[8,160,512]{2,1,0:T(8,128)(2,1)S(1)} %get-tuple-element.385), channel_id=1, source_target_pairs={{0,16},{1,3},{2,18},{3,1},{4,20},{5,7},{6,22},{7,5},{8,24},{9,11},... | collective-permute-start | bytes 3932168 | tf_op jit(solution)/shard_map/ppermute | solution.py:954
  383.0 25.8 %collective-permute-start.75 = (bf16[512,512]{1,0:T(8,128)(2,1)S(1)}, bf16[512,512]{1,0:T(8,128)(2,1)S(1)}, u32[]{:S(2)}, u32[]{:S(2)}) collective-permute-start(bf16[512,512]{1,0:T(8,128)(2,1)S(1)} %select_convert_fusion), channel_id=1, source_target_pairs={{0,16},{16,0},{1,17},{17,1},{2,18},{18,2},{3,19},{19,3},{4,20},{20... | collective-permute-start | bytes 1572872 | tf_op jit(solution)/shard_map/ppermute | solution.py:1024
  (98 other events, 1100.9 us)

commit v3 on v2

--- a/solution.py
+++ b/solution.py
@@ -76,7 +76,11 @@
 def start_load(ids, bufs, row, rows, scr, sem, flat=False):
     for cr, a, b, zk in pieces():
         px, d = piece_of(ids, cr, a, b, zk)
-        src = bufs[cr * 4 + a * 2 + b].at[zk, row : row + rows]
+        if len(bufs) == 4:
+            begin = row + a * (bufs[0].shape[1] // 2)
+            src = bufs[cr * 2 + b].at[zk, begin : begin + rows]
+        else:
+            src = bufs[cr * 4 + a * 2 + b].at[zk, row : row + rows]
         if flat:
             dst = scr.at[px * 16 + d]
         else:
@@ -300,9 +304,8 @@
 
 
 def conv_bwd(dx, x, gated, deep, w, prm, length, out, gw, small, s):
-    for pad in (s.pad, s.back):
-        pad[0:PAD, :] = jnp.zeros((PAD, 512), F32)
-        pad[PAD + 512 : 2 * PAD + 512, :] = jnp.zeros((PAD, 512), F32)
+    s.back[0:PAD, :] = jnp.zeros((PAD, 512), F32)
+    s.back[PAD + 512 : 2 * PAD + 512, :] = jnp.zeros((PAD, 512), F32)
     gain_in = prm[TAPS + 2 : TAPS + 3, :]
     gain_mid = prm[TAPS + 3 : TAPS + 4, :]
 
@@ -318,7 +321,7 @@
         ddeep, gg = unit_back(dmid, u3, r3, gain_mid)
         s.back[padded, :] = ddeep
         small[TAPS + 3 : TAPS + 4, :] += gg
-        s.pad[padded, :] = (
+        s.glu[rs, :] = (
             gated[rs, 0:512] * sigmoid(gated[rs, 512:1024]) * row_mask(length, start, RB, 512)
         )
 
@@ -326,13 +329,13 @@
     gw[:, 64:96, :] = dotl(s.act[...], s.d[...]).astype(BF).reshape(16, 32, 512)
     for i in range(512 // RB):
         rows = slice(i * RB, i * RB + RB)
-        ddeep = s.back[PAD + i * RB : PAD + i * RB + RB, :]
+        glu = s.glu[rows, :]
         dglu = jnp.zeros((RB, 512), F32)
         for t in range(TAPS):
-            begin = i * RB + PAD - TAPS // 2 + t
-            small[t : t + 1, :] += jnp.sum(ddeep * s.pad[begin : begin + RB, :], axis=0, keepdims=True)
             begin = i * RB + PAD + TAPS // 2 - t
-            dglu = dglu + prm[t : t + 1, :] * s.back[begin : begin + RB, :]
+            later = s.back[begin : begin + RB, :]
+            small[t : t + 1, :] += jnp.sum(glu * later, axis=0, keepdims=True)
+            dglu = dglu + prm[t : t + 1, :] * later
         dglu = dglu * row_mask(length, i * RB, RB, 512)
         sg = sigmoid(gated[rows, 512:1024])
         ga = dglu * sg
@@ -465,7 +468,7 @@
         out_specs=[pl.BlockSpec(memory_space=ANY if space is LATE else space) for _, _, space in outs.values()],
         scratch_shapes=[pltpu.VMEM(shape, dtype) for shape, dtype in [*scratch.values(), *held]]
         + [pltpu.SemaphoreType.DMA((8 + len(held),))],
-        compiler_params=pltpu.CompilerParams(vmem_limit_bytes=58 * 2**20),
+        compiler_params=pltpu.CompilerParams(vmem_limit_bytes=55 * 2**20),
         cost_estimate=pl.CostEstimate(flops=int(micros * 1.1e9), bytes_accessed=2**20, transcendentals=0),
         name=body.__name__,
     )(*[array for array, _ in flat])
@@ -595,8 +598,10 @@
 
     @pl.when(k.ids[5] != layer)
     def _():
-        for number, part in enumerate(k.cot_other):
-            pltpu.make_async_copy(part, k.cot.at[256 * number : 256 * number + 256], k.sems.at[2]).start()
+        at = 0
+        for part in k.cot_other:
+            pltpu.make_async_copy(part, k.cot.at[at : at + part.shape[0]], k.sems.at[2]).start()
+            at += part.shape[0]
 
 
 FEED_SCRATCH = dict(n=(ROWS, BF), d=(ROWS, BF), act=((512, FF), BF), dh=((512, FF), BF), wf=WF, gf=WF)
@@ -714,7 +719,7 @@
         k.small[...] = jnp.zeros((SMALL, 512), F32)
         wait_load(k.wc, k.sems.at[1])
         s = types.SimpleNamespace(
-            n=k.n, d=k.d, act=k.act.at[:, 0:512], dga=k.dh.at[:, 0:512], dgb=k.dh.at[:, 512:1024], pad=k.pad, back=k.back
+            n=k.n, d=k.d, act=k.act.at[:, 0:512], dga=k.dh.at[:, 0:512], dgb=k.dh.at[:, 512:1024], glu=k.glu, back=k.back
         )
         conv_bwd(k.dx3.get(), k.x2.get(), k.gated.get(), k.deep.get(), k.wc, prm, k.ids[4], k.dx2, k.gc, k.small, s)
         start_store(k.ids, k.gc, k.keep, k.send, ATTN // 2, CONV // 2, k.sems.at[3])
@@ -761,7 +766,7 @@
             dm=(ROWS, BF),
             act=((512, 1536), BF),
             dh=((512, 1024), BF),
-            pad=PADDED,
+            glu=(ROWS, F32),
             back=PADDED,
             dq=((128, 512), F32),
             kt=((256, 512), BF),
@@ -1034,7 +1039,7 @@
     if fast:
         chunks = [None] * 4
         own_first, rest = own_pieces(low, sec, dp, first)
-        early_cot, late_cot = cot_send[:256], cot_send[256:]
+        early_cot, late_cot = cot_send[:320], cot_send[320:]
         own_first, rest, early_cot = fence(own_first, rest, early_cot)
         z0 = z_parts(own_first)
         own = own_rest(rest, low, sec, first)
@@ -1043,46 +1048,48 @@
         quad0 = jnp.stack(z0)
         a0, b0 = ab_parts(quad0)
         z1 = z_parts(own[0])
-        quad0, a0, b0, *z1 = fence(quad0, a0, b0, *z1)
+        quad0, a0, b0, own[2], *z1 = fence(quad0, a0, b0, own[2], *z1)
+        pair3 = jnp.concatenate([own[2], over_a(own[2])])
         ab0 = over_b(a0)
         core0 = [over_core(v) for v in (quad0, b0, a0)]
         quad1 = jnp.stack(z1)
-        quad1, ab0, frames, *core0 = fence(quad1, ab0, frames, *core0)
+        quad1, ab0, frames, pair3, *core0 = fence(quad1, ab0, frames, pair3, *core0)
         a1, b1 = ab_parts(quad1)
         chunks[0] = [quad0, b0, a0, ab0] + core0 + [over_core(ab0)]
         *chunks[0], own[1] = fence(*chunks[0], own[1])
         z2 = z_parts(own[1])
     else:
         chunks = gather_plain(low)
-        early_cot, late_cot = swap(cot_send[:256]), swap(cot_send[256:])
+        early_cot, late_cot = swap(cot_send[:320]), swap(cot_send[320:])
     ka = kernel_stem_feed(ids, chunks[0], frames)
     prm = ka.prm
     if fast:
-        ka.x1, quad1, a1, b1, *z2 = fence(ka.x1, quad1, a1, b1, *z2)
+        ka.x1, quad1, a1, b1, pair3, *z2 = fence(ka.x1, quad1, a1, b1, pair3, *z2)
+        mid3 = over_z(pair3, 2)
         ab1 = over_b(a1)
         core1 = [over_core(v) for v in (quad1, b1, a1)]
         quad2 = jnp.stack(z2)
-        ab1, quad2, *core1 = fence(ab1, quad2, *core1)
+        ab1, quad2, pair3, mid3, *core1 = fence(ab1, quad2, pair3, mid3, *core1)
         a2, b2 = ab_parts(quad2)
         chunks[1] = [quad1, b1, a1, ab1] + core1 + [over_core(ab1)]
-        *chunks[1], own[2] = fence(*chunks[1], own[2])
-        z3 = z_parts(own[2])
+        *chunks[1], pair3 = fence(*chunks[1], pair3)
+        far3, near3 = over_z(pair3, 3), over_z(pair3, 1)
     kb = kernel_rest_first(ids, chunks[1], prm, ka.x1)
     if fast:
-        kb.sent, quad2, a2, b2, *z3 = fence(kb.sent, quad2, a2, b2, *z3)
+        kb.sent, quad2, a2, b2, near3, far3, pair3 = fence(kb.sent, quad2, a2, b2, near3, far3, pair3)
         ab2 = over_b(a2)
+        oct3 = jnp.stack([pair3, near3, mid3, far3])
         core2 = [over_core(v) for v in (quad2, b2, a2)]
-        quad3 = jnp.stack(z3)
-        ab2, quad3, late_cot, *core2 = fence(ab2, quad3, late_cot, *core2)
-        a3, b3 = ab_parts(quad3)
+        ab2, oct3, late_cot, *core2 = fence(ab2, oct3, late_cot, *core2)
+        b3 = over_b(oct3)
         late_cot = swap(late_cot)
         chunks[2] = [quad2, b2, a2, ab2] + core2 + [over_core(ab2)]
         chunks[2] = list(fence(*chunks[2]))
+        core3 = over_core(oct3)
     kc = kernel_first_second(ids, chunks[2], prm, kb.sent)
     if fast:
-        kc.x3, quad3, a3, b3, late_cot = fence(kc.x3, quad3, a3, b3, late_cot)
-        chunks[3] = [quad3, b3, a3] + [over_b(a3)]
-        chunks[3] += [over_core(v) for v in chunks[3]]
+        kc.x3, oct3, b3, core3, late_cot = fence(kc.x3, oct3, b3, core3, late_cot)
+        chunks[3] = [oct3, b3, core3, over_core(b3)]
     cot_other = [early_cot, late_cot]
     kd = kernel_turn(ids, chunks[3], prm, kc.x3, cots, cot_other, allowed)
     other_sent = swap(jnp.where(first, kd.sent, kb.sent))
@@ -1143,12 +1150,18 @@
         gather_parts(4)
         go_on(5)
         sum_4 = z_sum(parts[4])
-        came[5], sum_4, ki.ig = fence(came[5], sum_4, ki.ig)
+        late = join(sum_3[: FEED // 2], sums_a[: FEED // 2], first).reshape(FEED, 512)
+        head = sum_3[FEED // 2 :].T
+        came[5], sum_4, ki.ig, late, head = fence(came[5], sum_4, ki.ig, late, head)
         gather_parts(5)
-        shards = own_shards(sums_a, sum_2, sum_3, sum_4, z_sum(parts[5]), dp, first)
+        sum_5 = z_sum(parts[5])
+        late_in, late_out = unpack_in(late, 4), late[128:]
+    other_grad = swap(jnp.where(first, kf.ig, ki.ig).astype(BF))
+    if fast:
+        sum_5, other_grad, late_in, late_out = fence(sum_5, other_grad, late_in, late_out)
+        shards = all_shards(late_in, late_out, head, sums_a, sum_2, sum_4, sum_5, dp, first)
     else:
         shards = reduce_plain([(k.keep, k.send) for k in (kd, ke, kf, kg, kh, ki)])
-    other_grad = swap(jnp.where(first, kf.ig, ki.ig).astype(BF))
     input_grads = kernel_grads(ids, ki.ig, kf.ig, other_grad)[None, :, None]
     activations = ko.acts[None, :, None]
     log_probs = ko.logp[None, :, None]
@@ -1181,25 +1194,22 @@
     ]
 
 
-def own_shards(sums_a, sum_2, sum_3, sum_4, sum_5, dp, first):
+def join(of_first, of_second, first):
+    own = jnp.where(first, of_first, of_second)
+    other = over_x(jnp.where(first, of_second, of_first).astype(BF)).astype(F32)
+    return jnp.stack(pick(first, own, other))
+
+
+def all_shards(late_in, late_out, head, sums_a, sum_2, sum_4, sum_5, dp, first):
     half = FEED // 2
-    head, early_first, stem = sum_3[half:], sum_5[:half], sum_5[half:]
-
-    def join(of_first, of_second):
-        own = jnp.where(first, of_first, of_second)
-        other = over_x(jnp.where(first, of_second, of_first).astype(BF)).astype(F32)
-        return jnp.stack(pick(first, own, other))
-
-    rest = join(jnp.concatenate([sum_3[:half], sum_4]), sums_a)
-    late, rest = rest[:, :half].reshape(FEED, 512), rest[:, half:]
-    early = join(early_first, sum_2).reshape(FEED, 512)
-    attn = rest[:, : ATTN // 2].reshape(ATTN, 512)
-    conv = rest[:, ATTN // 2 : LATE_ROWS].reshape(CONV, 512)
-    feeds = [early, late]
-    g_stem_in, g_stem_out, g_depth, g_gains = unpack_stem(stem, dp % 4)
+    both = join(jnp.concatenate([sum_4, sum_5[:half]]), jnp.concatenate([sums_a[half:], sum_2]), first)
+    attn = both[:, : ATTN // 2].reshape(ATTN, 512)
+    conv = both[:, ATTN // 2 : LATE_ROWS].reshape(CONV, 512)
+    early = both[:, LATE_ROWS:].reshape(FEED, 512)
+    g_stem_in, g_stem_out, g_depth, g_gains = unpack_stem(sum_5[half:], dp % 4)
     return (
-        jnp.stack([unpack_in(f, 4) for f in feeds])[None],
-        jnp.stack([f[128:] for f in feeds])[None],
+        jnp.stack([unpack_in(early, 4), late_in])[None],
+        jnp.stack([early[128:], late_out])[None],
         unpack_in(attn, 3)[None],
         attn[96:][None],
         unpack_in(conv, 2)[None],
@@ -1208,7 +1218,7 @@
         g_gains[None],
         g_stem_in,
         g_stem_out,
-        head.T,
+        head,
     )
 
 

time: 417 us -> 402 us (0.964)
  other arithmetic: 27.3 us -> 19.1 us
  waiting for transfers between devices: 118 us -> 112 us
    ppermute x4, waiting for transfers between devices: 8.12 us -> 0.01 us  [on_device(): swap = lambda v: lax.ppermute(v, 'section', [(0, 1), (1, 0)])]
    ppermute x77 -> x74, waiting for transfers between devices: 109 us -> 112 us  [across(): return lax.ppermute(value, BOTH, permutation(target))]
    ppermute x77 -> x74, starting transfers between devices: 82.2 us -> 82.2 us  [across(): return lax.ppermute(value, BOTH, permutation(target))]
  transfers between devices with their start and end apart: 81 -> 78, of which waited for: 20 -> 23; matrix products, arithmetic and copies ran while one was open for 9% -> 6% of each run, Pallas kernels for 33% -> 35%
where the time goes in v3:
time: 402 us; the launch traced here: 398 us
  Pallas kernels  157 us (39%)
  waiting for transfers between devices  112 us (28%)
  starting transfers between devices  85.7 us (21%)
  other arithmetic  19.1 us (5%)
  local copies, waits for them, and re-layouts  17.7 us (4%)
  between operations  6.31 us (2%)
    pallas_call x11, Pallas kernels, run(): pl.pallas_call(kernel, out_shape=[jax.ShapeDtypeStruct(shape, dtype) for...  157 us
    ppermute x74, waiting for transfers between devices, across(): return lax.ppermute(value, BOTH, permutation(target))  112 us
    ppermute x74, starting transfers between devices, across(): return lax.ppermute(value, BOTH, permutation(target))  82.2 us
  transfers between devices with their start and end apart: 78, of which 23 were waited for; matrix products, arithmetic and copies ran while one was open for 6% of the time, Pallas kernels for 35%

profile of v3, /device:TPU:0, one launch (start us, length us, event | category | flops | bytes accessed | tf_op | source)
XLA Modules:
  0.0 398.0 jit_solution(10731186170924707336)
XLA Ops:
  3.4 3.0 collective-permute-start
  16.6 14.6 %collective-permute-done.4 = bf16[240,512]{1,0:T(8,128)(2,1)S(1)} collective-permute-done((bf16[240,512]{1,0:T(8,128)(2,1)S(1)}, bf16[240,512]{1,0:T(8,128)(2,1)S(1)}, u32[]{:S(2)}, u32[]{:S(2)}) %collective-permute-start.4) | collective-permute-done | bytes 245792 | tf_op jit(solution)/shard_map/ppermute | solution.py:959
  39.7 4.1 %collective-permute-done.8 = bf16[240,512]{1,0:T(8,128)(2,1)S(1)} collective-permute-done((bf16[240,512]{1,0:T(8,128)(2,1)S(1)}, bf16[240,512]{1,0:T(8,128)(2,1)S(1)}, u32[]{:S(2)}, u32[]{:S(2)}) %collective-permute-start.8) | collective-permute-done | bytes 245792 | tf_op jit(solution)/shard_map/ppermute | solution.py:959
  43.9 12.2 %collective-permute-done.9 = bf16[240,512]{1,0:T(8,128)(2,1)S(1)} collective-permute-done((bf16[240,512]{1,0:T(8,128)(2,1)S(1)}, bf16[240,512]{1,0:T(8,128)(2,1)S(1)}, u32[]{:S(2)}, u32[]{:S(2)}) %collective-permute-start.9) | collective-permute-done | bytes 245792 | tf_op jit(solution)/shard_map/ppermute | solution.py:959
  63.0 5.6 %collective-permute-done.11.refs_4_ = bf16[4,160,512]{2,1,0:T(8,128)(2,1)} collective-permute-done((bf16[4,160,512]{2,1,0:T(8,128)(2,1)}, bf16[4,160,512]{2,1,0:T(8,128)(2,1)}, u32[]{:S(2)}, u32[]{:S(2)}) %collective-permute-start.11) | collective-permute-done | bytes 655392 | tf_op jit(solution)/shard_map/ppermute | solution.py:959
  71.9 3.2 collective-permute-start.19
  77.6 9.4 %stem_feed.1 = (f32[2,16,512]{2,1,0:T(8,128)}, f32[512,256]{1,0:T(8,128)}, bf16[256,512]{1,0:T(8,128)(2,1)}, bf16[512,512]{1,0:T(8,128)(2,1)}, bf16[512,2048]{1,0:T(8,128)(2,1)}, /*index=5*/f32[512,512]{1,0:T(8,128)}) custom-call(s32[6]{0:T(128)} %stack.111.refs_0_, bf16[4,160,512]{2,1,0:T(8,128)(2,1)} %pad_maximum_fusion.3.refs_1_, ...), custom_call_target="tpu_custom_call" | custom-call | flops 9900000256 | bytes 1048576 | tf_op jit(solution)/shard_map/stem_feed/pallas_call | solution.py:464
  87.0 8.4 %collective-permute-done.20 = bf16[240,512]{1,0:T(8,128)(2,1)S(1)} collective-permute-done((bf16[240,512]{1,0:T(8,128)(2,1)S(1)}, bf16[240,512]{1,0:T(8,128)(2,1)S(1)}, u32[]{:S(2)}, u32[]{:S(2)}) %collective-permute-start.20) | collective-permute-done | bytes 245792 | tf_op jit(solution)/shard_map/ppermute | solution.py:959
  97.4 5.5 %collective-permute-start.23 = (bf16[320,512]{1,0:T(8,128)(2,1)S(1)}, bf16[320,512]{1,0:T(8,128)(2,1)S(1)}, u32[]{:S(2)}, u32[]{:S(2)}) collective-permute-start(bf16[320,512]{1,0:T(8,128)(2,1)S(1)} %pad_maximum_fusion.8), channel_id=1, source_target_pairs={{0,8},{1,9},{2,10},{3,11},{4,12},{5,13},{6,14},{7,15},{8,0},{9,1},... | collective-permute-start | bytes 983048 | tf_op jit(solution)/shard_map/ppermute | solution.py:959
  103.9 14.3 %collective-permute-done.23 = bf16[320,512]{1,0:T(8,128)(2,1)S(1)} collective-permute-done((bf16[320,512]{1,0:T(8,128)(2,1)S(1)}, bf16[320,512]{1,0:T(8,128)(2,1)S(1)}, u32[]{:S(2)}, u32[]{:S(2)}) %collective-permute-start.23) | collective-permute-done | bytes 327712 | tf_op jit(solution)/shard_map/ppermute | solution.py:959
  122.4 16.5 %rest_first.1 = (bf16[512,1536]{1,0:T(8,128)(2,1)}, f32[8,512]{1,0:T(8,128)}, bf16[512,512]{1,0:T(8,128)(2,1)}, f32[512,512]{1,0:T(8,128)}, f32[512,1024]{1,0:T(...) custom-call(s32[6]{0:T(128)} %stack.111.refs_0_, ...), custom_call_target="tpu_custom_call" | custom-call | flops 22000001024 | bytes 1048576 | tf_op jit(solution)/shard_map/rest_first/pallas_call | solution.py:464
  138.9 4.4 %collective-permute-done.28.refs_3_ = bf16[4,240,512]{2,1,0:T(8,128)(2,1)} collective-permute-done((bf16[4,240,512]{2,1,0:T(8,128)(2,1)}, bf16[4,240,512]{2,1,0:T(8,128)(2,1)}, u32[]{:S(2)}, u32[]{:S(2)}) %collective-permute-start.28) | collective-permute-done | bytes 983072 | tf_op jit(solution)/shard_map/ppermute | solution.py:959
  146.2 11.6 %collective-permute-done.32.refs_4_ = bf16[4,240,512]{2,1,0:T(8,128)(2,1)} collective-permute-done((bf16[4,240,512]{2,1,0:T(8,128)(2,1)}, bf16[4,240,512]{2,1,0:T(8,128)(2,1)}, u32[]{:S(2)}, u32[]{:S(2)}) %collective-permute-start.32) | collective-permute-done | bytes 983072 | tf_op jit(solution)/shard_map/ppermute | solution.py:959
  162.5 16.6 %first_second.1 = (bf16[512,2048]{1,0:T(8,128)(2,1)}, f32[512,512]{1,0:T(8,128)}, bf16[512,1536]{1,0:T(8,128)(2,1)}, f32[8,512]{1,0:T(8,128)}, bf16[512,512]{1,0...) custom-call(s32[6]{0:T(128)} %stack.111.refs_0_, ...), custom_call_target="tpu_custom_call" | custom-call | flops 22000001024 | bytes 1048576 | tf_op jit(solution)/shard_map/first_second/pallas_call | solution.py:464
  179.1 5.1 %collective-permute-start.40 = (bf16[4,320,512]{2,1,0:T(8,128)(2,1)S(1)}, bf16[4,320,512]{2,1,0:T(8,128)(2,1)}, u32[]{:S(2)}, u32[]{:S(2)}) collective-permute-start(bf16[4,320,512]{2,1,0:T(8,128)(2,1)S(1)} %collective-permute-done.37.refs_2_.refs_10_.refs_3_), channel_id=1, source_target_pairs={{0,1},{1,0},{2,3},{3,2},{4,5},{5,4},{6,7},{7,6},{8,9},{9,8},{10,11... | collective-permute-start | bytes 3932168 | tf_op jit(solution)/shard_map/ppermute | solution.py:959
  190.2 18.9 %turn.1 = (bf16[512,512]{1,0:T(8,128)(2,1)}, f32[1024,512]{1,0:T(8,128)}, f32[512,512]{1,0:T(8,128)}, f32[16,512]{1,0:T(8,128)}, bf16[16,128,512]{2,1,0:T(8,128)(2,1)}, /*index=5*/bf16[16,128,512]{2,1,0:T(8,128)(2,1)}) custom-call(s32[6]{0:T(128)} %stack.111.refs_0_, bf16[4,320,512]{2,1,0:T(8,128)(2,1)} %copy-done.7, bf16[4,320,512]{2,1,0:T(8,128)(2,1)} %copy-done.23, ...), custom_call_target="tpu_custom_call" | custom-call | flops 24199999488 | bytes 1048576 | tf_op jit(solution)/shard_map/turn/pallas_call | solution.py:464
  217.3 21.1 %mid.2 = (f32[512,512]{1,0:T(8,128)}, f32[16,512]{1,0:T(8,128)}, bf16[16,112,512]{2,1,0:T(8,128)(2,1)}, bf16[16,112,512]{2,1,0:T(8,128)(2,1)}) custom-call(s32[6]{0:T(128)} %stack.111.refs_0_, bf16[4,240,512]{2,1,0:T(8,128)(2,1)} %pad_maximum_fusion.2.refs_1_, bf16[4,240,512]{2,1,0:T(8,128)(2,1)} %collective-permute-done.29.refs_2_, ...), custom_call_target="tpu_custom_call" | custom-call | flops 23100000256 | bytes 1048576 | tf_op jit(solution)/shard_map/mid/pallas_call | solution.py:464
  239.5 3.0 collective-permute-done.44
  243.8 12.5 %early.2 = (f32[512,512]{1,0:T(8,128)}, f32[16,512]{1,0:T(8,128)}, bf16[16,128,512]{2,1,0:T(8,128)(2,1)}, bf16[16,128,512]{2,1,0:T(8,128)(2,1)}) custom-call(s32[6]{0:T(128)} %stack.111.refs_0_, bf16[4,240,512]{2,1,0:T(8,128)(2,1)} %pad_maximum_fusion.2.refs_1_, bf16[4,240,512]{2,1,0:T(8,128)(2,1)} %collective-permute-done.29.refs_2_, ...), custom_call_target="tpu_custom_call" | custom-call | flops 11000000512 | bytes 1048576 | tf_op jit(solution)/shard_map/early/pallas_call | solution.py:464
  258.7 3.1 collective-permute-done.48
  263.2 16.2 %late.1 = (f32[512,512]{1,0:T(8,128)}, f32[16,512]{1,0:T(8,128)}, bf16[16,160,512]{2,1,0:T(8,128)(2,1)}, bf16[16,160,512]{2,1,0:T(8,128)(2,1)}) custom-call(s32[6]{0:T(128)} %stack.111.refs_0_, bf16[4,240,512]{2,1,0:T(8,128)(2,1)} %copy-done.10, bf16[4,240,512]{2,1,0:T(8,128)(2,1)} %copy-done.26, bf16[4,240,512]{2,1,0:T(8,128)(2,1)} %copy-done.25, ...), custom_call_target="tpu_custom_call" | custom-call | flops 18699999232 | bytes 1048576 | tf_op jit(solution)/shard_map/late/pallas_call | solution.py:464
  283.2 3.1 collective-permute-start.53
  287.8 21.3 %mid.3 = (f32[512,512]{1,0:T(8,128)}, f32[16,512]{1,0:T(8,128)}, bf16[16,112,512]{2,1,0:T(8,128)(2,1)}, bf16[16,112,512]{2,1,0:T(8,128)(2,1)}) custom-call(s32[6]{0:T(128)} %stack.111.refs_0_, bf16[4,240,512]{2,1,0:T(8,128)(2,1)} %copy-done.10, bf16[4,240,512]{2,1,0:T(8,128)(2,1)} %copy-done.26, bf16[4,240,512]{2,1,0:T(8,128)(2,1)} %copy-done.25, ...), custom_call_target="tpu_custom_call" | custom-call | flops 23100000256 | bytes 1048576 | tf_op jit(solution)/shard_map/mid/pallas_call | solution.py:464
  317.2 13.0 %early.3 = (f32[512,512]{1,0:T(8,128)}, f32[16,512]{1,0:T(8,128)}, bf16[16,160,512]{2,1,0:T(8,128)(2,1)}, bf16[16,160,512]{2,1,0:T(8,128)(2,1)}) custom-call(s32[6]{0:T(128)} %stack.111.refs_0_, bf16[4,160,512]{2,1,0:T(8,128)(2,1)} %pad_maximum_fusion.3.refs_1_, bf16[4,160,512]{2,1,0:T(8,128)(2,1)} %collective-permute-done.7.refs_2_, ...), custom_call_target="tpu_custom_call" | custom-call | flops 14300000256 | bytes 1048576 | tf_op jit(solution)/shard_map/early/pallas_call | solution.py:464
  332.3 3.3 collective-permute-done.63
  339.7 2.9 collective-permute-start.65
  342.6 8.3 %outputs.1 = (f32[2,512,1024]{2,1,0:T(8,128)}, f32[2,512,512]{2,1,0:T(8,128)}) custom-call(s32[6]{0:T(128)} %stack.111.refs_0_, s32[2]{0:T(128)} %bitcast.236, bf16[4,320,512]{2,1,0:T(8,128)(2,1)} %copy-done.7, bf16[4,320,512]{2,1,0:T(8,128)(2,1)} %copy-done.23, bf16[4,320,512]{2,1,0:T(8,128)(2,1)} %copy-done.24, ...), custom_call_target="tpu_custom_call" | custom-call | flops 9900000256 | bytes 1048576 | tf_op jit(solution)/shard_map/outputs/pallas_call | solution.py:464
  350.9 3.2 collective-permute-done.66
  364.1 3.7 collective-permute-done.70
  373.6 4.5 %collective-permute-done.75 = bf16[160,512]{1,0:T(8,128)(2,1)S(1)} collective-permute-done((bf16[160,512]{1,0:T(8,128)(2,1)S(1)}, bf16[160,512]{1,0:T(8,128)(2,1)S(1)}, u32[]{:S(2)}, u32[]{:S(2)}) %collective-permute-start.75) | collective-permute-done | bytes 163872 | tf_op jit(solution)/shard_map/ppermute | solution.py:959
  378.1 5.8 %collective-permute-done.74 = bf16[160,512]{1,0:T(8,128)(2,1)S(1)} collective-permute-done((bf16[160,512]{1,0:T(8,128)(2,1)S(1)}, bf16[160,512]{1,0:T(8,128)(2,1)S(1)}, u32[]{:S(2)}, u32[]{:S(2)}) %collective-permute-start.74) | collective-permute-done | bytes 163872 | tf_op jit(solution)/shard_map/ppermute | solution.py:959
  387.6 3.2 grads.1
  (337 shorter events, 110.1 us)
Async XLA Ops:
  10.0 21.3 %collective-permute-start.5 = (bf16[320,1024]{1,0:T(8,128)(2,1)S(1)}, bf16[320,1024]{1,0:T(8,128)(2,1)S(1)}, u32[]{:S(2)}, u32[]{:S(2)}) collective-permute-start(bf16[320,1024]{1,0:T(8,128)(2,1)S(1)} %dynamic-slice_bitcast_fusion), channel_id=1, source_target_pairs={{0,16},{16,0},{1,17},{17,1},{2,18},{18,2},{3,19},{19,3},{4,20},{20... | collective-permute-start | bytes 1966088 | tf_op jit(solution)/shard_map/ppermute | solution.py:1029
  11.9 19.4 %collective-permute-start.4 = (bf16[240,512]{1,0:T(8,128)(2,1)S(1)}, bf16[240,512]{1,0:T(8,128)(2,1)S(1)}, u32[]{:S(2)}, u32[]{:S(2)}) collective-permute-start(bf16[240,512]{1,0:T(8,128)(2,1)S(1)} %dynamic-slice_bitcast_fusion.2), channel_id=1, source_target_pairs={{0,16},{1,17},{2,18},{3,19},{4,20},{5,21},{6,22},{7,23},{8,24},{9,... | collective-permute-start | bytes 737288 | tf_op jit(solution)/shard_map/ppermute | solution.py:959
  12.2 19.1 %collective-permute-start.1 = (bf16[160,512]{1,0:T(8,128)(2,1)S(1)}, bf16[160,512]{1,0:T(8,128)(2,1)S(1)}, u32[]{:S(2)}, u32[]{:S(2)}) collective-permute-start(bf16[160,512]{1,0:T(8,128)(2,1)S(1)} %get-tuple-element.190), channel_id=1, source_target_pairs={{0,4},{1,5},{2,6},{3,7},{4,0},{5,1},{6,2},{7,3},{8,12},{9,13},{10,... | collective-permute-start | bytes 491528 | tf_op jit(solution)/shard_map/ppermute | solution.py:959
  32.3 23.7 %collective-permute-start.6 = (bf16[4,160,512]{2,1,0:T(8,128)(2,1)}, bf16[4,160,512]{2,1,0:T(8,128)(2,1)}, u32[]{:S(2)}, u32[]{:S(2)}) collective-permute-start(bf16[4,160,512]{2,1,0:T(8,128)(2,1)} %pad_maximum_fusion.3.refs_1_), channel_id=1, source_target_pairs={{0,16},{1,3},{2,18},{3,1},{4,20},{5,7},{6,22},{7,5},{8,24},{9,11},... | collective-permute-start | bytes 1966088 | tf_op jit(solution)/shard_map/ppermute | solution.py:959
  33.8 22.3 %collective-permute-start.7 = (bf16[4,160,512]{2,1,0:T(8,128)(2,1)}, bf16[4,160,512]{2,1,0:T(8,128)(2,1)}, u32[]{:S(2)}, u32[]{:S(2)}) collective-permute-start(bf16[4,160,512]{2,1,0:T(8,128)(2,1)} %pad_maximum_fusion.3.refs_1_), channel_id=1, source_target_pairs={{0,2},{1,17},{2,0},{3,19},{4,6},{5,21},{6,4},{7,23},{8,10},{9,25},... | collective-permute-start | bytes 1966088 | tf_op jit(solution)/shard_map/ppermute | solution.py:959
  36.9 19.2 %collective-permute-start.9 = (bf16[240,512]{1,0:T(8,128)(2,1)S(1)}, bf16[240,512]{1,0:T(8,128)(2,1)S(1)}, u32[]{:S(2)}, u32[]{:S(2)}) collective-permute-start(bf16[240,512]{1,0:T(8,128)(2,1)S(1)} %get-tuple-element.198), channel_id=1, source_target_pairs={{0,8},{1,9},{2,10},{3,11},{4,12},{5,13},{6,14},{7,15},{8,0},{9,1},... | collective-permute-start | bytes 737288 | tf_op jit(solution)/shard_map/ppermute | solution.py:959
  70.6 24.8 %collective-permute-start.17 = (bf16[4,240,512]{2,1,0:T(8,128)(2,1)S(1)}, bf16[4,240,512]{2,1,0:T(8,128)(2,1)S(1)}, u32[]{:S(2)}, u32[]{:S(2)}) collective-permute-start(bf16[4,240,512]{2,1,0:T(8,128)(2,1)S(1)} %pad_maximum_fusion.1.refs_1_), channel_id=1, source_target_pairs={{0,16},{1,3},{2,18},{3,1},{4,20},{5,7},{6,22},{7,5},{8,24},{9,11},... | collective-permute-start | bytes 2949128 | tf_op jit(solution)/shard_map/ppermute | solution.py:959
  71.2 24.2 %collective-permute-start.18 = (bf16[4,240,512]{2,1,0:T(8,128)(2,1)S(1)}, bf16[4,240,512]{2,1,0:T(8,128)(2,1)S(1)}, u32[]{:S(2)}, u32[]{:S(2)}) collective-permute-start(bf16[4,240,512]{2,1,0:T(8,128)(2,1)S(1)} %pad_maximum_fusion.1.refs_1_), channel_id=1, source_target_pairs={{0,2},{1,17},{2,0},{3,19},{4,6},{5,21},{6,4},{7,23},{8,10},{9,25},... | collective-permute-start | bytes 2949128 | tf_op jit(solution)/shard_map/ppermute | solution.py:959
  75.1 20.3 %collective-permute-start.20 = (bf16[240,512]{1,0:T(8,128)(2,1)S(1)}, bf16[240,512]{1,0:T(8,128)(2,1)S(1)}, u32[]{:S(2)}, u32[]{:S(2)}) collective-permute-start(bf16[240,512]{1,0:T(8,128)(2,1)S(1)} %pad_maximum_fusion.12), channel_id=1, source_target_pairs={{0,8},{1,9},{2,10},{3,11},{4,12},{5,13},{6,14},{7,15},{8,0},{9,1},... | collective-permute-start | bytes 737288 | tf_op jit(solution)/shard_map/ppermute | solution.py:959
  76.2 19.2 %collective-permute-start.21 = (bf16[240,512]{1,0:T(8,128)(2,1)S(1)}, bf16[240,512]{1,0:T(8,128)(2,1)S(1)}, u32[]{:S(2)}, u32[]{:S(2)}) collective-permute-start(bf16[240,512]{1,0:T(8,128)(2,1)S(1)} %pad_maximum_fusion.12), channel_id=1, source_target_pairs={{0,12},{1,13},{2,14},{3,15},{4,8},{5,9},{6,10},{7,11},{8,4},{9,5},... | collective-permute-start | bytes 737288 | tf_op jit(solution)/shard_map/ppermute | solution.py:959
  95.4 22.8 %collective-permute-start.22 = (bf16[4,240,512]{2,1,0:T(8,128)(2,1)S(1)}, bf16[4,240,512]{2,1,0:T(8,128)(2,1)S(1)}, u32[]{:S(2)}, u32[]{:S(2)}) collective-permute-start(bf16[4,240,512]{2,1,0:T(8,128)(2,1)S(1)} %collective-permute-done.17.refs_3_), channel_id=1, source_target_pairs={{0,2},{1,17},{2,0},{3,19},{4,6},{5,21},{6,4},{7,23},{8,10},{9,25},... | collective-permute-start | bytes 2949128 | tf_op jit(solution)/shard_map/ppermute | solution.py:959
  96.9 21.4 %collective-permute-start.24 = (bf16[4,240,512]{2,1,0:T(8,128)(2,1)S(1)}, bf16[4,240,512]{2,1,0:T(8,128)(2,1)S(1)}, u32[]{:S(2)}, u32[]{:S(2)}) collective-permute-start(bf16[4,240,512]{2,1,0:T(8,128)(2,1)S(1)} %pad_maximum_fusion.1.refs_1_), channel_id=1, source_target_pairs={{0,1},{1,0},{2,3},{3,2},{4,5},{5,4},{6,7},{7,6},{8,9},{9,8},{10,11... | collective-permute-start | bytes 2949128 | tf_op jit(solution)/shard_map/ppermute | solution.py:959
  96.9 21.4 %collective-permute-start.25 = (bf16[4,240,512]{2,1,0:T(8,128)(2,1)S(1)}, bf16[4,240,512]{2,1,0:T(8,128)(2,1)S(1)}, u32[]{:S(2)}, u32[]{:S(2)}) collective-permute-start(bf16[4,240,512]{2,1,0:T(8,128)(2,1)S(1)} %collective-permute-done.18.refs_2_), channel_id=1, source_target_pairs={{0,1},{1,0},{2,3},{3,2},{4,5},{5,4},{6,7},{7,6},{8,9},{9,8},{10,11... | collective-permute-start | bytes 2949128 | tf_op jit(solution)/shard_map/ppermute | solution.py:959
  97.4 20.9 %collective-permute-start.26 = (bf16[4,240,512]{2,1,0:T(8,128)(2,1)S(1)}, bf16[4,240,512]{2,1,0:T(8,128)(2,1)S(1)}, u32[]{:S(2)}, u32[]{:S(2)}) collective-permute-start(bf16[4,240,512]{2,1,0:T(8,128)(2,1)S(1)} %collective-permute-done.17.refs_3_), channel_id=1, source_target_pairs={{0,1},{1,0},{2,3},{3,2},{4,5},{5,4},{6,7},{7,6},{8,9},{9,8},{10,11... | collective-permute-start | bytes 2949128 | tf_op jit(solution)/shard_map/ppermute | solution.py:959
  97.4 20.9 %collective-permute-start.23 = (bf16[320,512]{1,0:T(8,128)(2,1)S(1)}, bf16[320,512]{1,0:T(8,128)(2,1)S(1)}, u32[]{:S(2)}, u32[]{:S(2)}) collective-permute-start(bf16[320,512]{1,0:T(8,128)(2,1)S(1)} %pad_maximum_fusion.8), channel_id=1, source_target_pairs={{0,8},{1,9},{2,10},{3,11},{4,12},{5,13},{6,14},{7,15},{8,0},{9,1},... | collective-permute-start | bytes 983048 | tf_op jit(solution)/shard_map/ppermute | solution.py:959
  118.4 24.9 %collective-permute-start.28 = (bf16[4,240,512]{2,1,0:T(8,128)(2,1)}, bf16[4,240,512]{2,1,0:T(8,128)(2,1)}, u32[]{:S(2)}, u32[]{:S(2)}) collective-permute-start(bf16[4,240,512]{2,1,0:T(8,128)(2,1)} %pad_maximum_fusion.2.refs_1_), channel_id=1, source_target_pairs={{0,16},{1,3},{2,18},{3,1},{4,20},{5,7},{6,22},{7,5},{8,24},{9,11},... | collective-permute-start | bytes 2949128 | tf_op jit(solution)/shard_map/ppermute | solution.py:959
  120.0 23.3 %collective-permute-start.29 = (bf16[4,240,512]{2,1,0:T(8,128)(2,1)}, bf16[4,240,512]{2,1,0:T(8,128)(2,1)}, u32[]{:S(2)}, u32[]{:S(2)}) collective-permute-start(bf16[4,240,512]{2,1,0:T(8,128)(2,1)} %pad_maximum_fusion.2.refs_1_), channel_id=1, source_target_pairs={{0,2},{1,17},{2,0},{3,19},{4,6},{5,21},{6,4},{7,23},{8,10},{9,25},... | collective-permute-start | bytes 2949128 | tf_op jit(solution)/shard_map/ppermute | solution.py:959
  121.0 22.3 %collective-permute-start.30 = (bf16[320,512]{1,0:T(8,128)(2,1)S(1)}, bf16[320,512]{1,0:T(8,128)(2,1)S(1)}, u32[]{:S(2)}, u32[]{:S(2)}) collective-permute-start(bf16[320,512]{1,0:T(8,128)(2,1)S(1)} %pad_maximum_fusion.8), channel_id=1, source_target_pairs={{0,4},{1,5},{2,6},{3,7},{4,0},{5,1},{6,2},{7,3},{8,12},{9,13},{10,... | collective-permute-start | bytes 983048 | tf_op jit(solution)/shard_map/ppermute | solution.py:959
  121.0 22.3 %collective-permute-start.31 = (bf16[320,512]{1,0:T(8,128)(2,1)S(1)}, bf16[320,512]{1,0:T(8,128)(2,1)S(1)}, u32[]{:S(2)}, u32[]{:S(2)}) collective-permute-start(bf16[320,512]{1,0:T(8,128)(2,1)S(1)} %pad_maximum_fusion.8), channel_id=1, source_target_pairs={{0,12},{1,13},{2,14},{3,15},{4,8},{5,9},{6,10},{7,11},{8,4},{9,5},... | collective-permute-start | bytes 983048 | tf_op jit(solution)/shard_map/ppermute | solution.py:959
  158.7 20.4 %collective-permute-start.37 = (bf16[4,320,512]{2,1,0:T(8,128)(2,1)S(1)}, bf16[4,320,512]{2,1,0:T(8,128)(2,1)S(1)}, u32[]{:S(2)}, u32[]{:S(2)}) collective-permute-start(bf16[4,320,512]{2,1,0:T(8,128)(2,1)S(1)} %pad_maximum_fusion.refs_1_.refs_9_.refs_2_), channel_id=1, source_target_pairs={{0,2},{1,17},{2,0},{3,19},{4,6},{5,21},{6,4},{7,23},{8,10},{9,25},... | collective-permute-start | bytes 3932168 | tf_op jit(solution)/shard_map/ppermute | solution.py:959
  159.0 20.0 %collective-permute-start.38 = (bf16[4,320,512]{2,1,0:T(8,128)(2,1)S(1)}, bf16[4,320,512]{2,1,0:T(8,128)(2,1)S(1)}, u32[]{:S(2)}, u32[]{:S(2)}) collective-permute-start(bf16[4,320,512]{2,1,0:T(8,128)(2,1)S(1)} %pad_maximum_fusion.refs_1_.refs_9_.refs_2_), channel_id=1, source_target_pairs={{0,1},{1,0},{2,3},{3,2},{4,5},{5,4},{6,7},{7,6},{8,9},{9,8},{10,11... | collective-permute-start | bytes 3932168 | tf_op jit(solution)/shard_map/ppermute | solution.py:959
  210.7 27.8 %collective-permute-start.43 = (bf16[512,512]{1,0:T(8,128)(2,1)S(1)}, bf16[512,512]{1,0:T(8,128)(2,1)S(1)}, u32[]{:S(2)}, u32[]{:S(2)}) collective-permute-start(bf16[512,512]{1,0:T(8,128)(2,1)S(1)} %broadcast_select_fusion), channel_id=1, source_target_pairs={{0,16},{16,0},{1,17},{17,1},{2,18},{18,2},{3,19},{19,3},{4,20},{20... | collective-permute-start | bytes 1572872 | tf_op jit(solution)/shard_map/ppermute | solution.py:1029
  215.8 22.7 %collective-permute-start.42 = (bf16[8,128,512]{2,1,0:T(8,128)(2,1)S(1)}, bf16[8,128,512]{2,1,0:T(8,128)(2,1)S(1)}, u32[]{:S(2)}, u32[]{:S(2)}) collective-permute-start(bf16[8,128,512]{2,1,0:T(8,128)(2,1)S(1)} %get-tuple-element.410), channel_id=1, source_target_pairs={{0,16},{1,3},{2,18},{3,1},{4,20},{5,7},{6,22},{7,5},{8,24},{9,11},... | collective-permute-start | bytes 3145736 | tf_op jit(solution)/shard_map/ppermute | solution.py:959
  258.0 21.4 %collective-permute-start.47 = (bf16[4,112,512]{2,1,0:T(8,128)(2,1)S(1)}, bf16[4,112,512]{2,1,0:T(8,128)(2,1)S(1)}, u32[]{:S(2)}, u32[]{:S(2)}) collective-permute-start(bf16[4,112,512]{2,1,0:T(8,128)(2,1)S(1)} %get-tuple-element.427), channel_id=1, source_target_pairs={{0,2},{1,17},{2,0},{3,19},{4,6},{5,21},{6,4},{7,23},{8,10},{9,25},... | collective-permute-start | bytes 1376264 | tf_op jit(solution)/shard_map/ppermute | solution.py:959
  280.1 29.2 %collective-permute-start.50 = (bf16[4,128,512]{2,1,0:T(8,128)(2,1)S(1)}, bf16[4,128,512]{2,1,0:T(8,128)(2,1)S(1)}, u32[]{:S(2)}, u32[]{:S(2)}) collective-permute-start(bf16[4,128,512]{2,1,0:T(8,128)(2,1)S(1)} %get-tuple-element.421), channel_id=1, source_target_pairs={{0,2},{1,17},{2,0},{3,19},{4,6},{5,21},{6,4},{7,23},{8,10},{9,25},... | collective-permute-start | bytes 1572872 | tf_op jit(solution)/shard_map/ppermute | solution.py:959
  281.7 27.4 %collective-permute-start.55 = (bf16[240,512]{1,0:T(8,128)(2,1)S(1)}, bf16[240,512]{1,0:T(8,128)(2,1)S(1)}, u32[]{:S(2)}, u32[]{:S(2)}) collective-permute-start(bf16[240,512]{1,0:T(8,128)(2,1)S(1)} %pad_maximum_fusion.15), channel_id=1, source_target_pairs={{0,12},{1,13},{2,14},{3,15},{4,8},{5,9},{6,10},{7,11},{8,4},{9,5},... | collective-permute-start | bytes 737288 | tf_op jit(solution)/shard_map/ppermute | solution.py:959
  283.1 26.0 %collective-permute-start.54 = (bf16[240,512]{1,0:T(8,128)(2,1)S(1)}, bf16[240,512]{1,0:T(8,128)(2,1)S(1)}, u32[]{:S(2)}, u32[]{:S(2)}) collective-permute-start(bf16[240,512]{1,0:T(8,128)(2,1)S(1)} %pad_maximum_fusion.14), channel_id=1, source_target_pairs={{0,8},{1,9},{2,10},{3,11},{4,12},{5,13},{6,14},{7,15},{8,0},{9,1},... | collective-permute-start | bytes 737288 | tf_op jit(solution)/shard_map/ppermute | solution.py:959
  283.2 25.9 %collective-permute-start.53 = (bf16[240,512]{1,0:T(8,128)(2,1)S(1)}, bf16[240,512]{1,0:T(8,128)(2,1)S(1)}, u32[]{:S(2)}, u32[]{:S(2)}) collective-permute-start(bf16[240,512]{1,0:T(8,128)(2,1)S(1)} %pad_maximum_fusion.13), channel_id=1, source_target_pairs={{0,4},{1,5},{2,6},{3,7},{4,0},{5,1},{6,2},{7,3},{8,12},{9,13},{10,... | collective-permute-start | bytes 737288 | tf_op jit(solution)/shard_map/ppermute | solution.py:959
  287.2 22.1 %collective-permute-start.52 = (bf16[8,160,512]{2,1,0:T(8,128)(2,1)S(1)}, bf16[8,160,512]{2,1,0:T(8,128)(2,1)S(1)}, u32[]{:S(2)}, u32[]{:S(2)}) collective-permute-start(bf16[8,160,512]{2,1,0:T(8,128)(2,1)S(1)} %get-tuple-element.407), channel_id=1, source_target_pairs={{0,16},{1,3},{2,18},{3,1},{4,20},{5,7},{6,22},{7,5},{8,24},{9,11},... | collective-permute-start | bytes 3932168 | tf_op jit(solution)/shard_map/ppermute | solution.py:959
  309.8 20.6 %collective-permute-start.57 = (bf16[4,160,512]{2,1,0:T(8,128)(2,1)S(1)}, bf16[4,160,512]{2,1,0:T(8,128)(2,1)S(1)}, u32[]{:S(2)}, u32[]{:S(2)}) collective-permute-start(bf16[4,160,512]{2,1,0:T(8,128)(2,1)S(1)} %get-tuple-element.419), channel_id=1, source_target_pairs={{0,2},{1,17},{2,0},{3,19},{4,6},{5,21},{6,4},{7,23},{8,10},{9,25},... | collective-permute-start | bytes 1966088 | tf_op jit(solution)/shard_map/ppermute | solution.py:959
  311.5 18.7 %collective-permute-start.61 = (bf16[128,512]{1,0:T(8,128)(2,1)S(1)}, bf16[128,512]{1,0:T(8,128)(2,1)S(1)}, u32[]{:S(2)}, u32[]{:S(2)}) collective-permute-start(bf16[128,512]{1,0:T(8,128)(2,1)S(1)} %get-tuple-element.437), channel_id=1, source_target_pairs={{0,12},{1,13},{2,14},{3,15},{4,8},{5,9},{6,10},{7,11},{8,4},{9,5},... | collective-permute-start | bytes 393224 | tf_op jit(solution)/shard_map/ppermute | solution.py:959
  330.8 23.4 %collective-permute-start.62 = (bf16[4,112,512]{2,1,0:T(8,128)(2,1)S(1)}, bf16[4,112,512]{2,1,0:T(8,128)(2,1)S(1)}, u32[]{:S(2)}, u32[]{:S(2)}) collective-permute-start(bf16[4,112,512]{2,1,0:T(8,128)(2,1)S(1)} %get-tuple-element.425), channel_id=1, source_target_pairs={{0,2},{1,17},{2,0},{3,19},{4,6},{5,21},{6,4},{7,23},{8,10},{9,25},... | collective-permute-start | bytes 1376264 | tf_op jit(solution)/shard_map/ppermute | solution.py:959
  (86 other events, 991.1 us)

commit v4 on v3

--- a/solution.py
+++ b/solution.py
@@ -103,6 +103,18 @@
         pltpu.make_async_copy(src, dst, sem).start()
 
 
+def start_piece(ids, scr, keep, send, row, rows, sem, px, d):
+    pz, py, pc = d // 4, (d // 2) % 2, d % 2
+    xr, yr, zk, cr = px ^ ids[0], py ^ ids[2], pz ^ ids[1], pc ^ ids[3]
+    a, b = (yr, xr) if pc else (xr, yr)
+    src = scr.at[d, px * rows : px * rows + rows]
+    for side, target in enumerate((keep, send)):
+
+        @pl.when(cr == side)
+        def _():
+            pltpu.make_async_copy(src, target.at[a * 8 + b * 4 + zk, row : row + rows], sem).start()
+
+
 def wait_store(scr, sem):
     pltpu.make_async_copy(scr, scr, sem).wait()
 
@@ -130,7 +142,7 @@
     row_loop(body)
 
 
-def feed_bwd(dx, x, hid, w, gain, out, gw, small, row, s):
+def feed_bwd(dx, x, hid, w, gain, result, gw, small, row, s):
     def body(rs, start):
         g = dx[rs, :]
         v = x[rs, :].astype(F32)
@@ -147,14 +159,21 @@
             s.dh[rs, 512 * j : 512 * j + 512] = dh
             dn = dn + dotr(dh, in_block(w, j))
         dv, gg = unit_back(dn, u, r, gain)
-        out[rs, :] = g + dv
+        result.held[rs, :] = g + dv
         small[row : row + 1, :] += gg
 
     row_loop(body)
+    result.go()
+    for j in range(4):
+        cols = slice(512 * j, 512 * j + 512)
+        gw[4 * j : 4 * j + 4, 128:256, :] = dotl(s.act[:, cols], s.d[...]).astype(BF).reshape(4, 128, 512)
+        for d in range(4 * j, 4 * j + 4):
+            start_piece(s.ids, gw, s.keep, s.send, 0, FEED // 2, s.sems.at[3], 1, d)
     for j in range(4):
         cols = slice(512 * j, 512 * j + 512)
         gw[:, 32 * j : 32 * j + 32, :] = dotl(s.n[...], s.dh[:, cols]).astype(BF).reshape(16, 32, 512)
-        gw[4 * j : 4 * j + 4, 128:256, :] = dotl(s.act[:, cols], s.d[...]).astype(BF).reshape(4, 128, 512)
+    for d in range(16):
+        start_piece(s.ids, gw, s.keep, s.send, 0, FEED // 2, s.sems.at[3], 0, d)
 
 
 def lanes_of(half, axis=1, count=1):
@@ -610,23 +629,24 @@
 
 def kernel_turn(ids, bufs, prm, x3, cots, cot_other, allowed):
     def turn(k):
+        k.prm.go()
         k.x3.go()
         start_load(k.ids, k.bufs, 0, FEED // 2, k.wf, k.sems.at[0])
         start_load(k.ids, k.bufs, FEED // 2, FLAT, k.wh, k.sems.at[1], flat=True)
         start_cot(k, 1)
-        prm = k.prm.at[1]
-        k.small[...] = jnp.zeros((SMALL, 512), F32)
+        prm = k.prm.get().at[1]
+        small = k.small.held
+        small[...] = jnp.zeros((SMALL, 512), F32)
         x3 = k.x3.get()
         wait_load(k.wf, k.sems.at[0])
         feed_fwd(x3, k.wf, gain_of(prm, 4), k.hid, k.x4)
         finish_fwd(k.x4, prm, k.ids[4], k.sent)
         wait_load(k.wh, k.sems.at[1])
         wait_load(k.cot, k.sems.at[2])
-        head_bwd(k.x4, k.sent, k.wh, k.allowed, k.cot, prm, k.ids[4], None, k.dx4, k.gl, k.small)
+        head_bwd(k.x4, k.sent, k.wh, k.allowed, k.cot, prm, k.ids[4], None, k.dx4, k.gl, small)
         k.ghead.held[...] = dotl(k.gl[...], k.sent[...])
         k.ghead.go()
-        feed_bwd(k.dx4, x3, k.hid, k.wf, gain_of(prm, 4), k.dx3.held, k.gf, k.small, TAPS + 4, k)
-        start_store(k.ids, k.gf, k.keep, k.send, 0, FEED // 2, k.sems.at[3])
+        feed_bwd(k.dx4, x3, k.hid, k.wf, gain_of(prm, 4), k.dx3, k.gf, small, TAPS + 4, k)
         wait_store(k.gf, k.sems.at[3])
 
     rows = FEED // 2
@@ -636,7 +656,7 @@
         dict(
             ids=(ids, SMEM),
             bufs=(bufs, ANY),
-            prm=(prm, VMEM),
+            prm=(prm, LATE),
             x3=(x3, LATE),
             cots=(cots, ANY),
             cot_other=(cot_other, ANY),
@@ -646,7 +666,7 @@
             sent=(ROWS, BF, VMEM),
             ghead=((1024, 512), F32, LATE),
             dx3=(ROWS, F32, LATE),
-            small=((SMALL, 512), F32, VMEM),
+            small=((SMALL, 512), F32, LATE),
             keep=((16, rows, 512), BF, ANY),
             send=((16, rows, 512), BF, ANY),
         ),
@@ -658,21 +678,22 @@
     def late(k):
         start_load(k.ids, k.hbufs, FEED // 2, FLAT, k.wh, k.sems.at[1], flat=True)
         start_cot(k, 0)
-        k.x4.go()
-        k.ig.go()
+        for operand in (k.prm, k.x4, k.sent, k.ig):
+            operand.go()
         start_load(k.ids, k.bufs, LATE_ROWS, FEED // 2, k.wf, k.sems.at[0])
         for operand in (k.ghead, k.x3, k.hid):
             operand.go()
-        prm = k.prm.at[0]
-        k.small[...] = jnp.zeros((SMALL, 512), F32)
+        prm = k.prm.get().at[0]
+        small = k.small.held
+        small[...] = jnp.zeros((SMALL, 512), F32)
         wait_load(k.wh, k.sems.at[1])
         wait_load(k.cot, k.sems.at[2])
-        head_bwd(k.x4.get(), k.sent, k.wh, k.allowed, k.cot, prm, k.ids[4], k.ig.get(), k.dx4, k.gl, k.small)
-        k.gh[...] = (k.ghead.get()[...] + dotl(k.gl[...], k.sent[...])).astype(BF).reshape(32, FLAT, 512)
+        sent = k.sent.get()
+        head_bwd(k.x4.get(), sent, k.wh, k.allowed, k.cot, prm, k.ids[4], k.ig.get(), k.dx4, k.gl, small)
+        k.gh[...] = (k.ghead.get()[...] + dotl(k.gl[...], sent[...])).astype(BF).reshape(32, FLAT, 512)
         start_store(k.ids, k.gh, k.keep, k.send, FEED // 2, FLAT, k.sems.at[4], flat=True)
         wait_load(k.wf, k.sems.at[0])
-        feed_bwd(k.dx4, k.x3.get(), k.hid.get(), k.wf, gain_of(prm, 4), k.dx3.held, k.gf, k.small, TAPS + 4, k)
-        start_store(k.ids, k.gf, k.keep, k.send, 0, FEED // 2, k.sems.at[3])
+        feed_bwd(k.dx4, k.x3.get(), k.hid.get(), k.wf, gain_of(prm, 4), k.dx3, k.gf, small, TAPS + 4, k)
         wait_store(k.gh, k.sems.at[4])
         wait_store(k.gf, k.sems.at[3])
 
@@ -684,9 +705,9 @@
             ids=(ids, SMEM),
             bufs=(bufs, ANY),
             hbufs=(head_bufs, ANY),
-            prm=(prm, VMEM),
+            prm=(prm, LATE),
             x4=(x4, LATE),
-            sent=(sent, VMEM),
+            sent=(sent, LATE),
             cots=(cots, ANY),
             cot_other=(cot_other, ANY),
             allowed=(allowed, VMEM),
@@ -697,7 +718,7 @@
         ),
         dict(
             dx3=(ROWS, F32, LATE),
-            small=((SMALL, 512), F32, VMEM),
+            small=((SMALL, 512), F32, LATE),
             keep=((16, rows, 512), BF, ANY),
             send=((16, rows, 512), BF, ANY),
         ),
@@ -707,27 +728,28 @@
 
 def kernel_mid(layer, ids, bufs, row, prm, dx3, x2, gated, deep, x1, qkv, ls, mixed):
     def mid(k):
-        for operand in (k.dx3, k.deep):
+        for operand in (k.prm, k.dx3, k.deep):
             operand.go()
         start_load(k.ids, k.bufs, row + ATTN // 2, CONV // 2, k.wc, k.sems.at[1])
         for operand in (k.gated, k.x2):
             operand.go()
         start_load(k.ids, k.bufs, row, ATTN // 2, k.wa, k.sems.at[0])
-        for operand in (k.x1, k.mixed, k.qkv):
+        for operand in (k.x1, k.mixed, k.qkv, k.ls):
             operand.go()
-        prm = k.prm.at[layer]
-        k.small[...] = jnp.zeros((SMALL, 512), F32)
+        prm = k.prm.get().at[layer]
+        small = k.small.held
+        small[...] = jnp.zeros((SMALL, 512), F32)
         wait_load(k.wc, k.sems.at[1])
         s = types.SimpleNamespace(
             n=k.n, d=k.d, act=k.act.at[:, 0:512], dga=k.dh.at[:, 0:512], dgb=k.dh.at[:, 512:1024], glu=k.glu, back=k.back
         )
-        conv_bwd(k.dx3.get(), k.x2.get(), k.gated.get(), k.deep.get(), k.wc, prm, k.ids[4], k.dx2, k.gc, k.small, s)
+        conv_bwd(k.dx3.get(), k.x2.get(), k.gated.get(), k.deep.get(), k.wc, prm, k.ids[4], k.dx2, k.gc, small, s)
         start_store(k.ids, k.gc, k.keep, k.send, ATTN // 2, CONV // 2, k.sems.at[3])
         wait_load(k.wa, k.sems.at[0])
         s = types.SimpleNamespace(n=k.n, d=k.d, dm=k.dm, dpk=k.act, dq=k.dq, kt=k.kt)
         attn_bwd(
-            k.dx2, k.x1.get(), k.qkv.get(), k.ls, k.mixed.get(), k.wa, gain_of(prm, 1), k.ids[4], k.dx1.held, k.ga,
-            k.small, TAPS + 1, s,
+            k.dx2, k.x1.get(), k.qkv.get(), k.ls.get(), k.mixed.get(), k.wa, gain_of(prm, 1), k.ids[4], k.dx1.held, k.ga,
+            small, TAPS + 1, s,
         )
         start_store(k.ids, k.ga, k.keep, k.send, 0, ATTN // 2, k.sems.at[2])
         wait_store(k.gc, k.sems.at[3])
@@ -739,19 +761,19 @@
         dict(
             ids=(ids, SMEM),
             bufs=(bufs, ANY),
-            prm=(prm, VMEM),
+            prm=(prm, LATE),
             dx3=(dx3, LATE),
             x2=(x2, LATE),
             gated=(gated, LATE),
             deep=(deep, LATE),
             x1=(x1, LATE),
             qkv=(qkv, LATE),
-            ls=(ls, VMEM),
+            ls=(ls, LATE),
             mixed=(mixed, LATE),
         ),
         dict(
             dx1=(ROWS, F32, LATE),
-            small=((SMALL, 512), F32, VMEM),
+            small=((SMALL, 512), F32, LATE),
             keep=((16, LATE_ROWS, 512), BF, ANY),
             send=((16, LATE_ROWS, 512), BF, ANY),
         ),
@@ -776,20 +798,20 @@
 
 def kernel_early(layer, ids, bufs, row, prm, dx1, x0, hid, stem):
     def early(k):
-        k.dx1.go()
-        k.x0.go()
+        for operand in (k.prm, k.dx1, k.x0):
+            operand.go()
         start_load(k.ids, k.bufs, row, FEED // 2, k.wf, k.sems.at[1])
         k.hid.go()
         if stem is not None:
             k.pre.go()
             k.frames.go()
-        prm = k.prm.at[layer]
-        k.small[...] = jnp.zeros((SMALL, 512), F32)
+        prm = k.prm.get().at[layer]
+        small = k.small.held
+        small[...] = jnp.zeros((SMALL, 512), F32)
         wait_load(k.wf, k.sems.at[1])
         ig = k.ig.held
-        feed_bwd(k.dx1.get(), k.x0.get(), k.hid.get(), k.wf, gain_of(prm, 0), ig, k.gf, k.small, TAPS, k)
-        k.ig.go()
-        start_store(k.ids, k.gf, k.keep, k.send, 0, FEED // 2, k.sems.at[3])
+        feed_bwd(k.dx1.get(), k.x0.get(), k.hid.get(), k.wf, gain_of(prm, 0), k.ig, k.gf, small, TAPS, k)
+        k.small.go()
         if stem is not None:
             pre, frames = k.pre.get(), k.frames.get()
 
@@ -806,7 +828,7 @@
             k.gs[:, 8:16, 0:128] = dotl(k.n[:, 256:512], frames[:, 512:640]).reshape(32, 8, 128)
             k.gs[:, 8:16, 128:512] = jnp.zeros((32, 8, 384), F32)
             k.gs[:, 16:24, :] = dotl(k.n[:, 0:256], k.d[...]).reshape(32, 8, 512)
-            first, second = k.small[...], jnp.zeros((SMALL, 512), F32)
+            first, second = small[...], jnp.zeros((SMALL, 512), F32)
             for part in k.smalls[:2]:
                 first = first + part[...]
             for part in k.smalls[2:]:
@@ -826,7 +848,7 @@
     ins = dict(
         ids=(ids, SMEM),
         bufs=(bufs, ANY),
-        prm=(prm, VMEM),
+        prm=(prm, LATE),
         dx1=(dx1, LATE),
         x0=(x0, LATE),
         hid=(hid, LATE),
@@ -842,7 +864,7 @@
         ins,
         dict(
             ig=(ROWS, F32, LATE),
-            small=((SMALL, 512), F32, VMEM),
+            small=((SMALL, 512), F32, LATE),
             keep=((16, rows, 512), BF, ANY),
             send=((16, rows, 512), BF, ANY),
         ),

time: 402 us -> 399 us (level)
    pallas_call x11, Pallas kernels: 157 us -> 153 us  [run(): pl.pallas_call(kernel, out_shape=[jax.ShapeDtypeStruct(shape, dtype) for...]
  transfers between devices with their start and end apart: 78 -> 78, of which waited for: 23 -> 25; matrix products, arithmetic and copies ran while one was open for 6% -> 6% of each run, Pallas kernels for 35% -> 34%
where the time goes in v4:
time: 399 us; the launch traced here: 396 us
  Pallas kernels  153 us (38%)
  waiting for transfers between devices  114 us (29%)
  starting transfers between devices  85.7 us (21%)
  other arithmetic  19.3 us (5%)
  local copies, waits for them, and re-layouts  17.6 us (4%)
  between operations  6.28 us (2%)
    pallas_call x11, Pallas kernels, run(): pl.pallas_call(kernel, out_shape=[jax.ShapeDtypeStruct(shape, dtype) for...  153 us
    ppermute x74, waiting for transfers between devices, across(): return lax.ppermute(value, BOTH, permutation(target))  114 us
    ppermute x74, starting transfers between devices, across(): return lax.ppermute(value, BOTH, permutation(target))  81.9 us
  transfers between devices with their start and end apart: 78, of which 25 were waited for; matrix products, arithmetic and copies ran while one was open for 6% of the time, Pallas kernels for 34%

profile of v4, /device:TPU:0, one launch (start us, length us, event | category | flops | bytes accessed | tf_op | source)
XLA Modules:
  0.0 395.7 jit_solution(5517282067751867571)
XLA Ops:
  3.4 3.0 collective-permute-start
  16.6 14.6 %collective-permute-done.4 = bf16[240,512]{1,0:T(8,128)(2,1)S(1)} collective-permute-done((bf16[240,512]{1,0:T(8,128)(2,1)S(1)}, bf16[240,512]{1,0:T(8,128)(2,1)S(1)}, u32[]{:S(2)}, u32[]{:S(2)}) %collective-permute-start.4) | collective-permute-done | bytes 245792 | tf_op jit(solution)/shard_map/ppermute | solution.py:981
  39.7 4.1 %collective-permute-done.8 = bf16[240,512]{1,0:T(8,128)(2,1)S(1)} collective-permute-done((bf16[240,512]{1,0:T(8,128)(2,1)S(1)}, bf16[240,512]{1,0:T(8,128)(2,1)S(1)}, u32[]{:S(2)}, u32[]{:S(2)}) %collective-permute-start.8) | collective-permute-done | bytes 245792 | tf_op jit(solution)/shard_map/ppermute | solution.py:981
  43.9 12.2 %collective-permute-done.9 = bf16[240,512]{1,0:T(8,128)(2,1)S(1)} collective-permute-done((bf16[240,512]{1,0:T(8,128)(2,1)S(1)}, bf16[240,512]{1,0:T(8,128)(2,1)S(1)}, u32[]{:S(2)}, u32[]{:S(2)}) %collective-permute-start.9) | collective-permute-done | bytes 245792 | tf_op jit(solution)/shard_map/ppermute | solution.py:981
  63.0 5.6 %collective-permute-done.11.refs_4_ = bf16[4,160,512]{2,1,0:T(8,128)(2,1)} collective-permute-done((bf16[4,160,512]{2,1,0:T(8,128)(2,1)}, bf16[4,160,512]{2,1,0:T(8,128)(2,1)}, u32[]{:S(2)}, u32[]{:S(2)}) %collective-permute-start.11) | collective-permute-done | bytes 655392 | tf_op jit(solution)/shard_map/ppermute | solution.py:981
  71.9 3.2 collective-permute-start.19
  77.6 9.4 %stem_feed.1 = (f32[2,16,512]{2,1,0:T(8,128)}, f32[512,256]{1,0:T(8,128)}, bf16[256,512]{1,0:T(8,128)(2,1)}, bf16[512,512]{1,0:T(8,128)(2,1)}, bf16[512,2048]{1,0:T(8,128)(2,1)}, /*index=5*/f32[512,512]{1,0:T(8,128)}) custom-call(s32[6]{0:T(128)} %stack.111.refs_0_, bf16[4,160,512]{2,1,0:T(8,128)(2,1)} %pad_maximum_fusion.3.refs_1_, ...), custom_call_target="tpu_custom_call" | custom-call | flops 9900000256 | bytes 1048576 | tf_op jit(solution)/shard_map/stem_feed/pallas_call | solution.py:483
  87.0 8.4 %collective-permute-done.20 = bf16[240,512]{1,0:T(8,128)(2,1)S(1)} collective-permute-done((bf16[240,512]{1,0:T(8,128)(2,1)S(1)}, bf16[240,512]{1,0:T(8,128)(2,1)S(1)}, u32[]{:S(2)}, u32[]{:S(2)}) %collective-permute-start.20) | collective-permute-done | bytes 245792 | tf_op jit(solution)/shard_map/ppermute | solution.py:981
  97.4 5.5 %collective-permute-start.23 = (bf16[320,512]{1,0:T(8,128)(2,1)S(1)}, bf16[320,512]{1,0:T(8,128)(2,1)S(1)}, u32[]{:S(2)}, u32[]{:S(2)}) collective-permute-start(bf16[320,512]{1,0:T(8,128)(2,1)S(1)} %pad_maximum_fusion.8), channel_id=1, source_target_pairs={{0,8},{1,9},{2,10},{3,11},{4,12},{5,13},{6,14},{7,15},{8,0},{9,1},... | collective-permute-start | bytes 983048 | tf_op jit(solution)/shard_map/ppermute | solution.py:981
  103.9 14.3 %collective-permute-done.23 = bf16[320,512]{1,0:T(8,128)(2,1)S(1)} collective-permute-done((bf16[320,512]{1,0:T(8,128)(2,1)S(1)}, bf16[320,512]{1,0:T(8,128)(2,1)S(1)}, u32[]{:S(2)}, u32[]{:S(2)}) %collective-permute-start.23) | collective-permute-done | bytes 327712 | tf_op jit(solution)/shard_map/ppermute | solution.py:981
  122.4 16.8 %rest_first.1 = (bf16[512,1536]{1,0:T(8,128)(2,1)}, f32[8,512]{1,0:T(8,128)}, bf16[512,512]{1,0:T(8,128)(2,1)}, f32[512,512]{1,0:T(8,128)}, f32[512,1024]{1,0:T(...) custom-call(s32[6]{0:T(128)} %stack.111.refs_0_, ...), custom_call_target="tpu_custom_call" | custom-call | flops 22000001024 | bytes 1048576 | tf_op jit(solution)/shard_map/rest_first/pallas_call | solution.py:483
  139.2 4.0 %collective-permute-done.28.refs_3_ = bf16[4,240,512]{2,1,0:T(8,128)(2,1)} collective-permute-done((bf16[4,240,512]{2,1,0:T(8,128)(2,1)}, bf16[4,240,512]{2,1,0:T(8,128)(2,1)}, u32[]{:S(2)}, u32[]{:S(2)}) %collective-permute-start.28) | collective-permute-done | bytes 983072 | tf_op jit(solution)/shard_map/ppermute | solution.py:981
  146.2 11.6 %collective-permute-done.32.refs_4_ = bf16[4,240,512]{2,1,0:T(8,128)(2,1)} collective-permute-done((bf16[4,240,512]{2,1,0:T(8,128)(2,1)}, bf16[4,240,512]{2,1,0:T(8,128)(2,1)}, u32[]{:S(2)}, u32[]{:S(2)}) %collective-permute-start.32) | collective-permute-done | bytes 983072 | tf_op jit(solution)/shard_map/ppermute | solution.py:981
  162.5 16.5 %first_second.1 = (bf16[512,2048]{1,0:T(8,128)(2,1)}, f32[512,512]{1,0:T(8,128)}, bf16[512,1536]{1,0:T(8,128)(2,1)}, f32[8,512]{1,0:T(8,128)}, bf16[512,512]{1,0...) custom-call(s32[6]{0:T(128)} %stack.111.refs_0_, ...), custom_call_target="tpu_custom_call" | custom-call | flops 22000001024 | bytes 1048576 | tf_op jit(solution)/shard_map/first_second/pallas_call | solution.py:483
  179.1 5.1 %collective-permute-start.40 = (bf16[4,320,512]{2,1,0:T(8,128)(2,1)S(1)}, bf16[4,320,512]{2,1,0:T(8,128)(2,1)}, u32[]{:S(2)}, u32[]{:S(2)}) collective-permute-start(bf16[4,320,512]{2,1,0:T(8,128)(2,1)S(1)} %collective-permute-done.37.refs_2_.refs_10_.refs_3_), channel_id=1, source_target_pairs={{0,1},{1,0},{2,3},{3,2},{4,5},{5,4},{6,7},{7,6},{8,9},{9,8},{10,11... | collective-permute-start | bytes 3932168 | tf_op jit(solution)/shard_map/ppermute | solution.py:981
  190.2 17.9 %turn.1 = (bf16[512,512]{1,0:T(8,128)(2,1)}, f32[1024,512]{1,0:T(8,128)}, f32[512,512]{1,0:T(8,128)}, f32[16,512]{1,0:T(8,128)}, bf16[16,128,512]{2,1,0:T(8,128)(2,1)}, /*index=5*/bf16[16,128,512]{2,1,0:T(8,128)(2,1)}) custom-call(s32[6]{0:T(128)} %stack.111.refs_0_, bf16[4,320,512]{2,1,0:T(8,128)(2,1)} %copy-done.7, bf16[4,320,512]{2,1,0:T(8,128)(2,1)} %copy-done.23, ...), custom_call_target="tpu_custom_call" | custom-call | flops 24199999488 | bytes 1048576 | tf_op jit(solution)/shard_map/turn/pallas_call | solution.py:483
  216.4 21.4 %mid.2 = (f32[512,512]{1,0:T(8,128)}, f32[16,512]{1,0:T(8,128)}, bf16[16,112,512]{2,1,0:T(8,128)(2,1)}, bf16[16,112,512]{2,1,0:T(8,128)(2,1)}) custom-call(s32[6]{0:T(128)} %stack.111.refs_0_, bf16[4,240,512]{2,1,0:T(8,128)(2,1)} %pad_maximum_fusion.2.refs_1_, bf16[4,240,512]{2,1,0:T(8,128)(2,1)} %collective-permute-done.29.refs_2_, ...), custom_call_target="tpu_custom_call" | custom-call | flops 23100000256 | bytes 1048576 | tf_op jit(solution)/shard_map/mid/pallas_call | solution.py:483
  238.8 3.0 collective-permute-done.44
  243.1 11.3 %early.2 = (f32[512,512]{1,0:T(8,128)}, f32[16,512]{1,0:T(8,128)}, bf16[16,128,512]{2,1,0:T(8,128)(2,1)}, bf16[16,128,512]{2,1,0:T(8,128)(2,1)}) custom-call(s32[6]{0:T(128)} %stack.111.refs_0_, bf16[4,240,512]{2,1,0:T(8,128)(2,1)} %pad_maximum_fusion.2.refs_1_, bf16[4,240,512]{2,1,0:T(8,128)(2,1)} %collective-permute-done.29.refs_2_, ...), custom_call_target="tpu_custom_call" | custom-call | flops 11000000512 | bytes 1048576 | tf_op jit(solution)/shard_map/early/pallas_call | solution.py:483
  258.0 3.2 collective-permute-done.48
  262.5 14.7 %late.1 = (f32[512,512]{1,0:T(8,128)}, f32[16,512]{1,0:T(8,128)}, bf16[16,160,512]{2,1,0:T(8,128)(2,1)}, bf16[16,160,512]{2,1,0:T(8,128)(2,1)}) custom-call(s32[6]{0:T(128)} %stack.111.refs_0_, bf16[4,240,512]{2,1,0:T(8,128)(2,1)} %copy-done.10, bf16[4,240,512]{2,1,0:T(8,128)(2,1)} %copy-done.26, bf16[4,240,512]{2,1,0:T(8,128)(2,1)} %copy-done.25, ...), custom_call_target="tpu_custom_call" | custom-call | flops 18699999232 | bytes 1048576 | tf_op jit(solution)/shard_map/late/pallas_call | solution.py:483
  281.1 3.1 collective-permute-start.53
  285.6 21.1 %mid.3 = (f32[512,512]{1,0:T(8,128)}, f32[16,512]{1,0:T(8,128)}, bf16[16,112,512]{2,1,0:T(8,128)(2,1)}, bf16[16,112,512]{2,1,0:T(8,128)(2,1)}) custom-call(s32[6]{0:T(128)} %stack.111.refs_0_, bf16[4,240,512]{2,1,0:T(8,128)(2,1)} %copy-done.10, bf16[4,240,512]{2,1,0:T(8,128)(2,1)} %copy-done.26, bf16[4,240,512]{2,1,0:T(8,128)(2,1)} %copy-done.25, ...), custom_call_target="tpu_custom_call" | custom-call | flops 23100000256 | bytes 1048576 | tf_op jit(solution)/shard_map/mid/pallas_call | solution.py:483
  315.2 12.3 %early.3 = (f32[512,512]{1,0:T(8,128)}, f32[16,512]{1,0:T(8,128)}, bf16[16,160,512]{2,1,0:T(8,128)(2,1)}, bf16[16,160,512]{2,1,0:T(8,128)(2,1)}) custom-call(s32[6]{0:T(128)} %stack.111.refs_0_, bf16[4,160,512]{2,1,0:T(8,128)(2,1)} %pad_maximum_fusion.3.refs_1_, bf16[4,160,512]{2,1,0:T(8,128)(2,1)} %collective-permute-done.7.refs_2_, ...), custom_call_target="tpu_custom_call" | custom-call | flops 14300000256 | bytes 1048576 | tf_op jit(solution)/shard_map/early/pallas_call | solution.py:483
  329.6 3.6 collective-permute-done.63
  339.9 8.3 %outputs.1 = (f32[2,512,1024]{2,1,0:T(8,128)}, f32[2,512,512]{2,1,0:T(8,128)}) custom-call(s32[6]{0:T(128)} %stack.111.refs_0_, s32[2]{0:T(128)} %bitcast.236, bf16[4,320,512]{2,1,0:T(8,128)(2,1)} %copy-done.7, bf16[4,320,512]{2,1,0:T(8,128)(2,1)} %copy-done.23, bf16[4,320,512]{2,1,0:T(8,128)(2,1)} %copy-done.24, ...), custom_call_target="tpu_custom_call" | custom-call | flops 9900000256 | bytes 1048576 | tf_op jit(solution)/shard_map/outputs/pallas_call | solution.py:483
  348.2 3.2 collective-permute-done.66
  354.9 2.9 collective-permute-start.69
  361.3 3.7 collective-permute-done.70
  371.3 4.5 %collective-permute-done.75 = bf16[160,512]{1,0:T(8,128)(2,1)S(1)} collective-permute-done((bf16[160,512]{1,0:T(8,128)(2,1)S(1)}, bf16[160,512]{1,0:T(8,128)(2,1)S(1)}, u32[]{:S(2)}, u32[]{:S(2)}) %collective-permute-start.75) | collective-permute-done | bytes 163872 | tf_op jit(solution)/shard_map/ppermute | solution.py:981
  375.8 5.4 %collective-permute-done.74 = bf16[160,512]{1,0:T(8,128)(2,1)S(1)} collective-permute-done((bf16[160,512]{1,0:T(8,128)(2,1)S(1)}, bf16[160,512]{1,0:T(8,128)(2,1)S(1)}, u32[]{:S(2)}, u32[]{:S(2)}) %collective-permute-start.74) | collective-permute-done | bytes 163872 | tf_op jit(solution)/shard_map/ppermute | solution.py:981
  385.1 3.2 grads.1
  (337 shorter events, 112.3 us)
Async XLA Ops:
  10.0 21.3 %collective-permute-start.5 = (bf16[320,1024]{1,0:T(8,128)(2,1)S(1)}, bf16[320,1024]{1,0:T(8,128)(2,1)S(1)}, u32[]{:S(2)}, u32[]{:S(2)}) collective-permute-start(bf16[320,1024]{1,0:T(8,128)(2,1)S(1)} %dynamic-slice_bitcast_fusion), channel_id=1, source_target_pairs={{0,16},{16,0},{1,17},{17,1},{2,18},{18,2},{3,19},{19,3},{4,20},{20... | collective-permute-start | bytes 1966088 | tf_op jit(solution)/shard_map/ppermute | solution.py:1051
  11.9 19.4 %collective-permute-start.4 = (bf16[240,512]{1,0:T(8,128)(2,1)S(1)}, bf16[240,512]{1,0:T(8,128)(2,1)S(1)}, u32[]{:S(2)}, u32[]{:S(2)}) collective-permute-start(bf16[240,512]{1,0:T(8,128)(2,1)S(1)} %dynamic-slice_bitcast_fusion.2), channel_id=1, source_target_pairs={{0,16},{1,17},{2,18},{3,19},{4,20},{5,21},{6,22},{7,23},{8,24},{9,... | collective-permute-start | bytes 737288 | tf_op jit(solution)/shard_map/ppermute | solution.py:981
  12.2 19.1 %collective-permute-start.1 = (bf16[160,512]{1,0:T(8,128)(2,1)S(1)}, bf16[160,512]{1,0:T(8,128)(2,1)S(1)}, u32[]{:S(2)}, u32[]{:S(2)}) collective-permute-start(bf16[160,512]{1,0:T(8,128)(2,1)S(1)} %get-tuple-element.190), channel_id=1, source_target_pairs={{0,4},{1,5},{2,6},{3,7},{4,0},{5,1},{6,2},{7,3},{8,12},{9,13},{10,... | collective-permute-start | bytes 491528 | tf_op jit(solution)/shard_map/ppermute | solution.py:981
  32.3 23.7 %collective-permute-start.6 = (bf16[4,160,512]{2,1,0:T(8,128)(2,1)}, bf16[4,160,512]{2,1,0:T(8,128)(2,1)}, u32[]{:S(2)}, u32[]{:S(2)}) collective-permute-start(bf16[4,160,512]{2,1,0:T(8,128)(2,1)} %pad_maximum_fusion.3.refs_1_), channel_id=1, source_target_pairs={{0,16},{1,3},{2,18},{3,1},{4,20},{5,7},{6,22},{7,5},{8,24},{9,11},... | collective-permute-start | bytes 1966088 | tf_op jit(solution)/shard_map/ppermute | solution.py:981
  33.8 22.3 %collective-permute-start.7 = (bf16[4,160,512]{2,1,0:T(8,128)(2,1)}, bf16[4,160,512]{2,1,0:T(8,128)(2,1)}, u32[]{:S(2)}, u32[]{:S(2)}) collective-permute-start(bf16[4,160,512]{2,1,0:T(8,128)(2,1)} %pad_maximum_fusion.3.refs_1_), channel_id=1, source_target_pairs={{0,2},{1,17},{2,0},{3,19},{4,6},{5,21},{6,4},{7,23},{8,10},{9,25},... | collective-permute-start | bytes 1966088 | tf_op jit(solution)/shard_map/ppermute | solution.py:981
  36.9 19.2 %collective-permute-start.9 = (bf16[240,512]{1,0:T(8,128)(2,1)S(1)}, bf16[240,512]{1,0:T(8,128)(2,1)S(1)}, u32[]{:S(2)}, u32[]{:S(2)}) collective-permute-start(bf16[240,512]{1,0:T(8,128)(2,1)S(1)} %get-tuple-element.198), channel_id=1, source_target_pairs={{0,8},{1,9},{2,10},{3,11},{4,12},{5,13},{6,14},{7,15},{8,0},{9,1},... | collective-permute-start | bytes 737288 | tf_op jit(solution)/shard_map/ppermute | solution.py:981
  70.6 24.8 %collective-permute-start.17 = (bf16[4,240,512]{2,1,0:T(8,128)(2,1)S(1)}, bf16[4,240,512]{2,1,0:T(8,128)(2,1)S(1)}, u32[]{:S(2)}, u32[]{:S(2)}) collective-permute-start(bf16[4,240,512]{2,1,0:T(8,128)(2,1)S(1)} %pad_maximum_fusion.1.refs_1_), channel_id=1, source_target_pairs={{0,16},{1,3},{2,18},{3,1},{4,20},{5,7},{6,22},{7,5},{8,24},{9,11},... | collective-permute-start | bytes 2949128 | tf_op jit(solution)/shard_map/ppermute | solution.py:981
  71.2 24.2 %collective-permute-start.18 = (bf16[4,240,512]{2,1,0:T(8,128)(2,1)S(1)}, bf16[4,240,512]{2,1,0:T(8,128)(2,1)S(1)}, u32[]{:S(2)}, u32[]{:S(2)}) collective-permute-start(bf16[4,240,512]{2,1,0:T(8,128)(2,1)S(1)} %pad_maximum_fusion.1.refs_1_), channel_id=1, source_target_pairs={{0,2},{1,17},{2,0},{3,19},{4,6},{5,21},{6,4},{7,23},{8,10},{9,25},... | collective-permute-start | bytes 2949128 | tf_op jit(solution)/shard_map/ppermute | solution.py:981
  75.1 20.3 %collective-permute-start.20 = (bf16[240,512]{1,0:T(8,128)(2,1)S(1)}, bf16[240,512]{1,0:T(8,128)(2,1)S(1)}, u32[]{:S(2)}, u32[]{:S(2)}) collective-permute-start(bf16[240,512]{1,0:T(8,128)(2,1)S(1)} %pad_maximum_fusion.12), channel_id=1, source_target_pairs={{0,8},{1,9},{2,10},{3,11},{4,12},{5,13},{6,14},{7,15},{8,0},{9,1},... | collective-permute-start | bytes 737288 | tf_op jit(solution)/shard_map/ppermute | solution.py:981
  76.2 19.2 %collective-permute-start.21 = (bf16[240,512]{1,0:T(8,128)(2,1)S(1)}, bf16[240,512]{1,0:T(8,128)(2,1)S(1)}, u32[]{:S(2)}, u32[]{:S(2)}) collective-permute-start(bf16[240,512]{1,0:T(8,128)(2,1)S(1)} %pad_maximum_fusion.12), channel_id=1, source_target_pairs={{0,12},{1,13},{2,14},{3,15},{4,8},{5,9},{6,10},{7,11},{8,4},{9,5},... | collective-permute-start | bytes 737288 | tf_op jit(solution)/shard_map/ppermute | solution.py:981
  95.4 22.8 %collective-permute-start.22 = (bf16[4,240,512]{2,1,0:T(8,128)(2,1)S(1)}, bf16[4,240,512]{2,1,0:T(8,128)(2,1)S(1)}, u32[]{:S(2)}, u32[]{:S(2)}) collective-permute-start(bf16[4,240,512]{2,1,0:T(8,128)(2,1)S(1)} %collective-permute-done.17.refs_3_), channel_id=1, source_target_pairs={{0,2},{1,17},{2,0},{3,19},{4,6},{5,21},{6,4},{7,23},{8,10},{9,25},... | collective-permute-start | bytes 2949128 | tf_op jit(solution)/shard_map/ppermute | solution.py:981
  96.9 21.4 %collective-permute-start.24 = (bf16[4,240,512]{2,1,0:T(8,128)(2,1)S(1)}, bf16[4,240,512]{2,1,0:T(8,128)(2,1)S(1)}, u32[]{:S(2)}, u32[]{:S(2)}) collective-permute-start(bf16[4,240,512]{2,1,0:T(8,128)(2,1)S(1)} %pad_maximum_fusion.1.refs_1_), channel_id=1, source_target_pairs={{0,1},{1,0},{2,3},{3,2},{4,5},{5,4},{6,7},{7,6},{8,9},{9,8},{10,11... | collective-permute-start | bytes 2949128 | tf_op jit(solution)/shard_map/ppermute | solution.py:981
  96.9 21.4 %collective-permute-start.25 = (bf16[4,240,512]{2,1,0:T(8,128)(2,1)S(1)}, bf16[4,240,512]{2,1,0:T(8,128)(2,1)S(1)}, u32[]{:S(2)}, u32[]{:S(2)}) collective-permute-start(bf16[4,240,512]{2,1,0:T(8,128)(2,1)S(1)} %collective-permute-done.18.refs_2_), channel_id=1, source_target_pairs={{0,1},{1,0},{2,3},{3,2},{4,5},{5,4},{6,7},{7,6},{8,9},{9,8},{10,11... | collective-permute-start | bytes 2949128 | tf_op jit(solution)/shard_map/ppermute | solution.py:981
  97.4 20.9 %collective-permute-start.26 = (bf16[4,240,512]{2,1,0:T(8,128)(2,1)S(1)}, bf16[4,240,512]{2,1,0:T(8,128)(2,1)S(1)}, u32[]{:S(2)}, u32[]{:S(2)}) collective-permute-start(bf16[4,240,512]{2,1,0:T(8,128)(2,1)S(1)} %collective-permute-done.17.refs_3_), channel_id=1, source_target_pairs={{0,1},{1,0},{2,3},{3,2},{4,5},{5,4},{6,7},{7,6},{8,9},{9,8},{10,11... | collective-permute-start | bytes 2949128 | tf_op jit(solution)/shard_map/ppermute | solution.py:981
  97.4 20.9 %collective-permute-start.23 = (bf16[320,512]{1,0:T(8,128)(2,1)S(1)}, bf16[320,512]{1,0:T(8,128)(2,1)S(1)}, u32[]{:S(2)}, u32[]{:S(2)}) collective-permute-start(bf16[320,512]{1,0:T(8,128)(2,1)S(1)} %pad_maximum_fusion.8), channel_id=1, source_target_pairs={{0,8},{1,9},{2,10},{3,11},{4,12},{5,13},{6,14},{7,15},{8,0},{9,1},... | collective-permute-start | bytes 983048 | tf_op jit(solution)/shard_map/ppermute | solution.py:981
  118.4 24.9 %collective-permute-start.28 = (bf16[4,240,512]{2,1,0:T(8,128)(2,1)}, bf16[4,240,512]{2,1,0:T(8,128)(2,1)}, u32[]{:S(2)}, u32[]{:S(2)}) collective-permute-start(bf16[4,240,512]{2,1,0:T(8,128)(2,1)} %pad_maximum_fusion.2.refs_1_), channel_id=1, source_target_pairs={{0,16},{1,3},{2,18},{3,1},{4,20},{5,7},{6,22},{7,5},{8,24},{9,11},... | collective-permute-start | bytes 2949128 | tf_op jit(solution)/shard_map/ppermute | solution.py:981
  120.0 23.3 %collective-permute-start.29 = (bf16[4,240,512]{2,1,0:T(8,128)(2,1)}, bf16[4,240,512]{2,1,0:T(8,128)(2,1)}, u32[]{:S(2)}, u32[]{:S(2)}) collective-permute-start(bf16[4,240,512]{2,1,0:T(8,128)(2,1)} %pad_maximum_fusion.2.refs_1_), channel_id=1, source_target_pairs={{0,2},{1,17},{2,0},{3,19},{4,6},{5,21},{6,4},{7,23},{8,10},{9,25},... | collective-permute-start | bytes 2949128 | tf_op jit(solution)/shard_map/ppermute | solution.py:981
  121.0 22.3 %collective-permute-start.30 = (bf16[320,512]{1,0:T(8,128)(2,1)S(1)}, bf16[320,512]{1,0:T(8,128)(2,1)S(1)}, u32[]{:S(2)}, u32[]{:S(2)}) collective-permute-start(bf16[320,512]{1,0:T(8,128)(2,1)S(1)} %pad_maximum_fusion.8), channel_id=1, source_target_pairs={{0,4},{1,5},{2,6},{3,7},{4,0},{5,1},{6,2},{7,3},{8,12},{9,13},{10,... | collective-permute-start | bytes 983048 | tf_op jit(solution)/shard_map/ppermute | solution.py:981
  121.0 22.3 %collective-permute-start.31 = (bf16[320,512]{1,0:T(8,128)(2,1)S(1)}, bf16[320,512]{1,0:T(8,128)(2,1)S(1)}, u32[]{:S(2)}, u32[]{:S(2)}) collective-permute-start(bf16[320,512]{1,0:T(8,128)(2,1)S(1)} %pad_maximum_fusion.8), channel_id=1, source_target_pairs={{0,12},{1,13},{2,14},{3,15},{4,8},{5,9},{6,10},{7,11},{8,4},{9,5},... | collective-permute-start | bytes 983048 | tf_op jit(solution)/shard_map/ppermute | solution.py:981
  158.7 20.3 %collective-permute-start.37 = (bf16[4,320,512]{2,1,0:T(8,128)(2,1)S(1)}, bf16[4,320,512]{2,1,0:T(8,128)(2,1)S(1)}, u32[]{:S(2)}, u32[]{:S(2)}) collective-permute-start(bf16[4,320,512]{2,1,0:T(8,128)(2,1)S(1)} %pad_maximum_fusion.refs_1_.refs_9_.refs_2_), channel_id=1, source_target_pairs={{0,2},{1,17},{2,0},{3,19},{4,6},{5,21},{6,4},{7,23},{8,10},{9,25},... | collective-permute-start | bytes 3932168 | tf_op jit(solution)/shard_map/ppermute | solution.py:981
  159.0 20.0 %collective-permute-start.38 = (bf16[4,320,512]{2,1,0:T(8,128)(2,1)S(1)}, bf16[4,320,512]{2,1,0:T(8,128)(2,1)S(1)}, u32[]{:S(2)}, u32[]{:S(2)}) collective-permute-start(bf16[4,320,512]{2,1,0:T(8,128)(2,1)S(1)} %pad_maximum_fusion.refs_1_.refs_9_.refs_2_), channel_id=1, source_target_pairs={{0,1},{1,0},{2,3},{3,2},{4,5},{5,4},{6,7},{7,6},{8,9},{9,8},{10,11... | collective-permute-start | bytes 3932168 | tf_op jit(solution)/shard_map/ppermute | solution.py:981
  160.4 18.6 %collective-permute-start.39 = (bf16[192,1024]{1,0:T(8,128)(2,1)S(1)}, bf16[192,1024]{1,0:T(8,128)(2,1)S(1)}, u32[]{:S(2)}, u32[]{:S(2)}) collective-permute-start(bf16[192,1024]{1,0:T(8,128)(2,1)S(1)} %dynamic-slice_bitcast_fusion.1), channel_id=1, source_target_pairs={{0,16},{16,0},{1,17},{17,1},{2,18},{18,2},{3,19},{19,3},{4,20},{20... | collective-permute-start | bytes 1179656 | tf_op jit(solution)/shard_map/ppermute | solution.py:1051
  209.7 28.1 %collective-permute-start.43 = (bf16[512,512]{1,0:T(8,128)(2,1)S(1)}, bf16[512,512]{1,0:T(8,128)(2,1)S(1)}, u32[]{:S(2)}, u32[]{:S(2)}) collective-permute-start(bf16[512,512]{1,0:T(8,128)(2,1)S(1)} %broadcast_select_fusion), channel_id=1, source_target_pairs={{0,16},{16,0},{1,17},{17,1},{2,18},{18,2},{3,19},{19,3},{4,20},{20... | collective-permute-start | bytes 1572872 | tf_op jit(solution)/shard_map/ppermute | solution.py:1051
  214.8 23.0 %collective-permute-start.42 = (bf16[8,128,512]{2,1,0:T(8,128)(2,1)S(1)}, bf16[8,128,512]{2,1,0:T(8,128)(2,1)S(1)}, u32[]{:S(2)}, u32[]{:S(2)}) collective-permute-start(bf16[8,128,512]{2,1,0:T(8,128)(2,1)S(1)} %get-tuple-element.410), channel_id=1, source_target_pairs={{0,16},{1,3},{2,18},{3,1},{4,20},{5,7},{6,22},{7,5},{8,24},{9,11},... | collective-permute-start | bytes 3145736 | tf_op jit(solution)/shard_map/ppermute | solution.py:981
  257.3 19.9 %collective-permute-start.47 = (bf16[4,112,512]{2,1,0:T(8,128)(2,1)S(1)}, bf16[4,112,512]{2,1,0:T(8,128)(2,1)S(1)}, u32[]{:S(2)}, u32[]{:S(2)}) collective-permute-start(bf16[4,112,512]{2,1,0:T(8,128)(2,1)S(1)} %get-tuple-element.427), channel_id=1, source_target_pairs={{0,2},{1,17},{2,0},{3,19},{4,6},{5,21},{6,4},{7,23},{8,10},{9,25},... | collective-permute-start | bytes 1376264 | tf_op jit(solution)/shard_map/ppermute | solution.py:981
  277.9 29.0 %collective-permute-start.50 = (bf16[4,128,512]{2,1,0:T(8,128)(2,1)S(1)}, bf16[4,128,512]{2,1,0:T(8,128)(2,1)S(1)}, u32[]{:S(2)}, u32[]{:S(2)}) collective-permute-start(bf16[4,128,512]{2,1,0:T(8,128)(2,1)S(1)} %get-tuple-element.421), channel_id=1, source_target_pairs={{0,2},{1,17},{2,0},{3,19},{4,6},{5,21},{6,4},{7,23},{8,10},{9,25},... | collective-permute-start | bytes 1572872 | tf_op jit(solution)/shard_map/ppermute | solution.py:981
  279.5 27.2 %collective-permute-start.55 = (bf16[240,512]{1,0:T(8,128)(2,1)S(1)}, bf16[240,512]{1,0:T(8,128)(2,1)S(1)}, u32[]{:S(2)}, u32[]{:S(2)}) collective-permute-start(bf16[240,512]{1,0:T(8,128)(2,1)S(1)} %pad_maximum_fusion.15), channel_id=1, source_target_pairs={{0,12},{1,13},{2,14},{3,15},{4,8},{5,9},{6,10},{7,11},{8,4},{9,5},... | collective-permute-start | bytes 737288 | tf_op jit(solution)/shard_map/ppermute | solution.py:981
  281.0 25.7 %collective-permute-start.54 = (bf16[240,512]{1,0:T(8,128)(2,1)S(1)}, bf16[240,512]{1,0:T(8,128)(2,1)S(1)}, u32[]{:S(2)}, u32[]{:S(2)}) collective-permute-start(bf16[240,512]{1,0:T(8,128)(2,1)S(1)} %pad_maximum_fusion.14), channel_id=1, source_target_pairs={{0,8},{1,9},{2,10},{3,11},{4,12},{5,13},{6,14},{7,15},{8,0},{9,1},... | collective-permute-start | bytes 737288 | tf_op jit(solution)/shard_map/ppermute | solution.py:981
  281.1 25.6 %collective-permute-start.53 = (bf16[240,512]{1,0:T(8,128)(2,1)S(1)}, bf16[240,512]{1,0:T(8,128)(2,1)S(1)}, u32[]{:S(2)}, u32[]{:S(2)}) collective-permute-start(bf16[240,512]{1,0:T(8,128)(2,1)S(1)} %pad_maximum_fusion.13), channel_id=1, source_target_pairs={{0,4},{1,5},{2,6},{3,7},{4,0},{5,1},{6,2},{7,3},{8,12},{9,13},{10,... | collective-permute-start | bytes 737288 | tf_op jit(solution)/shard_map/ppermute | solution.py:981
  285.0 21.9 %collective-permute-start.52 = (bf16[8,160,512]{2,1,0:T(8,128)(2,1)S(1)}, bf16[8,160,512]{2,1,0:T(8,128)(2,1)S(1)}, u32[]{:S(2)}, u32[]{:S(2)}) collective-permute-start(bf16[8,160,512]{2,1,0:T(8,128)(2,1)S(1)} %get-tuple-element.407), channel_id=1, source_target_pairs={{0,16},{1,3},{2,18},{3,1},{4,20},{5,7},{6,22},{7,5},{8,24},{9,11},... | collective-permute-start | bytes 3932168 | tf_op jit(solution)/shard_map/ppermute | solution.py:981
  307.4 20.3 %collective-permute-start.57 = (bf16[4,160,512]{2,1,0:T(8,128)(2,1)S(1)}, bf16[4,160,512]{2,1,0:T(8,128)(2,1)S(1)}, u32[]{:S(2)}, u32[]{:S(2)}) collective-permute-start(bf16[4,160,512]{2,1,0:T(8,128)(2,1)S(1)} %get-tuple-element.419), channel_id=1, source_target_pairs={{0,2},{1,17},{2,0},{3,19},{4,6},{5,21},{6,4},{7,23},{8,10},{9,25},... | collective-permute-start | bytes 1966088 | tf_op jit(solution)/shard_map/ppermute | solution.py:981
  328.4 23.1 %collective-permute-start.62 = (bf16[4,112,512]{2,1,0:T(8,128)(2,1)S(1)}, bf16[4,112,512]{2,1,0:T(8,128)(2,1)S(1)}, u32[]{:S(2)}, u32[]{:S(2)}) collective-permute-start(bf16[4,112,512]{2,1,0:T(8,128)(2,1)S(1)} %get-tuple-element.425), channel_id=1, source_target_pairs={{0,2},{1,17},{2,0},{3,19},{4,6},{5,21},{6,4},{7,23},{8,10},{9,25},... | collective-permute-start | bytes 1376264 | tf_op jit(solution)/shard_map/ppermute | solution.py:981
  (86 other events, 987.2 us)

commit v5 on v4

--- a/solution.py
+++ b/solution.py
@@ -446,7 +446,7 @@
         self.copy.wait()
 
 
-def run(body, micros, ins, outs, scratch):
+def run(body, micros, ins, outs, scratch, room=55):
     flat, held = [], []
     for value, space in ins.values():
         flat += [(array, ANY if space is LATE else space) for array in (value if isinstance(value, list) else [value])]
@@ -487,7 +487,7 @@
         out_specs=[pl.BlockSpec(memory_space=ANY if space is LATE else space) for _, _, space in outs.values()],
         scratch_shapes=[pltpu.VMEM(shape, dtype) for shape, dtype in [*scratch.values(), *held]]
         + [pltpu.SemaphoreType.DMA((8 + len(held),))],
-        compiler_params=pltpu.CompilerParams(vmem_limit_bytes=55 * 2**20),
+        compiler_params=pltpu.CompilerParams(vmem_limit_bytes=room * 2**20),
         cost_estimate=pl.CostEstimate(flops=int(micros * 1.1e9), bytes_accessed=2**20, transcendentals=0),
         name=body.__name__,
     )(*[array for array, _ in flat])
@@ -671,6 +671,7 @@
             send=((16, rows, 512), BF, ANY),
         ),
         FEED_SCRATCH | HEAD_SCRATCH | dict(hid=((512, FF), BF), x4=(ROWS, F32)),
+        room=52,
     )
 
 
@@ -723,6 +724,7 @@
             send=((16, rows, 512), BF, ANY),
         ),
         FEED_SCRATCH | HEAD_SCRATCH | dict(gh=WH),
+        room=52,
     )
 
 
@@ -793,6 +795,7 @@
             dq=((128, 512), F32),
             kt=((256, 512), BF),
         ),
+        room=52,
     )
 
 
@@ -869,6 +872,7 @@
             send=((16, rows, 512), BF, ANY),
         ),
         scratch,
+        room=55 if stem is not None else 52,
     )
 
 

time: 399 us -> 394 us (0.987)
  Pallas kernels: 153 us -> 149 us
  transfers between devices with their start and end apart: 78 -> 78, of which waited for: 25 -> 26; matrix products, arithmetic and copies ran while one was open for 6% -> 6% of each run, Pallas kernels for 34% -> 34%
where the time goes in v5:
time: 394 us; the launch traced here: 390 us
  Pallas kernels  149 us (38%)
  waiting for transfers between devices  114 us (29%)
  starting transfers between devices  86.6 us (22%)
  other arithmetic  18 us (5%)
  local copies, waits for them, and re-layouts  16.1 us (4%)
  between operations  6.48 us (2%)
    pallas_call x11, Pallas kernels, run(): pl.pallas_call(kernel, out_shape=[jax.ShapeDtypeStruct(shape, dtype) for...  149 us
    ppermute x74, waiting for transfers between devices, across(): return lax.ppermute(value, BOTH, permutation(target))  114 us
    ppermute x74, starting transfers between devices, across(): return lax.ppermute(value, BOTH, permutation(target))  81.4 us
  transfers between devices with their start and end apart: 78, of which 26 were waited for; matrix products, arithmetic and copies ran while one was open for 6% of the time, Pallas kernels for 34%

profile of v5, /device:TPU:0, one launch (start us, length us, event | category | flops | bytes accessed | tf_op | source)
XLA Modules:
  0.0 390.4 jit_solution(16506669200913923157)
XLA Ops:
  3.4 3.0 collective-permute-start
  16.6 14.6 %collective-permute-done.4 = bf16[240,512]{1,0:T(8,128)(2,1)S(1)} collective-permute-done((bf16[240,512]{1,0:T(8,128)(2,1)S(1)}, bf16[240,512]{1,0:T(8,128)(2,1)S(1)}, u32[]{:S(2)}, u32[]{:S(2)}) %collective-permute-start.4) | collective-permute-done | bytes 245792 | tf_op jit(solution)/shard_map/ppermute | solution.py:985
  39.6 4.1 %collective-permute-done.8 = bf16[240,512]{1,0:T(8,128)(2,1)S(1)} collective-permute-done((bf16[240,512]{1,0:T(8,128)(2,1)S(1)}, bf16[240,512]{1,0:T(8,128)(2,1)S(1)}, u32[]{:S(2)}, u32[]{:S(2)}) %collective-permute-start.8) | collective-permute-done | bytes 245792 | tf_op jit(solution)/shard_map/ppermute | solution.py:985
  43.8 12.2 %collective-permute-done.9 = bf16[240,512]{1,0:T(8,128)(2,1)S(1)} collective-permute-done((bf16[240,512]{1,0:T(8,128)(2,1)S(1)}, bf16[240,512]{1,0:T(8,128)(2,1)S(1)}, u32[]{:S(2)}, u32[]{:S(2)}) %collective-permute-start.9) | collective-permute-done | bytes 245792 | tf_op jit(solution)/shard_map/ppermute | solution.py:985
  62.9 5.6 %collective-permute-done.11.refs_4_ = bf16[4,160,512]{2,1,0:T(8,128)(2,1)} collective-permute-done((bf16[4,160,512]{2,1,0:T(8,128)(2,1)}, bf16[4,160,512]{2,1,0:T(8,128)(2,1)}, u32[]{:S(2)}, u32[]{:S(2)}) %collective-permute-start.11) | collective-permute-done | bytes 655392 | tf_op jit(solution)/shard_map/ppermute | solution.py:985
  71.8 3.2 collective-permute-start.19
  77.6 9.4 %stem_feed.1 = (f32[2,16,512]{2,1,0:T(8,128)}, f32[512,256]{1,0:T(8,128)}, bf16[256,512]{1,0:T(8,128)(2,1)}, bf16[512,512]{1,0:T(8,128)(2,1)}, bf16[512,2048]{1,0:T(8,128)(2,1)}, /*index=5*/f32[512,512]{1,0:T(8,128)}) custom-call(s32[6]{0:T(128)} %stack.111.refs_0_, bf16[4,160,512]{2,1,0:T(8,128)(2,1)} %pad_maximum_fusion.3.refs_1_, ...), custom_call_target="tpu_custom_call" | custom-call | flops 9900000256 | bytes 1048576 | tf_op jit(solution)/shard_map/stem_feed/pallas_call | solution.py:483
  86.9 8.4 %collective-permute-done.20 = bf16[240,512]{1,0:T(8,128)(2,1)S(1)} collective-permute-done((bf16[240,512]{1,0:T(8,128)(2,1)S(1)}, bf16[240,512]{1,0:T(8,128)(2,1)S(1)}, u32[]{:S(2)}, u32[]{:S(2)}) %collective-permute-start.20) | collective-permute-done | bytes 245792 | tf_op jit(solution)/shard_map/ppermute | solution.py:985
  97.4 5.5 %collective-permute-start.23 = (bf16[320,512]{1,0:T(8,128)(2,1)S(1)}, bf16[320,512]{1,0:T(8,128)(2,1)S(1)}, u32[]{:S(2)}, u32[]{:S(2)}) collective-permute-start(bf16[320,512]{1,0:T(8,128)(2,1)S(1)} %pad_maximum_fusion.8), channel_id=1, source_target_pairs={{0,8},{1,9},{2,10},{3,11},{4,12},{5,13},{6,14},{7,15},{8,0},{9,1},... | collective-permute-start | bytes 983048 | tf_op jit(solution)/shard_map/ppermute | solution.py:985
  103.0 15.3 %collective-permute-done.23 = bf16[320,512]{1,0:T(8,128)(2,1)S(1)} collective-permute-done((bf16[320,512]{1,0:T(8,128)(2,1)S(1)}, bf16[320,512]{1,0:T(8,128)(2,1)S(1)}, u32[]{:S(2)}, u32[]{:S(2)}) %collective-permute-start.23) | collective-permute-done | bytes 327712 | tf_op jit(solution)/shard_map/ppermute | solution.py:985
  122.4 16.9 %rest_first.1 = (bf16[512,1536]{1,0:T(8,128)(2,1)}, f32[8,512]{1,0:T(8,128)}, bf16[512,512]{1,0:T(8,128)(2,1)}, f32[512,512]{1,0:T(8,128)}, f32[512,1024]{1,0:T(...) custom-call(s32[6]{0:T(128)} %stack.111.refs_0_, ...), custom_call_target="tpu_custom_call" | custom-call | flops 22000001024 | bytes 1048576 | tf_op jit(solution)/shard_map/rest_first/pallas_call | solution.py:483
  139.3 3.7 collective-permute-done.28.refs_3_
  147.0 10.5 %collective-permute-done.32.refs_4_ = bf16[4,240,512]{2,1,0:T(8,128)(2,1)} collective-permute-done((bf16[4,240,512]{2,1,0:T(8,128)(2,1)}, bf16[4,240,512]{2,1,0:T(8,128)(2,1)}, u32[]{:S(2)}, u32[]{:S(2)}) %collective-permute-start.32) | collective-permute-done | bytes 983072 | tf_op jit(solution)/shard_map/ppermute | solution.py:985
  161.4 16.5 %first_second.1 = (bf16[512,2048]{1,0:T(8,128)(2,1)}, f32[512,512]{1,0:T(8,128)}, bf16[512,1536]{1,0:T(8,128)(2,1)}, f32[8,512]{1,0:T(8,128)}, bf16[512,512]{1,0...) custom-call(s32[6]{0:T(128)} %stack.111.refs_0_, ...), custom_call_target="tpu_custom_call" | custom-call | flops 22000001024 | bytes 1048576 | tf_op jit(solution)/shard_map/first_second/pallas_call | solution.py:483
  177.9 5.2 %collective-permute-start.40 = (bf16[4,320,512]{2,1,0:T(8,128)(2,1)S(1)}, bf16[4,320,512]{2,1,0:T(8,128)(2,1)}, u32[]{:S(2)}, u32[]{:S(2)}) collective-permute-start(bf16[4,320,512]{2,1,0:T(8,128)(2,1)S(1)} %collective-permute-done.37.refs_2_.refs_10_.refs_3_), channel_id=1, source_target_pairs={{0,1},{1,0},{2,3},{3,2},{4,5},{5,4},{6,7},{7,6},{8,9},{9,8},{10,11... | collective-permute-start | bytes 3932168 | tf_op jit(solution)/shard_map/ppermute | solution.py:985
  188.5 16.1 %turn.1 = (bf16[512,512]{1,0:T(8,128)(2,1)S(1)}, f32[1024,512]{1,0:T(8,128)}, f32[512,512]{1,0:T(8,128)}, f32[16,512]{1,0:T(8,128)S(1)}, bf16[16,128,512]{2,1,0:T(8,128)(2,1)}, /*index=5*/bf16[16,128,512]{2,1,0:T(8,128)(2,1)}) custom-call(s32[6]{0:T(128)S(1)} %copy-done.8, bf16[4,320,512]{2,1,0:T(8,128)(2,1)} %copy-done.24, bf16[4,320,512]{2,1,0:T(8,128)(2,1)} %copy-done.45, ...), custom_call_target="tpu_custom_call" | custom-call | flops 24199999488 | bytes 1048576 | tf_op jit(solution)/shard_map/turn/pallas_call | solution.py:483
  213.0 20.7 %mid.2 = (f32[512,512]{1,0:T(8,128)}, f32[16,512]{1,0:T(8,128)S(1)}, bf16[16,112,512]{2,1,0:T(8,128)(2,1)}, bf16[16,112,512]{2,1,0:T(8,128)(2,1)}) custom-call(s32[6]{0:T(128)S(1)} %copy-done.8, bf16[4,240,512]{2,1,0:T(8,128)(2,1)S(1)} %copy-done.5, bf16[4,240,512]{2,1,0:T(8,128)(2,1)} %collective-permute-done.29.refs_2_, ...), custom_call_target="tpu_custom_call" | custom-call | flops 23100000256 | bytes 1048576 | tf_op jit(solution)/shard_map/mid/pallas_call | solution.py:483
  234.8 3.0 collective-permute-done.44
  239.0 11.4 %early.2 = (f32[512,512]{1,0:T(8,128)}, f32[16,512]{1,0:T(8,128)S(1)}, bf16[16,128,512]{2,1,0:T(8,128)(2,1)}, bf16[16,128,512]{2,1,0:T(8,128)(2,1)}) custom-call(s32[6]{0:T(128)S(1)} %copy-done.8, bf16[4,240,512]{2,1,0:T(8,128)(2,1)S(1)} %copy-done.5, bf16[4,240,512]{2,1,0:T(8,128)(2,1)} %collective-permute-done.29.refs_2_, ...), custom_call_target="tpu_custom_call" | custom-call | flops 11000000512 | bytes 1048576 | tf_op jit(solution)/shard_map/early/pallas_call | solution.py:483
  254.0 3.2 collective-permute-done.48
  258.4 13.6 %late.1 = (f32[512,512]{1,0:T(8,128)}, f32[16,512]{1,0:T(8,128)S(1)}, bf16[16,160,512]{2,1,0:T(8,128)(2,1)}, bf16[16,160,512]{2,1,0:T(8,128)(2,1)}) custom-call(s32[6]{0:T(128)S(1)} %copy-done.8, bf16[4,240,512]{2,1,0:T(8,128)(2,1)} %copy-done.2, bf16[4,240,512]{2,1,0:T(8,128)(2,1)} %copy-done.48, bf16[4,240,512]{2,1,0:T(8,128)(2,1)} %copy-done.47, ...), custom_call_target="tpu_custom_call" | custom-call | flops 18699999232 | bytes 1048576 | tf_op jit(solution)/shard_map/late/pallas_call | solution.py:483
  275.9 3.1 collective-permute-start.53
  281.3 20.7 %mid.3 = (f32[512,512]{1,0:T(8,128)}, f32[16,512]{1,0:T(8,128)S(1)}, bf16[16,112,512]{2,1,0:T(8,128)(2,1)}, bf16[16,112,512]{2,1,0:T(8,128)(2,1)}) custom-call(s32[6]{0:T(128)S(1)} %copy-done.8, bf16[4,240,512]{2,1,0:T(8,128)(2,1)S(1)} %copy-done.3, bf16[4,240,512]{2,1,0:T(8,128)(2,1)} %copy-done.48, bf16[4,240,512]{2,1,0:T(8,128)(2,1)} %copy-done.47, ...), custom_call_target="tpu_custom_call" | custom-call | flops 23100000256 | bytes 1048576 | tf_op jit(solution)/shard_map/mid/pallas_call | solution.py:483
  310.0 12.3 %early.3 = (f32[512,512]{1,0:T(8,128)}, f32[16,512]{1,0:T(8,128)}, bf16[16,160,512]{2,1,0:T(8,128)(2,1)}, bf16[16,160,512]{2,1,0:T(8,128)(2,1)}) custom-call(s32[6]{0:T(128)} %stack.111.refs_0_, bf16[4,160,512]{2,1,0:T(8,128)(2,1)} %pad_maximum_fusion.3.refs_1_, bf16[4,160,512]{2,1,0:T(8,128)(2,1)} %collective-permute-done.7.refs_2_, ...), custom_call_target="tpu_custom_call" | custom-call | flops 14300000256 | bytes 1048576 | tf_op jit(solution)/shard_map/early/pallas_call | solution.py:483
  324.2 3.7 collective-permute-done.63
  334.1 8.5 %outputs.1 = (f32[2,512,1024]{2,1,0:T(8,128)}, f32[2,512,512]{2,1,0:T(8,128)}) custom-call(s32[6]{0:T(128)} %stack.111.refs_0_, s32[2]{0:T(128)} %bitcast.236, bf16[4,320,512]{2,1,0:T(8,128)(2,1)} %copy-done.24, bf16[4,320,512]{2,1,0:T(8,128)(2,1)} %copy-done.45, bf16[4,320,512]{2,1,0:T(8,128)(2,1)} %copy-done.46, ...), custom_call_target="tpu_custom_call" | custom-call | flops 9900000256 | bytes 1048576 | tf_op jit(solution)/shard_map/outputs/pallas_call | solution.py:483
  342.5 3.4 collective-permute-done.66
  349.4 2.9 collective-permute-start.69
  355.8 3.7 collective-permute-done.70
  365.8 4.6 %collective-permute-done.75 = bf16[160,512]{1,0:T(8,128)(2,1)S(1)} collective-permute-done((bf16[160,512]{1,0:T(8,128)(2,1)S(1)}, bf16[160,512]{1,0:T(8,128)(2,1)S(1)}, u32[]{:S(2)}, u32[]{:S(2)}) %collective-permute-start.75) | collective-permute-done | bytes 163872 | tf_op jit(solution)/shard_map/ppermute | solution.py:985
  370.4 5.4 %collective-permute-done.74 = bf16[160,512]{1,0:T(8,128)(2,1)S(1)} collective-permute-done((bf16[160,512]{1,0:T(8,128)(2,1)S(1)}, bf16[160,512]{1,0:T(8,128)(2,1)S(1)}, u32[]{:S(2)}, u32[]{:S(2)}) %collective-permute-start.74) | collective-permute-done | bytes 163872 | tf_op jit(solution)/shard_map/ppermute | solution.py:985
  380.0 3.2 grads.1
  (375 shorter events, 110.3 us)
Async XLA Ops:
  10.0 21.3 %collective-permute-start.5 = (bf16[320,1024]{1,0:T(8,128)(2,1)S(1)}, bf16[320,1024]{1,0:T(8,128)(2,1)S(1)}, u32[]{:S(2)}, u32[]{:S(2)}) collective-permute-start(bf16[320,1024]{1,0:T(8,128)(2,1)S(1)} %dynamic-slice_bitcast_fusion), channel_id=1, source_target_pairs={{0,16},{16,0},{1,17},{17,1},{2,18},{18,2},{3,19},{19,3},{4,20},{20... | collective-permute-start | bytes 1966088 | tf_op jit(solution)/shard_map/ppermute | solution.py:1055
  11.9 19.4 %collective-permute-start.4 = (bf16[240,512]{1,0:T(8,128)(2,1)S(1)}, bf16[240,512]{1,0:T(8,128)(2,1)S(1)}, u32[]{:S(2)}, u32[]{:S(2)}) collective-permute-start(bf16[240,512]{1,0:T(8,128)(2,1)S(1)} %dynamic-slice_bitcast_fusion.2), channel_id=1, source_target_pairs={{0,16},{1,17},{2,18},{3,19},{4,20},{5,21},{6,22},{7,23},{8,24},{9,... | collective-permute-start | bytes 737288 | tf_op jit(solution)/shard_map/ppermute | solution.py:985
  12.2 19.1 %collective-permute-start.1 = (bf16[160,512]{1,0:T(8,128)(2,1)S(1)}, bf16[160,512]{1,0:T(8,128)(2,1)S(1)}, u32[]{:S(2)}, u32[]{:S(2)}) collective-permute-start(bf16[160,512]{1,0:T(8,128)(2,1)S(1)} %get-tuple-element.190), channel_id=1, source_target_pairs={{0,4},{1,5},{2,6},{3,7},{4,0},{5,1},{6,2},{7,3},{8,12},{9,13},{10,... | collective-permute-start | bytes 491528 | tf_op jit(solution)/shard_map/ppermute | solution.py:985
  32.3 23.7 %collective-permute-start.6 = (bf16[4,160,512]{2,1,0:T(8,128)(2,1)}, bf16[4,160,512]{2,1,0:T(8,128)(2,1)}, u32[]{:S(2)}, u32[]{:S(2)}) collective-permute-start(bf16[4,160,512]{2,1,0:T(8,128)(2,1)} %pad_maximum_fusion.3.refs_1_), channel_id=1, source_target_pairs={{0,16},{1,3},{2,18},{3,1},{4,20},{5,7},{6,22},{7,5},{8,24},{9,11},... | collective-permute-start | bytes 1966088 | tf_op jit(solution)/shard_map/ppermute | solution.py:985
  33.7 22.3 %collective-permute-start.7 = (bf16[4,160,512]{2,1,0:T(8,128)(2,1)}, bf16[4,160,512]{2,1,0:T(8,128)(2,1)}, u32[]{:S(2)}, u32[]{:S(2)}) collective-permute-start(bf16[4,160,512]{2,1,0:T(8,128)(2,1)} %pad_maximum_fusion.3.refs_1_), channel_id=1, source_target_pairs={{0,2},{1,17},{2,0},{3,19},{4,6},{5,21},{6,4},{7,23},{8,10},{9,25},... | collective-permute-start | bytes 1966088 | tf_op jit(solution)/shard_map/ppermute | solution.py:985
  36.8 19.2 %collective-permute-start.9 = (bf16[240,512]{1,0:T(8,128)(2,1)S(1)}, bf16[240,512]{1,0:T(8,128)(2,1)S(1)}, u32[]{:S(2)}, u32[]{:S(2)}) collective-permute-start(bf16[240,512]{1,0:T(8,128)(2,1)S(1)} %get-tuple-element.198), channel_id=1, source_target_pairs={{0,8},{1,9},{2,10},{3,11},{4,12},{5,13},{6,14},{7,15},{8,0},{9,1},... | collective-permute-start | bytes 737288 | tf_op jit(solution)/shard_map/ppermute | solution.py:985
  70.5 24.9 %collective-permute-start.17 = (bf16[4,240,512]{2,1,0:T(8,128)(2,1)S(1)}, bf16[4,240,512]{2,1,0:T(8,128)(2,1)S(1)}, u32[]{:S(2)}, u32[]{:S(2)}) collective-permute-start(bf16[4,240,512]{2,1,0:T(8,128)(2,1)S(1)} %pad_maximum_fusion.1.refs_1_), channel_id=1, source_target_pairs={{0,16},{1,3},{2,18},{3,1},{4,20},{5,7},{6,22},{7,5},{8,24},{9,11},... | collective-permute-start | bytes 2949128 | tf_op jit(solution)/shard_map/ppermute | solution.py:985
  71.1 24.3 %collective-permute-start.18 = (bf16[4,240,512]{2,1,0:T(8,128)(2,1)S(1)}, bf16[4,240,512]{2,1,0:T(8,128)(2,1)S(1)}, u32[]{:S(2)}, u32[]{:S(2)}) collective-permute-start(bf16[4,240,512]{2,1,0:T(8,128)(2,1)S(1)} %pad_maximum_fusion.1.refs_1_), channel_id=1, source_target_pairs={{0,2},{1,17},{2,0},{3,19},{4,6},{5,21},{6,4},{7,23},{8,10},{9,25},... | collective-permute-start | bytes 2949128 | tf_op jit(solution)/shard_map/ppermute | solution.py:985
  75.1 20.3 %collective-permute-start.20 = (bf16[240,512]{1,0:T(8,128)(2,1)S(1)}, bf16[240,512]{1,0:T(8,128)(2,1)S(1)}, u32[]{:S(2)}, u32[]{:S(2)}) collective-permute-start(bf16[240,512]{1,0:T(8,128)(2,1)S(1)} %pad_maximum_fusion.12), channel_id=1, source_target_pairs={{0,8},{1,9},{2,10},{3,11},{4,12},{5,13},{6,14},{7,15},{8,0},{9,1},... | collective-permute-start | bytes 737288 | tf_op jit(solution)/shard_map/ppermute | solution.py:985
  76.2 19.2 %collective-permute-start.21 = (bf16[240,512]{1,0:T(8,128)(2,1)S(1)}, bf16[240,512]{1,0:T(8,128)(2,1)S(1)}, u32[]{:S(2)}, u32[]{:S(2)}) collective-permute-start(bf16[240,512]{1,0:T(8,128)(2,1)S(1)} %pad_maximum_fusion.12), channel_id=1, source_target_pairs={{0,12},{1,13},{2,14},{3,15},{4,8},{5,9},{6,10},{7,11},{8,4},{9,5},... | collective-permute-start | bytes 737288 | tf_op jit(solution)/shard_map/ppermute | solution.py:985
  95.4 22.8 %collective-permute-start.22 = (bf16[4,240,512]{2,1,0:T(8,128)(2,1)S(1)}, bf16[4,240,512]{2,1,0:T(8,128)(2,1)S(1)}, u32[]{:S(2)}, u32[]{:S(2)}) collective-permute-start(bf16[4,240,512]{2,1,0:T(8,128)(2,1)S(1)} %collective-permute-done.17.refs_3_), channel_id=1, source_target_pairs={{0,2},{1,17},{2,0},{3,19},{4,6},{5,21},{6,4},{7,23},{8,10},{9,25},... | collective-permute-start | bytes 2949128 | tf_op jit(solution)/shard_map/ppermute | solution.py:985
  96.8 21.4 %collective-permute-start.24 = (bf16[4,240,512]{2,1,0:T(8,128)(2,1)S(1)}, bf16[4,240,512]{2,1,0:T(8,128)(2,1)S(1)}, u32[]{:S(2)}, u32[]{:S(2)}) collective-permute-start(bf16[4,240,512]{2,1,0:T(8,128)(2,1)S(1)} %pad_maximum_fusion.1.refs_1_), channel_id=1, source_target_pairs={{0,1},{1,0},{2,3},{3,2},{4,5},{5,4},{6,7},{7,6},{8,9},{9,8},{10,11... | collective-permute-start | bytes 2949128 | tf_op jit(solution)/shard_map/ppermute | solution.py:985
  96.8 21.4 %collective-permute-start.25 = (bf16[4,240,512]{2,1,0:T(8,128)(2,1)S(1)}, bf16[4,240,512]{2,1,0:T(8,128)(2,1)S(1)}, u32[]{:S(2)}, u32[]{:S(2)}) collective-permute-start(bf16[4,240,512]{2,1,0:T(8,128)(2,1)S(1)} %collective-permute-done.18.refs_2_), channel_id=1, source_target_pairs={{0,1},{1,0},{2,3},{3,2},{4,5},{5,4},{6,7},{7,6},{8,9},{9,8},{10,11... | collective-permute-start | bytes 2949128 | tf_op jit(solution)/shard_map/ppermute | solution.py:985
  97.4 20.9 %collective-permute-start.26 = (bf16[4,240,512]{2,1,0:T(8,128)(2,1)S(1)}, bf16[4,240,512]{2,1,0:T(8,128)(2,1)S(1)}, u32[]{:S(2)}, u32[]{:S(2)}) collective-permute-start(bf16[4,240,512]{2,1,0:T(8,128)(2,1)S(1)} %collective-permute-done.17.refs_3_), channel_id=1, source_target_pairs={{0,1},{1,0},{2,3},{3,2},{4,5},{5,4},{6,7},{7,6},{8,9},{9,8},{10,11... | collective-permute-start | bytes 2949128 | tf_op jit(solution)/shard_map/ppermute | solution.py:985
  97.4 20.9 %collective-permute-start.23 = (bf16[320,512]{1,0:T(8,128)(2,1)S(1)}, bf16[320,512]{1,0:T(8,128)(2,1)S(1)}, u32[]{:S(2)}, u32[]{:S(2)}) collective-permute-start(bf16[320,512]{1,0:T(8,128)(2,1)S(1)} %pad_maximum_fusion.8), channel_id=1, source_target_pairs={{0,8},{1,9},{2,10},{3,11},{4,12},{5,13},{6,14},{7,15},{8,0},{9,1},... | collective-permute-start | bytes 983048 | tf_op jit(solution)/shard_map/ppermute | solution.py:985
  118.4 24.7 %collective-permute-start.28 = (bf16[4,240,512]{2,1,0:T(8,128)(2,1)S(1)}, bf16[4,240,512]{2,1,0:T(8,128)(2,1)}, u32[]{:S(2)}, u32[]{:S(2)}) collective-permute-start(bf16[4,240,512]{2,1,0:T(8,128)(2,1)S(1)} %pad_maximum_fusion.2.refs_1_), channel_id=1, source_target_pairs={{0,16},{1,3},{2,18},{3,1},{4,20},{5,7},{6,22},{7,5},{8,24},{9,11},... | collective-permute-start | bytes 2949128 | tf_op jit(solution)/shard_map/ppermute | solution.py:985
  119.9 23.1 %collective-permute-start.29 = (bf16[4,240,512]{2,1,0:T(8,128)(2,1)S(1)}, bf16[4,240,512]{2,1,0:T(8,128)(2,1)}, u32[]{:S(2)}, u32[]{:S(2)}) collective-permute-start(bf16[4,240,512]{2,1,0:T(8,128)(2,1)S(1)} %pad_maximum_fusion.2.refs_1_), channel_id=1, source_target_pairs={{0,2},{1,17},{2,0},{3,19},{4,6},{5,21},{6,4},{7,23},{8,10},{9,25},... | collective-permute-start | bytes 2949128 | tf_op jit(solution)/shard_map/ppermute | solution.py:985
  120.9 22.1 %collective-permute-start.30 = (bf16[320,512]{1,0:T(8,128)(2,1)S(1)}, bf16[320,512]{1,0:T(8,128)(2,1)S(1)}, u32[]{:S(2)}, u32[]{:S(2)}) collective-permute-start(bf16[320,512]{1,0:T(8,128)(2,1)S(1)} %pad_maximum_fusion.8), channel_id=1, source_target_pairs={{0,4},{1,5},{2,6},{3,7},{4,0},{5,1},{6,2},{7,3},{8,12},{9,13},{10,... | collective-permute-start | bytes 983048 | tf_op jit(solution)/shard_map/ppermute | solution.py:985
  120.9 22.1 %collective-permute-start.31 = (bf16[320,512]{1,0:T(8,128)(2,1)S(1)}, bf16[320,512]{1,0:T(8,128)(2,1)S(1)}, u32[]{:S(2)}, u32[]{:S(2)}) collective-permute-start(bf16[320,512]{1,0:T(8,128)(2,1)S(1)} %pad_maximum_fusion.8), channel_id=1, source_target_pairs={{0,12},{1,13},{2,14},{3,15},{4,8},{5,9},{6,10},{7,11},{8,4},{9,5},... | collective-permute-start | bytes 983048 | tf_op jit(solution)/shard_map/ppermute | solution.py:985
  157.6 20.3 %collective-permute-start.37 = (bf16[4,320,512]{2,1,0:T(8,128)(2,1)S(1)}, bf16[4,320,512]{2,1,0:T(8,128)(2,1)S(1)}, u32[]{:S(2)}, u32[]{:S(2)}) collective-permute-start(bf16[4,320,512]{2,1,0:T(8,128)(2,1)S(1)} %pad_maximum_fusion.refs_1_.refs_9_.refs_2_), channel_id=1, source_target_pairs={{0,2},{1,17},{2,0},{3,19},{4,6},{5,21},{6,4},{7,23},{8,10},{9,25},... | collective-permute-start | bytes 3932168 | tf_op jit(solution)/shard_map/ppermute | solution.py:985
  158.0 19.9 %collective-permute-start.38 = (bf16[4,320,512]{2,1,0:T(8,128)(2,1)S(1)}, bf16[4,320,512]{2,1,0:T(8,128)(2,1)S(1)}, u32[]{:S(2)}, u32[]{:S(2)}) collective-permute-start(bf16[4,320,512]{2,1,0:T(8,128)(2,1)S(1)} %pad_maximum_fusion.refs_1_.refs_9_.refs_2_), channel_id=1, source_target_pairs={{0,1},{1,0},{2,3},{3,2},{4,5},{5,4},{6,7},{7,6},{8,9},{9,8},{10,11... | collective-permute-start | bytes 3932168 | tf_op jit(solution)/shard_map/ppermute | solution.py:985
  205.1 28.6 %collective-permute-start.43 = (bf16[512,512]{1,0:T(8,128)(2,1)S(1)}, bf16[512,512]{1,0:T(8,128)(2,1)S(1)}, u32[]{:S(2)}, u32[]{:S(2)}) collective-permute-start(bf16[512,512]{1,0:T(8,128)(2,1)S(1)} %broadcast_select_fusion), channel_id=1, source_target_pairs={{0,16},{16,0},{1,17},{17,1},{2,18},{18,2},{3,19},{19,3},{4,20},{20... | collective-permute-start | bytes 1572872 | tf_op jit(solution)/shard_map/ppermute | solution.py:1055
  211.4 22.4 %collective-permute-start.42 = (bf16[8,128,512]{2,1,0:T(8,128)(2,1)S(1)}, bf16[8,128,512]{2,1,0:T(8,128)(2,1)S(1)}, u32[]{:S(2)}, u32[]{:S(2)}) collective-permute-start(bf16[8,128,512]{2,1,0:T(8,128)(2,1)S(1)} %get-tuple-element.410), channel_id=1, source_target_pairs={{0,16},{1,3},{2,18},{3,1},{4,20},{5,7},{6,22},{7,5},{8,24},{9,11},... | collective-permute-start | bytes 3145736 | tf_op jit(solution)/shard_map/ppermute | solution.py:985
  253.4 18.7 %collective-permute-start.47 = (bf16[4,112,512]{2,1,0:T(8,128)(2,1)S(1)}, bf16[4,112,512]{2,1,0:T(8,128)(2,1)S(1)}, u32[]{:S(2)}, u32[]{:S(2)}) collective-permute-start(bf16[4,112,512]{2,1,0:T(8,128)(2,1)S(1)} %get-tuple-element.427), channel_id=1, source_target_pairs={{0,2},{1,17},{2,0},{3,19},{4,6},{5,21},{6,4},{7,23},{8,10},{9,25},... | collective-permute-start | bytes 1376264 | tf_op jit(solution)/shard_map/ppermute | solution.py:985
  273.4 28.8 %collective-permute-start.50 = (bf16[4,128,512]{2,1,0:T(8,128)(2,1)S(1)}, bf16[4,128,512]{2,1,0:T(8,128)(2,1)S(1)}, u32[]{:S(2)}, u32[]{:S(2)}) collective-permute-start(bf16[4,128,512]{2,1,0:T(8,128)(2,1)S(1)} %get-tuple-element.421), channel_id=1, source_target_pairs={{0,2},{1,17},{2,0},{3,19},{4,6},{5,21},{6,4},{7,23},{8,10},{9,25},... | collective-permute-start | bytes 1572872 | tf_op jit(solution)/shard_map/ppermute | solution.py:985
  274.4 27.7 %collective-permute-start.55 = (bf16[240,512]{1,0:T(8,128)(2,1)S(1)}, bf16[240,512]{1,0:T(8,128)(2,1)S(1)}, u32[]{:S(2)}, u32[]{:S(2)}) collective-permute-start(bf16[240,512]{1,0:T(8,128)(2,1)S(1)} %pad_maximum_fusion.15), channel_id=1, source_target_pairs={{0,12},{1,13},{2,14},{3,15},{4,8},{5,9},{6,10},{7,11},{8,4},{9,5},... | collective-permute-start | bytes 737288 | tf_op jit(solution)/shard_map/ppermute | solution.py:985
  275.8 26.3 %collective-permute-start.54 = (bf16[240,512]{1,0:T(8,128)(2,1)S(1)}, bf16[240,512]{1,0:T(8,128)(2,1)S(1)}, u32[]{:S(2)}, u32[]{:S(2)}) collective-permute-start(bf16[240,512]{1,0:T(8,128)(2,1)S(1)} %pad_maximum_fusion.14), channel_id=1, source_target_pairs={{0,8},{1,9},{2,10},{3,11},{4,12},{5,13},{6,14},{7,15},{8,0},{9,1},... | collective-permute-start | bytes 737288 | tf_op jit(solution)/shard_map/ppermute | solution.py:985
  275.9 26.2 %collective-permute-start.53 = (bf16[240,512]{1,0:T(8,128)(2,1)S(1)}, bf16[240,512]{1,0:T(8,128)(2,1)S(1)}, u32[]{:S(2)}, u32[]{:S(2)}) collective-permute-start(bf16[240,512]{1,0:T(8,128)(2,1)S(1)} %pad_maximum_fusion.13), channel_id=1, source_target_pairs={{0,4},{1,5},{2,6},{3,7},{4,0},{5,1},{6,2},{7,3},{8,12},{9,13},{10,... | collective-permute-start | bytes 737288 | tf_op jit(solution)/shard_map/ppermute | solution.py:985
  279.9 22.3 %collective-permute-start.52 = (bf16[8,160,512]{2,1,0:T(8,128)(2,1)S(1)}, bf16[8,160,512]{2,1,0:T(8,128)(2,1)S(1)}, u32[]{:S(2)}, u32[]{:S(2)}) collective-permute-start(bf16[8,160,512]{2,1,0:T(8,128)(2,1)S(1)} %get-tuple-element.407), channel_id=1, source_target_pairs={{0,16},{1,3},{2,18},{3,1},{4,20},{5,7},{6,22},{7,5},{8,24},{9,11},... | collective-permute-start | bytes 3932168 | tf_op jit(solution)/shard_map/ppermute | solution.py:985
  302.7 19.8 %collective-permute-start.57 = (bf16[4,160,512]{2,1,0:T(8,128)(2,1)S(1)}, bf16[4,160,512]{2,1,0:T(8,128)(2,1)S(1)}, u32[]{:S(2)}, u32[]{:S(2)}) collective-permute-start(bf16[4,160,512]{2,1,0:T(8,128)(2,1)S(1)} %get-tuple-element.419), channel_id=1, source_target_pairs={{0,2},{1,17},{2,0},{3,19},{4,6},{5,21},{6,4},{7,23},{8,10},{9,25},... | collective-permute-start | bytes 1966088 | tf_op jit(solution)/shard_map/ppermute | solution.py:985
  303.7 18.7 %collective-permute-start.61 = (bf16[128,512]{1,0:T(8,128)(2,1)S(1)}, bf16[128,512]{1,0:T(8,128)(2,1)S(1)}, u32[]{:S(2)}, u32[]{:S(2)}) collective-permute-start(bf16[128,512]{1,0:T(8,128)(2,1)S(1)} %get-tuple-element.437), channel_id=1, source_target_pairs={{0,12},{1,13},{2,14},{3,15},{4,8},{5,9},{6,10},{7,11},{8,4},{9,5},... | collective-permute-start | bytes 393224 | tf_op jit(solution)/shard_map/ppermute | solution.py:985
  323.3 22.7 %collective-permute-start.62 = (bf16[4,112,512]{2,1,0:T(8,128)(2,1)S(1)}, bf16[4,112,512]{2,1,0:T(8,128)(2,1)S(1)}, u32[]{:S(2)}, u32[]{:S(2)}) collective-permute-start(bf16[4,112,512]{2,1,0:T(8,128)(2,1)S(1)} %get-tuple-element.425), channel_id=1, source_target_pairs={{0,2},{1,17},{2,0},{3,19},{4,6},{5,21},{6,4},{7,23},{8,10},{9,25},... | collective-permute-start | bytes 1376264 | tf_op jit(solution)/shard_map/ppermute | solution.py:985
  (105 other events, 1131.6 us)
